TPU v7x, 32 devices: a whole 2x2x4 slice. The times are simulated.
32 devices in a mesh: dp: 4 (over y, x), row: 4 (over z), col: 2 (over core).
Axes of the slice: x: 2, y: 2, z: 4, core: 2. Of those that a mesh axis runs over, the one named last changes fastest.
Arguments:
- outer_gate: bfloat16 [4, 8, 1024, 1024], P('dp', None, ('row', 'col')), may hold values from -6 to 6
- inner_gate: bfloat16 [4, 8, 1024, 1024], P('dp', None, ('row', 'col')), may hold values from -6 to 6
- signal: bfloat16 [4, 8, 1024, 1024], P('dp', None, ('row', 'col')), may hold values from -6 to 6
- grad_out: bfloat16 [4, 8, 1024, 1024], P('dp', None, ('row', 'col')), may hold values from -6 to 6
- filter_weight: float32 [1024, 1024], P(('row', 'col')), may hold values from -6 to 6
Outputs:
- grad_outer: bfloat16 [4, 8, 1024, 1024], P('dp', None, ('row', 'col'))
- grad_inner: bfloat16 [4, 8, 1024, 1024], P('dp', None, ('row', 'col'))
- grad_signal: bfloat16 [4, 8, 1024, 1024], P('dp', None, ('row', 'col'))
- grad_filter: float32 [1024, 1024], P(('row', 'col'))
All inputs are finite; a program needn't handle non-finite values.
Results may differ from a plain program's by a relative error of at most 0.0013.
Values sent between devices are 32-bit elements; how exact they have to be, the bound alone decides.
No kernel may reach another device: no remote copies, remote signals or barrier semaphores. Data moves between devices by JAX's collectives and lax.ppermute only.
A program may use at most 192 MiB of HBM per device.

v0:
```python
import functools
import math

import jax
import jax.numpy as jnp
import numpy as np
from jax import lax
from jax.experimental import pallas as pl
from jax.experimental.pallas import tpu as pltpu
from jax.sharding import PartitionSpec as P

TWO_PI = 2.0 * math.pi


def contract(form, left, right):
    return jnp.einsum(
        form, left, right, precision=lax.Precision.HIGHEST, preferred_element_type=jnp.float32
    )


def redistribute(blocks):
    return lax.all_to_all(blocks, ("row", "col"), split_axis=0, concat_axis=0, tiled=True)


def own_block():
    return lax.axis_index("row") * lax.axis_size("col") + lax.axis_index("col")


def turn_angles(first_index, second_index, total):
    product = first_index * second_index % total
    angles = product.astype(jnp.float32) * (TWO_PI / total)
    return (jnp.cos(angles), jnp.sin(angles))


def axis_dft(real, imag, sign):
    length, width = real.shape
    first = 1 << (length.bit_length() - 1) // 2
    second = length // first
    index_a = jnp.arange(first, dtype=jnp.int32)
    index_b = jnp.arange(second, dtype=jnp.int32)
    cos_a, sin_a = turn_angles(index_a[:, None], index_a[None, :], first)
    sin_a = sign * sin_a
    cos_b, sin_b = turn_angles(index_b[:, None], index_b[None, :], second)
    sin_b = sign * sin_b
    twist_cos, twist_sin = turn_angles(index_a[:, None], index_b[None, :], length)
    twist_cos = twist_cos[:, :, None]
    twist_sin = sign * twist_sin[:, :, None]
    real_three = real.reshape(first, second, width)
    step_real = contract("abm,ak->kbm", real_three, cos_a)
    step_imag = contract("abm,ak->kbm", real_three, sin_a)
    if imag is not None:
        imag_three = imag.reshape(first, second, width)
        step_real = step_real - contract("abm,ak->kbm", imag_three, sin_a)
        step_imag = step_imag + contract("abm,ak->kbm", imag_three, cos_a)
    turned_real = step_real * twist_cos - step_imag * twist_sin
    turned_imag = step_real * twist_sin + step_imag * twist_cos
    out_real = contract("kbm,bj->jkm", turned_real, cos_b) - contract(
        "kbm,bj->jkm", turned_imag, sin_b
    )
    out_imag = contract("kbm,bj->jkm", turned_real, sin_b) + contract(
        "kbm,bj->jkm", turned_imag, cos_b
    )
    return (out_real.reshape(length, width), out_imag.reshape(length, width))


def forward(stacked, order):
    count, block, grid_side = stacked.shape
    owners = grid_side // block
    total = grid_side * grid_side
    send = jnp.transpose(stacked.reshape(count, block, owners, block), (2, 1, 0, 3)).reshape(
        owners, block, count * block
    )
    columns = redistribute(send).reshape(grid_side, count * block)
    first_real, first_imag = axis_dft(columns, None, -1.0)
    first_real = first_real.reshape(grid_side, count, block)
    first_imag = first_imag.reshape(grid_side, count, block)
    col_index = own_block() * block + jnp.arange(block, dtype=jnp.int32)
    cos_turn, sin_turn = turn_angles(order[:, None, None], col_index[None, None, :], total)
    turned_real = first_real * cos_turn + first_imag * sin_turn
    turned_imag = first_imag * cos_turn - first_real * sin_turn
    send_two = jnp.concatenate([turned_real, turned_imag], axis=1).reshape(
        owners, block, 2 * count * block
    )
    gotten = redistribute(send_two).reshape(owners, block, 2 * count, block)
    flat_real = jnp.transpose(gotten[:, :, :count, :], (0, 3, 1, 2)).reshape(
        grid_side, block * count
    )
    flat_imag = jnp.transpose(gotten[:, :, count:, :], (0, 3, 1, 2)).reshape(
        grid_side, block * count
    )
    out_real, out_imag = axis_dft(flat_real, flat_imag, -1.0)
    spec_real = jnp.transpose(out_real.reshape(grid_side, block, count), (1, 2, 0))
    spec_imag = jnp.transpose(out_imag.reshape(grid_side, block, count), (1, 2, 0))
    return (spec_real, spec_imag)


def inverse(spec_real, spec_imag, order):
    block, count, grid_side = spec_real.shape
    owners = grid_side // block
    total = grid_side * grid_side
    flat_real = jnp.transpose(spec_real, (2, 0, 1)).reshape(grid_side, block * count)
    flat_imag = jnp.transpose(spec_imag, (2, 0, 1)).reshape(grid_side, block * count)
    out_real, out_imag = axis_dft(flat_real, flat_imag, 1.0)
    back_real = jnp.transpose(out_real.reshape(owners, block, block, count), (0, 2, 3, 1))
    back_imag = jnp.transpose(out_imag.reshape(owners, block, block, count), (0, 2, 3, 1))
    freq_index = lax.dynamic_slice_in_dim(order, own_block() * block, block, 0)
    col_index = (
        jnp.arange(owners, dtype=jnp.int32)[:, None] * block
        + jnp.arange(block, dtype=jnp.int32)[None, :]
    )
    cos_turn, sin_turn = turn_angles(
        freq_index[None, :, None, None], col_index[:, None, None, :], total
    )
    turned_real = back_real * cos_turn - back_imag * sin_turn
    turned_imag = back_real * sin_turn + back_imag * cos_turn
    send = jnp.concatenate([turned_real, turned_imag], axis=2).reshape(
        owners, block, 2 * count * block
    )
    gotten = redistribute(send).reshape(grid_side, 2 * count * block)
    real_part = gotten[:, : count * block]
    imag_part = gotten[:, count * block :]
    full_real, full_imag = axis_dft(real_part, imag_part, 1.0)
    values = full_real * (1.0 / total)
    returned = redistribute(values.reshape(owners, block, count * block)).reshape(
        owners, block, count, block
    )
    return jnp.transpose(returned, (2, 1, 0, 3)).reshape(count, block, grid_side)


def spread_shards(outer_gate, inner_gate, signal, grad_out, filter_weight):
    grid_side = filter_weight.shape[1]
    freq_index = jnp.arange(grid_side, dtype=jnp.int32)
    outer_f = outer_gate[0].astype(jnp.float32)
    inner_f = inner_gate[0].astype(jnp.float32)
    signal_f = signal[0].astype(jnp.float32)
    grad_f = grad_out[0].astype(jnp.float32)
    channels = inner_f.shape[0]
    gated = inner_f * signal_f
    grad_conv = grad_f * outer_f
    taps = (filter_weight * (1.0 / grid_side))[None]
    spec_real, spec_imag = forward(jnp.concatenate([gated, grad_conv], axis=0), freq_index)
    filt_real, filt_imag = forward(taps, freq_index)
    gated_real = spec_real[:, :channels]
    gated_imag = spec_imag[:, :channels]
    cot_real = spec_real[:, channels : 2 * channels]
    cot_imag = spec_imag[:, channels : 2 * channels]
    conv_real = filt_real * gated_real - filt_imag * gated_imag
    conv_imag = filt_real * gated_imag + filt_imag * gated_real
    back_real = filt_real * cot_real + filt_imag * cot_imag
    back_imag = filt_real * cot_imag - filt_imag * cot_real
    term_real = jnp.sum(gated_real * cot_real + gated_imag * cot_imag, axis=1, keepdims=True)
    term_imag = jnp.sum(gated_real * cot_imag - gated_imag * cot_real, axis=1, keepdims=True)
    values = inverse(
        jnp.concatenate([conv_real, back_real, term_real], axis=1),
        jnp.concatenate([conv_imag, back_imag, term_imag], axis=1),
        freq_index,
    )
    grad_filter = lax.psum(values[2 * channels], "dp") * (1.0 / grid_side)
    conv = values[:channels]
    grad_gated = values[channels : 2 * channels]
    grad_outer = (grad_f * conv).astype(jnp.bfloat16)[None]
    grad_inner = (grad_gated * signal_f).astype(jnp.bfloat16)[None]
    grad_signal = (grad_gated * inner_f).astype(jnp.bfloat16)[None]
    return (grad_outer, grad_inner, grad_signal, grad_filter)


VMEM_LIMIT = 18 * 1024 * 1024
UNDER_WAY = 4
ROW_PAD = 16
LANE_PAD = 128


def up_to(value, unit):
    return -(-value // unit) * unit


def high_low(table):
    high = table.astype(jnp.bfloat16)
    low = (table - high.astype(np.float64)).astype(jnp.bfloat16)
    return np.stack([high, low])


class Plan:
    def __init__(self, side):
        half = side // 2
        self.side, self.half, self.quarter = side, half, side // 4
        self.evens = up_to(half // 2 + 1, ROW_PAD)
        self.odds = half // 2
        self.rows = self.evens + self.odds
        self.even_depth = up_to(2 * self.evens, LANE_PAD)
        total = side * side
        even_k = 2 * np.arange(self.evens)
        odd_k = 2 * np.arange(self.odds) + 1
        live = (even_k <= half).astype(np.float64)
        p = np.arange(half)

        def waves(k, scale):
            angle = 2.0 * np.pi * (k[:, None] * p[None, :] % side) / side
            return np.concatenate([np.cos(angle) * scale[:, None], -np.sin(angle) * scale[:, None]])

        ones = np.ones(self.odds)
        self.into_even = high_low(waves(even_k, live))
        self.into_odd = high_low(waves(odd_k, ones))
        weight = np.where((even_k == 0) | (even_k == half), 1.0, 2.0) * live / total
        back_even = np.zeros((half, self.even_depth))
        back_even[:, : 2 * self.evens] = waves(even_k, weight).T
        self.back_even = high_low(back_even)
        self.back_odd = high_low(waves(odd_k, ones * 2.0 / total).T)
        k = np.concatenate([even_k, odd_k])
        turn = 2.0 * np.pi * (k[:, None] * np.arange(side)[None, :] % total) / total
        self.turn = np.stack([np.cos(turn), np.sin(turn)]).astype(np.float32)
        q = np.arange(self.quarter)
        mixes = []
        for r in range(4):
            angle = 2.0 * np.pi * (q[:, None] * (4 * q[None, :] + r) % side) / side
            cos, sin = np.cos(angle), np.sin(angle)
            mixes.append(np.block([[cos, -sin], [sin, cos]]))
        self.mix = high_low(np.stack(mixes))
        self.row_tile = next(t for t in (176, 264, 16, 8) if self.rows % t == 0)


def split_terms(values):
    high = values.astype(jnp.bfloat16)
    return high, (values - high.astype(jnp.float32)).astype(jnp.bfloat16)


def dot_in(table, rows, high, low):
    dot = functools.partial(jnp.dot, preferred_element_type=jnp.float32)
    first, second = table[0, rows], table[1, rows]
    return dot(first, high) + (dot(first, low) + dot(second, high))


def block_views(plan, owners, me, blocks, values):
    size = plan.side // owners
    for step in range(owners):
        at = pl.multiple_of((me[0] ^ step) * size, size)
        yield blocks[step].at[pl.ds(0, size)], values.at[pl.ds(at, size)]


def tile_views(plan, grid, me, tiles, values):
    parts, rows, cols = grid
    block = plan.side // (rows * cols)
    height = block // parts
    own_row = me[0] // cols
    for part in range(parts):
        for col in range(cols):
            for i in range(rows):
                at = ((own_row ^ i) * cols + col) * block + part * height
                yield tiles[0].at[part * cols + col, i], values.at[pl.ds(pl.multiple_of(at, height), height)]


def start_all(pairs, sems):
    copies = [pltpu.make_async_copy(source, to, sems.at[i]) for i, (source, to) in enumerate(pairs)]
    for copy in copies:
        copy.start()
    return copies


def wait_all(copies):
    for copy in copies:
        copy.wait()


def to_spectrum(plan, values, into_even, into_odd, turn, mix, spec, mid):
    side, half, quarter = plan.side, plan.half, plan.quarter

    @pl.loop(0, side // quarter)
    def columns(tile):
        cols = pl.ds(pl.multiple_of(tile * quarter, quarter), quarter)
        top, bottom = values[pl.ds(0, half), cols], values[pl.ds(half, half), cols]
        for first, count, table, part in (
            (0, plan.evens, into_even, top + bottom),
            (plan.evens, plan.odds, into_odd, top - bottom),
        ):
            out = dot_in(table, slice(None), *split_terms(part))
            real, imag = out[:count], out[count:]
            rows = pl.ds(first, count)
            cos, sin = turn[0, rows, cols], turn[1, rows, cols]
            mid[0, rows, cols] = real * cos + imag * sin
            mid[1, rows, cols] = imag * cos - real * sin

    @pl.loop(0, plan.rows // plan.row_tile)
    def rows_loop(tile):
        rows = pl.ds(pl.multiple_of(tile * plan.row_tile, plan.row_tile), plan.row_tile)
        real = [mid[0, rows, pl.ds(j * quarter, quarter)] for j in range(4)]
        imag = [mid[1, rows, pl.ds(j * quarter, quarter)] for j in range(4)]
        sum_r, sum_i = real[0] + real[2], imag[0] + imag[2]
        dif_r, dif_i = real[0] - real[2], imag[0] - imag[2]
        two_r, two_i = real[1] + real[3], imag[1] + imag[3]
        odd_r, odd_i = real[1] - real[3], imag[1] - imag[3]
        turns = (
            (sum_r + two_r, sum_i + two_i),
            (dif_r + odd_i, dif_i - odd_r),
            (sum_r - two_r, sum_i - two_i),
            (dif_r - odd_i, dif_i + odd_r),
        )
        dot = functools.partial(jnp.dot, preferred_element_type=jnp.float32)
        for r, pair in enumerate(turns):
            high, low = split_terms(jnp.concatenate(pair, axis=1))
            out = dot(high, mix[0, r]) + (dot(low, mix[0, r]) + dot(high, mix[1, r]))
            cols = pl.ds(r * quarter, quarter)
            spec[0, rows, cols] = out[:, :quarter]
            spec[1, rows, cols] = out[:, quarter:]


def inverse_rows(plan, conjugate, left, right, turn, mix, mid):
    quarter = plan.quarter

    @pl.loop(0, plan.rows // plan.row_tile)
    def rows_loop(tile):
        rows = pl.ds(pl.multiple_of(tile * plan.row_tile, plan.row_tile), plan.row_tile)
        real, imag = [], []
        for r in range(4):
            cols = pl.ds(r * quarter, quarter)
            left_r, left_i = left[0, rows, cols], left[1, rows, cols]
            right_r, right_i = right[0, rows, cols], right[1, rows, cols]
            if conjugate:
                left_i = -left_i
            pair = (left_r * right_r - left_i * right_i, left_r * right_i + left_i * right_r)
            high, low = split_terms(jnp.concatenate(pair, axis=1))

            def dot(part, table):
                return lax.dot_general(
                    part, table, (((1,), (1,)), ((), ())), preferred_element_type=jnp.float32
                )

            out = dot(high, mix[0, r]) + (dot(low, mix[0, r]) + dot(high, mix[1, r]))
            real.append(out[:, :quarter])
            imag.append(out[:, quarter:])
        sum_r, sum_i = real[0] + real[2], imag[0] + imag[2]
        dif_r, dif_i = real[0] - real[2], imag[0] - imag[2]
        two_r, two_i = real[1] + real[3], imag[1] + imag[3]
        odd_r, odd_i = real[1] - real[3], imag[1] - imag[3]
        turns = (
            (sum_r + two_r, sum_i + two_i),
            (dif_r - odd_i, dif_i + odd_r),
            (sum_r - two_r, sum_i - two_i),
            (dif_r + odd_i, dif_i - odd_r),
        )
        for j, (got_r, got_i) in enumerate(turns):
            cols = pl.ds(j * quarter, quarter)
            cos, sin = turn[0, rows, cols], turn[1, rows, cols]
            mid[0, rows, cols] = got_r * cos - got_i * sin
            mid[1, rows, cols] = got_r * sin + got_i * cos


def inverse_columns(plan, back_even, back_odd, mid, values):
    side, half, quarter = plan.side, plan.half, plan.quarter

    @pl.loop(0, side // quarter)
    def columns(tile):
        cols = pl.ds(pl.multiple_of(tile * quarter, quarter), quarter)
        even = [mid[0, pl.ds(0, plan.evens), cols], mid[1, pl.ds(0, plan.evens), cols]]
        if plan.even_depth > 2 * plan.evens:
            even.append(jnp.zeros((plan.even_depth - 2 * plan.evens, quarter), jnp.float32))
        odd = [mid[0, pl.ds(plan.evens, plan.odds), cols], mid[1, pl.ds(plan.evens, plan.odds), cols]]
        from_even = dot_in(back_even, slice(None), *split_terms(jnp.concatenate(even)))
        from_odd = dot_in(back_odd, slice(None), *split_terms(jnp.concatenate(odd)))
        values[pl.ds(0, half), cols] = from_even + from_odd
        values[pl.ds(half, half), cols] = from_even - from_odd


def filter_kernel(plan, views, count, me, *refs):
    tiles = refs[:count]
    into_even, into_odd, turn, mix, spec, values, mid, sems = refs[count:]
    wait_all(start_all(views(me, tiles, values), sems))
    to_spectrum(plan, values, into_even, into_odd, turn, mix, spec, mid)


def conv_kernel(plan, views, count, me, filt, *refs):
    blocks, tables = refs[:count], refs[count : count + 6]
    into_even, into_odd, back_even, back_odd, turn, mix = tables
    spec, outs = refs[count + 6], refs[count + 7 : 2 * count + 7]
    values, mid, sems = refs[2 * count + 7 :]
    wait_all(start_all(views(me, blocks, values), sems))
    to_spectrum(plan, values, into_even, into_odd, turn, mix, spec, mid)
    inverse_rows(plan, False, filt, spec, turn, mix, mid)
    inverse_columns(plan, back_even, back_odd, mid, values)
    wait_all(start_all(((to, source) for source, to in views(me, outs, values)), sems))


def grads_kernel(plan, views, term_views, count, me, filt, gated, *refs):
    blocks, tables = refs[:count], refs[count : count + 6]
    into_even, into_odd, back_even, back_odd, turn, mix = tables
    outs, term = refs[count + 6 : 2 * count + 6], refs[2 * count + 6]
    values, mid, spec, sems, term_sems = refs[2 * count + 7 :]
    wait_all(start_all(views(me, blocks, values), sems))
    to_spectrum(plan, values, into_even, into_odd, turn, mix, spec, mid)
    inverse_rows(plan, True, filt, spec, turn, mix, mid)
    inverse_columns(plan, back_even, back_odd, mid, values)
    copies = start_all(((to, source) for source, to in views(me, outs, values)), sems)
    inverse_rows(plan, True, gated, spec, turn, mix, mid)
    wait_all(copies)
    inverse_columns(plan, back_even, back_odd, mid, values)
    wait_all(start_all(((to, source) for source, to in term_views(me, [term], values)), term_sems))


def smem():
    return pl.BlockSpec(memory_space=pltpu.SMEM)


def vmem():
    return pl.BlockSpec(memory_space=pltpu.VMEM)


def anywhere():
    return pl.BlockSpec(memory_space=pl.ANY)


def kernel_cost(plan):
    return pl.CostEstimate(flops=plan.side**2, bytes_accessed=plan.side**2, transcendentals=0)


def call_kernel(plan, kernel, name, args, in_specs, out_shape, out_specs, scratch):
    return pl.pallas_call(
        kernel,
        out_shape=out_shape,
        in_specs=in_specs,
        out_specs=out_specs,
        scratch_shapes=scratch,
        compiler_params=pltpu.CompilerParams(vmem_limit_bytes=VMEM_LIMIT),
        cost_estimate=kernel_cost(plan),
        name=name,
    )(*args)


def float_array(shape):
    return jax.ShapeDtypeStruct(shape, jnp.float32)


def filter_spectrum(plan, me, tiles, views, copies):
    shape = (2, plan.rows, plan.side)
    return call_kernel(
        plan,
        functools.partial(filter_kernel, plan, views, len(tiles)),
        "filter_spectrum",
        (me, *tiles, plan.into_even, plan.into_odd, plan.turn, plan.mix),
        [smem()] + [anywhere()] * len(tiles) + [vmem()] * 4,
        float_array(shape),
        vmem(),
        [
            pltpu.VMEM((plan.side, plan.side), jnp.float32),
            pltpu.VMEM(shape, jnp.float32),
            pltpu.SemaphoreType.DMA((copies,)),
        ],
    )


def tables_of(plan):
    return (plan.into_even, plan.into_odd, plan.back_even, plan.back_odd, plan.turn, plan.mix)


def conv_of(plan, me, filt, blocks, views):
    count = len(blocks)
    shape = (2, plan.rows, plan.side)
    spec, *outs = call_kernel(
        plan,
        functools.partial(conv_kernel, plan, views, count),
        "conv_of",
        (me, filt, *blocks, *tables_of(plan)),
        [smem(), vmem()] + [vmem()] * count + [vmem()] * 6,
        [float_array(shape)] + [float_array((plan.side // count, plan.side))] * count,
        [vmem()] * (count + 1),
        [
            pltpu.VMEM((plan.side, plan.side), jnp.float32),
            pltpu.VMEM(shape, jnp.float32),
            pltpu.SemaphoreType.DMA((count,)),
        ],
    )
    return spec, outs


def grads_of(plan, me, filt, gated, blocks, views, term_shape, term_views):
    count = len(blocks)
    shape = (2, plan.rows, plan.side)
    *outs, term = call_kernel(
        plan,
        functools.partial(grads_kernel, plan, views, term_views, count),
        "grads_of",
        (me, filt, gated, *blocks, *tables_of(plan)),
        [smem(), vmem(), vmem()] + [vmem()] * count + [vmem()] * 6,
        [float_array((plan.side // count, plan.side))] * count + [float_array(term_shape)],
        [vmem()] * count + [anywhere()],
        [
            pltpu.VMEM((plan.side, plan.side), jnp.float32),
            pltpu.VMEM(shape, jnp.float32),
            pltpu.VMEM(shape, jnp.float32),
            pltpu.SemaphoreType.DMA((count,)),
            pltpu.SemaphoreType.DMA((math.prod(term_shape[:2]),)),
        ],
    )
    return outs, term


def pairwise(block, axis, step):
    return lax.ppermute(block, axis, [(i, i ^ step) for i in range(lax.axis_size(axis))])


def after(first, then):
    return lax.optimization_barrier((first, then))[1]


def gate_kernel(steps, gates, me, *refs):
    count = len(steps)
    blocks = refs[:count]
    ins = refs[count : count + gates]
    outs, got, sems = refs[-gates - 2 : -2], refs[-2], refs[-1]
    here = pl.program_id(0)

    def copy_of(i):
        return pltpu.make_async_copy(blocks[i], got.at[i], sems.at[i])

    @pl.when(here == 0)
    def start():
        for i in range(count):
            copy_of(i).start()

    for i in range(count):

        @pl.when(here == i)
        def wait():
            copy_of(i).wait()

    values = got[here]
    for gate, out in zip(ins, outs):
        out[0] = (gate[0].astype(jnp.float32) * values).astype(jnp.bfloat16)


def gated_by(me, steps, blocks, gates, done=()):
    count = len(steps)
    shape = gates[0].shape

    def place(i, me):
        step = steps[-1]
        for j in range(count - 1):
            step = jnp.where(i == j, steps[j], step)
        return (me[0] ^ step, 0, 0)

    spec = pl.BlockSpec((1,) + shape[1:], place)
    size = count * shape[1] * shape[2]
    first_done = 1 + count + len(gates)
    return pl.pallas_call(
        functools.partial(gate_kernel, steps, len(gates)),
        grid_spec=pltpu.PrefetchScalarGridSpec(
            num_scalar_prefetch=1,
            grid=(count,),
            in_specs=[anywhere()] * count + [spec] * len(gates) + [anywhere()] * len(done),
            out_specs=[spec] * len(gates),
            scratch_shapes=[
                pltpu.VMEM((count,) + shape[1:], jnp.float32),
                pltpu.SemaphoreType.DMA((count,)),
            ],
        ),
        out_shape=[jax.ShapeDtypeStruct(shape, jnp.bfloat16)] * len(gates),
        input_output_aliases={first_done + i: i for i in range(len(done))},
        compiler_params=pltpu.CompilerParams(vmem_limit_bytes=VMEM_LIMIT),
        cost_estimate=pl.CostEstimate(
            flops=size * len(gates), bytes_accessed=4 * size * (1 + len(gates)), transcendentals=0
        ),
        name="gate_out",
    )(me, *blocks, *gates, *done)


def send_order(owners):
    far = sorted(range(owners // 2, owners), key=lambda s: (s & 1, -s))
    return far + sorted(range(1, owners // 2), reverse=True)


def channel_shards(outer_gate, inner_gate, signal, grad_out, filter_weight):
    block, side = filter_weight.shape
    plan = Plan(side)
    parts, rows, cols = (lax.axis_size(name) for name in ("dp", "row", "col"))
    owners = rows * cols
    place = own_block()
    me = jnp.reshape(place, (1,)).astype(jnp.int32)
    order = send_order(owners)
    far, near = order[: owners // 2], order[owners // 2 :]
    mixed_order = far[:1] + [step for pair in zip(far[1:], sorted(near, key=lambda s: s % cols)) for step in pair]
    last_order = far[:-1] + near + far[-1:]
    by_block = functools.partial(block_views, plan, owners)
    by_tile = functools.partial(tile_views, plan, (parts, rows, cols))

    def gated_block(left, right, step):
        at = place ^ step
        return lax.dynamic_index_in_dim(left[0], at, 0, False).astype(
            jnp.float32
        ) * lax.dynamic_index_in_dim(right[0], at, 0, False).astype(jnp.float32)

    sent = []

    def exchange(blocks, what, order=order):
        got = [blocks[0]] + [None] * (owners - 1)
        for step in order:
            mine = blocks[step]
            if len(sent) >= UNDER_WAY:
                mine = after(sent[: len(sent) - UNDER_WAY + 1][-owners:], mine)
            with jax.named_scope(f"{what}_{step}"):
                got[step] = pairwise(mine, ("row", "col"), step)
            sent.append(got[step])
        return got

    height = block // parts
    own_part = lax.dynamic_slice_in_dim(filter_weight, lax.axis_index("dp") * height, height, 0)
    own_part = own_part * (1.0 / side)
    inner, values = inner_gate, signal
    gated = [None] * owners
    for step in order + [0]:
        gated[step] = gated_block(inner, values, step)
        if step and step % cols == 0:
            gated[step] = jnp.concatenate([gated[step], own_part])
        if step == order[0]:
            inner, values = after(gated[step], [inner_gate, signal])
    gated = exchange(gated, "gated", mixed_order)
    over_row = jnp.stack([own_part] + [gated[i * cols][block:] for i in range(1, rows)])
    over_row = after([gated[step] for step in far], over_row)
    over_all = [lax.all_gather(over_row, ("dp", "col"))]
    filt = filter_spectrum(plan, me, over_all, by_tile, parts * owners)

    grad_conv = [gated_block(grad_out, outer_gate, step) for step in range(owners)]
    spec, conv_out = conv_of(plan, me, filt, after(filt, gated), by_block)
    for step in near:
        grad_conv[step] = after(conv_out[0], grad_conv[step])
    grad_conv = exchange(grad_conv, "grad_conv")
    conv = exchange(conv_out, "conv")
    tile_shape = (parts * cols, rows, height, side)
    back_out, term = grads_of(plan, me, filt, spec, grad_conv, by_block, tile_shape, by_tile)
    grad_gated = exchange(back_out, "grad_gated", last_order)

    term = after([conv[step] for step in far], term)
    term = lax.psum_scatter(term, ("dp", "col"), scatter_dimension=0, tiled=False)
    with jax.named_scope("rows_sum"):
        arrived = [pairwise(term[i], "row", i) for i in range(1, rows)]
    total = sum(arrived, term[0]) * (1.0 / side)
    with jax.named_scope("parts_gather"):
        others = [pairwise(total, "dp", i) for i in range(1, parts)]
    pieces = jnp.stack([total] + others)
    bit = 1
    while bit < parts:
        upper = (lax.axis_index("dp") & bit) != 0
        swapped = jnp.flip(pieces.reshape(parts // (2 * bit), 2, bit, height, side), 1)
        pieces = jnp.where(upper, swapped.reshape(pieces.shape), pieces)
        bit *= 2
    grad_filter = pieces.reshape(block, side)

    every = [0] + last_order
    (grad_outer,) = gated_by(me, every, [conv[step] for step in every], [grad_out[0]])
    gates = [signal[0], inner_gate[0]]
    early, late = every[:-1], every[-1:]
    done = gated_by(me, early, [grad_gated[step] for step in early], gates)
    grad_inner, grad_signal = gated_by(me, late, [grad_gated[step] for step in late], gates, done)
    return (grad_outer[None], grad_inner[None], grad_signal[None], grad_filter)


def powers_of_two(*sizes):
    return all(size & (size - 1) == 0 for size in sizes)


def shards(*arrays):
    parts, rows, cols = (lax.axis_size(name) for name in ("dp", "row", "col"))
    side = arrays[0].shape[3]
    whole = arrays[0].shape[1] == rows * cols and rows >= 2 and cols == 2
    fits = powers_of_two(parts, rows, cols, side) and side // 4 % LANE_PAD == 0
    fits = fits and arrays[4].shape[0] // parts % ROW_PAD == 0
    return (channel_shards if whole and fits else spread_shards)(*arrays)


def solution(mesh):
    placed = (
        P("dp", None, ("row", "col"), None),
        P("dp", None, ("row", "col"), None),
        P("dp", None, ("row", "col"), None),
        P("dp", None, ("row", "col"), None),
        P(("row", "col"), None),
    )
    return jax.shard_map(
        shards,
        mesh=mesh,
        in_specs=placed,
        out_specs=(
            P("dp", None, ("row", "col"), None),
            P("dp", None, ("row", "col"), None),
            P("dp", None, ("row", "col"), None),
            P(("row", "col"), None),
        ),
        check_vma=False,
    )
```

profile of v0, /device:TPU:7, one launch (start us, length us, event | category | flops | bytes accessed | tf_op | source)
XLA Modules:
  0.0 438.2 jit_solution(16346140802679948569)
XLA Ops:
  10.3 3.3 collective-permute-start
  13.6 3.1 multiply_bitcast_fusion.8
  17.2 4.7 %collective-permute-start.2 = (f32[128,1024]{1,0:T(8,128)}, f32[128,1024]{1,0:T(8,128)S(1)}, u32[]{:S(2)}, u32[]{:S(2)}) collective-permute-start(f32[128,1024]{1,0:T(8,128)} %get-tuple-element.139), channel_id=1, source_target_pairs={{0,7},{1,6},{2,5},{3,4},{4,3},{5,2},{6,1},{7,0},{8,15},{9,14},{10,... | collective-permute-start | bytes 1572872 | tf_op jit(solution)/shard_map/gated_7/ppermute | solution.py:496
  22.8 5.3 %collective-permute-done.refs_6_ = f32[160,1024]{1,0:T(8,128)S(1)} collective-permute-done((f32[160,1024]{1,0:T(8,128)}, f32[160,1024]{1,0:T(8,128)S(1)}, u32[]{:S(2)}, u32[]{:S(2)}) %collective-permute-start) | collective-permute-done | bytes 655392 | tf_op jit(solution)/shard_map/gated_6/ppermute | solution.py:496
  28.2 52.5 %collective-permute-done.1.refs_4_ = f32[160,1024]{1,0:T(8,128)S(1)} collective-permute-done((f32[160,1024]{1,0:T(8,128)S(1)}, f32[160,1024]{1,0:T(8,128)S(1)}, u32[]{:S(2)}, u32[]{:S(2)}) %collective-permute-start.1) | collective-permute-done | bytes 655392 | tf_op jit(solution)/shard_map/gated_4/ppermute | solution.py:496
  84.7 30.4 %collective-permute-done.3.refs_5_ = f32[128,1024]{1,0:T(8,128)} collective-permute-done((f32[128,1024]{1,0:T(8,128)}, f32[128,1024]{1,0:T(8,128)}, u32[]{:S(2)}, u32[]{:S(2)}) %collective-permute-start.3) | collective-permute-done | bytes 524320 | tf_op jit(solution)/shard_map/gated_5/ppermute | solution.py:496
  115.4 4.5 %multiply_bitcast_fusion = (f32[128,1024]{1,0:T(8,128)}, f32[128,1024]{1,0:T(8,128)}, f32[128,1024]{1,0:T(8,128)}, f32[128,1024]{1,0:T(8,128)}, f32[128,1024]{1,...) fusion(bf16[1,8,128,1024]{3,2,1,0:T(8,128)(2,1)} %param.11, s32[]{:T(128)S(6)} %select_n.85, ...), kind=kLoop, calls=%fused_computation.8 | loop fusion | flops 3145728 | bytes 8388640 | tf_op jit(solution)/shard_map/mul | solution.py:585
  119.9 2.2 collective-permute-start.7
  122.1 7.1 %collective-permute-done.6.refs_3_ = f32[128,1024]{1,0:T(8,128)S(1)} collective-permute-done((f32[128,1024]{1,0:T(8,128)}, f32[128,1024]{1,0:T(8,128)S(1)}, u32[]{:S(2)}, u32[]{:S(2)}) %collective-permute-start.6) | collective-permute-done | bytes 524320 | tf_op jit(solution)/shard_map/gated_3/ppermute | solution.py:496
  134.5 16.6 %all-gather.3.cloned.1.call-done = f32[32,32,1024]{2,1,0:T(8,128)} async-done(((f32[4,32,1024]{2,1,0:T(8,128)}), f32[32,32,1024]{2,1,0:T(8,128)}) %all-gather.3.cloned.1.call-update) | async-done | bytes 4194320 | tf_op jit(solution)/shard_map/all_gather | solution.py:616
  151.1 2.2 copy-done
  153.3 2.2 copy-done.1
  156.7 2.2 copy-done.11
  159.0 14.4 %filter_spectrum.1.filt = f32[2,528,1024]{2,1,0:T(8,128)S(1)} custom-call(s32[1]{0:T(128)} %bitcast.me, f32[8,4,32,1024]{3,2,1,0:T(8,128)S(1)} %bitcast.87, bf16[2,544,512]{2,1,0:T(8,128)(2,1)S(1)} %copy-done.4, bf16[2,512,512]{2,1,0:T(8,128)(2,1)S(1)} %copy-done.5, f32[2,528,1024]{2,1,0:T(8,128)S(1)} %copy-done, bf16[2,4,512,512]{3,2,1,0:T(8,128)(2,1)S(1)} %copy-done.1), custom_call_target="tpu_custom_call" | custom-call | flops 1048576 | bytes 1048576 | tf_op jit(solution)/shard_map/filter_spectrum/pallas_call | solution.py:415
  173.6 22.6 %conv_of.1 = (f32[2,528,1024]{2,1,0:T(8,128)S(1)}, f32[128,1024]{1,0:T(8,128)S(1)}, f32[128,1024]{1,0:T(8,128)S(1)}, f32[128,1024]{1,0:T(8,128)S(1)}, f32[128,10...) custom-call(s32[1]{0:T(128)} %bitcast.me, ...), custom_call_target="tpu_custom_call" | custom-call | flops 1048576 | bytes 1048576 | tf_op jit(solution)/shard_map/conv_of/pallas_call | solution.py:415
  201.7 12.4 %collective-permute-done.10.refs_5_ = f32[128,1024]{1,0:T(8,128)} collective-permute-done((f32[128,1024]{1,0:T(8,128)}, f32[128,1024]{1,0:T(8,128)}, u32[]{:S(2)}, u32[]{:S(2)}) %collective-permute-start.10) | collective-permute-done | bytes 524320 | tf_op jit(solution)/shard_map/grad_conv_5/ppermute | solution.py:496
  214.0 2.2 collective-permute-start.11
  216.2 8.5 %collective-permute-done.12.refs_3_ = f32[128,1024]{1,0:T(8,128)S(1)} collective-permute-done((f32[128,1024]{1,0:T(8,128)S(1)}, f32[128,1024]{1,0:T(8,128)S(1)}, u32[]{:S(2)}, u32[]{:S(2)}) %collective-permute-start.12) | collective-permute-done | bytes 524320 | tf_op jit(solution)/shard_map/grad_conv_3/ppermute | solution.py:496
  225.4 21.7 %collective-permute-done.14.refs_2_ = f32[128,1024]{1,0:T(8,128)S(1)} collective-permute-done((f32[128,1024]{1,0:T(8,128)S(1)}, f32[128,1024]{1,0:T(8,128)S(1)}, u32[]{:S(2)}, u32[]{:S(2)}) %collective-permute-start.14) | collective-permute-done | bytes 524320 | tf_op jit(solution)/shard_map/grad_conv_2/ppermute | solution.py:496
  247.0 3.2 collective-permute-start.15
  250.3 42.3 %grads_of.1 = (f32[128,1024]{1,0:T(8,128)S(1)}, f32[128,1024]{1,0:T(8,128)S(1)}, f32[128,1024]{1,0:T(8,128)S(1)}, f32[128,1024]{1,0:T(8,128)S(1)}, f32[128,1024]...) custom-call(s32[1]{0:T(128)} %bitcast.me, ...), custom_call_target="tpu_custom_call" | custom-call | flops 1048576 | bytes 1048576 | tf_op jit(solution)/shard_map/grads_of/pallas_call | solution.py:415
  302.6 2.9 collective-permute-done.20.refs_7_
  309.5 11.2 %collective-permute-done.17.refs_4_ = f32[128,1024]{1,0:T(8,128)S(1)} collective-permute-done((f32[128,1024]{1,0:T(8,128)}, f32[128,1024]{1,0:T(8,128)S(1)}, u32[]{:S(2)}, u32[]{:S(2)}) %collective-permute-start.17) | collective-permute-done | bytes 524320 | tf_op jit(solution)/shard_map/conv_3/ppermute | solution.py:496
  321.8 27.3 %collective-permute-done.18.refs_5_ = f32[128,1024]{1,0:T(8,128)S(1)} collective-permute-done((f32[128,1024]{1,0:T(8,128)}, f32[128,1024]{1,0:T(8,128)S(1)}, u32[]{:S(2)}, u32[]{:S(2)}) %collective-permute-start.18) | collective-permute-done | bytes 524320 | tf_op jit(solution)/shard_map/conv_2/ppermute | solution.py:496
  349.9 2.6 collective-permute-start.23
  356.5 3.1 collective-permute-start.30
  362.0 10.8 %collective-permute-done.22.refs_2_ = f32[128,1024]{1,0:T(8,128)} collective-permute-done((f32[128,1024]{1,0:T(8,128)}, f32[128,1024]{1,0:T(8,128)}, u32[]{:S(2)}, u32[]{:S(2)}) %collective-permute-start.22) | collective-permute-done | bytes 524320 | tf_op jit(solution)/shard_map/grad_gated_4/ppermute | solution.py:496
  374.3 13.9 %collective-permute-start.24 = (f32[128,1024]{1,0:T(8,128)}, f32[128,1024]{1,0:T(8,128)}, u32[]{:S(2)}, u32[]{:S(2)}) collective-permute-start(f32[128,1024]{1,0:T(8,128)} %copy-done.48), channel_id=1, source_target_pairs={{0,5},{1,4},{2,7},{3,6},{4,1},{5,0},{6,3},{7,2},{8,13},{9,12},{10,... | collective-permute-start | bytes 1572872 | tf_op jit(solution)/shard_map/grad_gated_5/ppermute | solution.py:496
  388.2 4.4 %collective-permute-done.29 = f32[32,1024]{1,0:T(8,128)S(1)} collective-permute-done((f32[32,1024]{1,0:T(8,128)S(1)}, f32[32,1024]{1,0:T(8,128)S(1)}, u32[]{:S(2)}, u32[]{:S(2)}) %collective-permute-start.29) | collective-permute-done | bytes 131104 | tf_op jit(solution)/shard_map/rows_sum/ppermute | solution.py:496
  394.7 12.0 %collective-permute-done.28 = f32[32,1024]{1,0:T(8,128)S(1)} collective-permute-done((f32[32,1024]{1,0:T(8,128)S(1)}, f32[32,1024]{1,0:T(8,128)S(1)}, u32[]{:S(2)}, u32[]{:S(2)}) %collective-permute-start.28) | collective-permute-done | bytes 131104 | tf_op jit(solution)/shard_map/rows_sum/ppermute | solution.py:496
  419.8 3.5 gate_out.3
  423.3 4.1 gate_out.4
  (193 shorter events, 64.2 us)
Async XLA Ops:
  7.2 143.9 %all-gather.3.cloned.1.call-start = ((), (), s32[]{:S(2)}) async-start(), calls=%async_computation.2 | async-start | bytes 4718592 | tf_op jit(solution)/shard_map/all_gather | solution.py:616
  10.3 17.9 %collective-permute-start = (f32[160,1024]{1,0:T(8,128)}, f32[160,1024]{1,0:T(8,128)S(1)}, u32[]{:S(2)}, u32[]{:S(2)}) collective-permute-start(f32[160,1024]{1,0:T(8,128)} %pad_maximum_fusion.2), channel_id=1, source_target_pairs={{0,6},{1,7},{2,4},{3,5},{4,2},{5,3},{6,0},{7,1},{8,14},{9,15},{10,... | collective-permute-start | bytes 1966088 | tf_op jit(solution)/shard_map/gated_6/ppermute | solution.py:496
  16.9 63.8 %collective-permute-start.1 = (f32[160,1024]{1,0:T(8,128)S(1)}, f32[160,1024]{1,0:T(8,128)S(1)}, u32[]{:S(2)}, u32[]{:S(2)}) collective-permute-start(f32[160,1024]{1,0:T(8,128)S(1)} %get-tuple-element.145), channel_id=1, source_target_pairs={{0,4},{1,5},{2,6},{3,7},{4,0},{5,1},{6,2},{7,3},{8,12},{9,13},{10,... | collective-permute-start | bytes 1966088 | tf_op jit(solution)/shard_map/gated_4/ppermute | solution.py:496
  17.0 66.0 %collective-permute-start.4 = (f32[160,1024]{1,0:T(8,128)S(1)}, f32[160,1024]{1,0:T(8,128)S(1)}, u32[]{:S(2)}, u32[]{:S(2)}) collective-permute-start(f32[160,1024]{1,0:T(8,128)S(1)} %get-tuple-element.144), channel_id=1, source_target_pairs={{0,2},{1,3},{2,0},{3,1},{4,6},{5,7},{6,4},{7,5},{8,10},{9,11},{10,... | collective-permute-start | bytes 1966088 | tf_op jit(solution)/shard_map/gated_2/ppermute | solution.py:496
  17.2 67.5 %collective-permute-start.2 = (f32[128,1024]{1,0:T(8,128)}, f32[128,1024]{1,0:T(8,128)S(1)}, u32[]{:S(2)}, u32[]{:S(2)}) collective-permute-start(f32[128,1024]{1,0:T(8,128)} %get-tuple-element.139), channel_id=1, source_target_pairs={{0,7},{1,6},{2,5},{3,4},{4,3},{5,2},{6,1},{7,0},{8,15},{9,14},{10,... | collective-permute-start | bytes 1572872 | tf_op jit(solution)/shard_map/gated_7/ppermute | solution.py:496
  80.7 34.5 %collective-permute-start.3 = (f32[128,1024]{1,0:T(8,128)}, f32[128,1024]{1,0:T(8,128)}, u32[]{:S(2)}, u32[]{:S(2)}) collective-permute-start(f32[128,1024]{1,0:T(8,128)} %get-tuple-element.67), channel_id=1, source_target_pairs={{0,5},{1,4},{2,7},{3,6},{4,1},{5,0},{6,3},{7,2},{8,13},{9,12},{10,... | collective-permute-start | bytes 1572872 | tf_op jit(solution)/shard_map/gated_5/ppermute | solution.py:496
  115.2 240.3 %reduce-scatter.2.cloned.1.call-start = ((), (), s32[]{:S(2)}) async-start(), calls=%async_computation.1 | async-start | bytes 4718592 | tf_op jit(solution)/shard_map/reduce_scatter | solution.py:630
  119.9 79.6 %collective-permute-start.7 = (f32[128,1024]{1,0:T(8,128)}, f32[128,1024]{1,0:T(8,128)}, u32[]{:S(2)}, u32[]{:S(2)}) collective-permute-start(f32[128,1024]{1,0:T(8,128)} %get-tuple-element.80), channel_id=1, source_target_pairs={{0,6},{1,7},{2,4},{3,5},{4,2},{5,3},{6,0},{7,1},{8,14},{9,15},{10,... | collective-permute-start | bytes 1572872 | tf_op jit(solution)/shard_map/grad_conv_6/ppermute | solution.py:496
  130.0 70.9 %collective-permute-start.8 = (f32[128,1024]{1,0:T(8,128)}, f32[128,1024]{1,0:T(8,128)}, u32[]{:S(2)}, u32[]{:S(2)}) collective-permute-start(f32[128,1024]{1,0:T(8,128)} %get-tuple-element.81), channel_id=1, source_target_pairs={{0,4},{1,5},{2,6},{3,7},{4,0},{5,1},{6,2},{7,3},{8,12},{9,13},{10,... | collective-permute-start | bytes 1572872 | tf_op jit(solution)/shard_map/grad_conv_4/ppermute | solution.py:496
  130.8 70.3 %collective-permute-start.9 = (f32[128,1024]{1,0:T(8,128)}, f32[128,1024]{1,0:T(8,128)}, u32[]{:S(2)}, u32[]{:S(2)}) collective-permute-start(f32[128,1024]{1,0:T(8,128)} %get-tuple-element.82), channel_id=1, source_target_pairs={{0,7},{1,6},{2,5},{3,4},{4,3},{5,2},{6,1},{7,0},{8,15},{9,14},{10,... | collective-permute-start | bytes 1572872 | tf_op jit(solution)/shard_map/grad_conv_7/ppermute | solution.py:496
  133.7 80.3 %collective-permute-start.10 = (f32[128,1024]{1,0:T(8,128)}, f32[128,1024]{1,0:T(8,128)}, u32[]{:S(2)}, u32[]{:S(2)}) collective-permute-start(f32[128,1024]{1,0:T(8,128)} %get-tuple-element.83), channel_id=1, source_target_pairs={{0,5},{1,4},{2,7},{3,6},{4,1},{5,0},{6,3},{7,2},{8,13},{9,12},{10,... | collective-permute-start | bytes 1572872 | tf_op jit(solution)/shard_map/grad_conv_5/ppermute | solution.py:496
  199.5 25.3 %collective-permute-start.12 = (f32[128,1024]{1,0:T(8,128)S(1)}, f32[128,1024]{1,0:T(8,128)S(1)}, u32[]{:S(2)}, u32[]{:S(2)}) collective-permute-start(f32[128,1024]{1,0:T(8,128)S(1)} %copy-done.60), channel_id=1, source_target_pairs={{0,3},{1,2},{2,1},{3,0},{4,7},{5,6},{6,5},{7,4},{8,11},{9,10},{10,... | collective-permute-start | bytes 1572872 | tf_op jit(solution)/shard_map/grad_conv_3/ppermute | solution.py:496
  200.8 46.2 %collective-permute-start.14 = (f32[128,1024]{1,0:T(8,128)S(1)}, f32[128,1024]{1,0:T(8,128)S(1)}, u32[]{:S(2)}, u32[]{:S(2)}) collective-permute-start(f32[128,1024]{1,0:T(8,128)S(1)} %copy-done.59), channel_id=1, source_target_pairs={{0,2},{1,3},{2,0},{3,1},{4,6},{5,7},{6,4},{7,5},{8,10},{9,11},{10,... | collective-permute-start | bytes 1572872 | tf_op jit(solution)/shard_map/grad_conv_2/ppermute | solution.py:496
  201.1 49.1 %collective-permute-start.16 = (f32[128,1024]{1,0:T(8,128)S(1)}, f32[128,1024]{1,0:T(8,128)S(1)}, u32[]{:S(2)}, u32[]{:S(2)}) collective-permute-start(f32[128,1024]{1,0:T(8,128)S(1)} %copy-done.58), channel_id=1, source_target_pairs={{0,1},{1,0},{2,3},{3,2},{4,5},{5,4},{6,7},{7,6},{8,9},{9,8},{10,11... | collective-permute-start | bytes 1572872 | tf_op jit(solution)/shard_map/grad_conv_1/ppermute | solution.py:496
  214.0 86.1 %collective-permute-start.11 = (f32[128,1024]{1,0:T(8,128)S(1)}, f32[128,1024]{1,0:T(8,128)S(1)}, u32[]{:S(2)}, u32[]{:S(2)}) collective-permute-start(f32[128,1024]{1,0:T(8,128)S(1)} %get-tuple-element.85), channel_id=1, source_target_pairs={{0,6},{1,7},{2,4},{3,5},{4,2},{5,3},{6,0},{7,1},{8,14},{9,15},{10,... | collective-permute-start | bytes 1572872 | tf_op jit(solution)/shard_map/conv_6/ppermute | solution.py:496
  224.8 76.2 %collective-permute-start.13 = (f32[128,1024]{1,0:T(8,128)S(1)}, f32[128,1024]{1,0:T(8,128)S(1)}, u32[]{:S(2)}, u32[]{:S(2)}) collective-permute-start(f32[128,1024]{1,0:T(8,128)S(1)} %get-tuple-element.89), channel_id=1, source_target_pairs={{0,4},{1,5},{2,6},{3,7},{4,0},{5,1},{6,2},{7,3},{8,12},{9,13},{10,... | collective-permute-start | bytes 1572872 | tf_op jit(solution)/shard_map/conv_4/ppermute | solution.py:496
  247.0 54.7 %collective-permute-start.15 = (f32[128,1024]{1,0:T(8,128)S(1)}, f32[128,1024]{1,0:T(8,128)S(1)}, u32[]{:S(2)}, u32[]{:S(2)}) collective-permute-start(f32[128,1024]{1,0:T(8,128)S(1)} %get-tuple-element.93), channel_id=1, source_target_pairs={{0,7},{1,6},{2,5},{3,4},{4,3},{5,2},{6,1},{7,0},{8,15},{9,14},{10,... | collective-permute-start | bytes 1572872 | tf_op jit(solution)/shard_map/conv_7/ppermute | solution.py:496
  250.2 55.2 %collective-permute-start.20 = (f32[128,1024]{1,0:T(8,128)S(1)}, f32[128,1024]{1,0:T(8,128)S(1)}, u32[]{:S(2)}, u32[]{:S(2)}) collective-permute-start(f32[128,1024]{1,0:T(8,128)S(1)} %get-tuple-element.103), channel_id=1, source_target_pairs={{0,5},{1,4},{2,7},{3,6},{4,1},{5,0},{6,3},{7,2},{8,13},{9,12},{10,... | collective-permute-start | bytes 1572872 | tf_op jit(solution)/shard_map/conv_5/ppermute | solution.py:496
  306.4 42.7 %collective-permute-start.18 = (f32[128,1024]{1,0:T(8,128)}, f32[128,1024]{1,0:T(8,128)S(1)}, u32[]{:S(2)}, u32[]{:S(2)}) collective-permute-start(f32[128,1024]{1,0:T(8,128)} %copy-done.53), channel_id=1, source_target_pairs={{0,2},{1,3},{2,0},{3,1},{4,6},{5,7},{6,4},{7,5},{8,10},{9,11},{10,... | collective-permute-start | bytes 1572872 | tf_op jit(solution)/shard_map/conv_2/ppermute | solution.py:496
  308.1 44.4 %collective-permute-start.19 = (f32[128,1024]{1,0:T(8,128)}, f32[128,1024]{1,0:T(8,128)S(1)}, u32[]{:S(2)}, u32[]{:S(2)}) collective-permute-start(f32[128,1024]{1,0:T(8,128)} %copy-done.52), channel_id=1, source_target_pairs={{0,1},{1,0},{2,3},{3,2},{4,5},{5,4},{6,7},{7,6},{8,9},{9,8},{10,11... | collective-permute-start | bytes 1572872 | tf_op jit(solution)/shard_map/conv_1/ppermute | solution.py:496
  308.5 51.4 %collective-permute-start.21 = (f32[128,1024]{1,0:T(8,128)}, f32[128,1024]{1,0:T(8,128)}, u32[]{:S(2)}, u32[]{:S(2)}) collective-permute-start(f32[128,1024]{1,0:T(8,128)} %copy-done.57), channel_id=1, source_target_pairs={{0,6},{1,7},{2,4},{3,5},{4,2},{5,3},{6,0},{7,1},{8,14},{9,15},{10,... | collective-permute-start | bytes 1572872 | tf_op jit(solution)/shard_map/grad_gated_6/ppermute | solution.py:496
  321.6 51.2 %collective-permute-start.22 = (f32[128,1024]{1,0:T(8,128)}, f32[128,1024]{1,0:T(8,128)}, u32[]{:S(2)}, u32[]{:S(2)}) collective-permute-start(f32[128,1024]{1,0:T(8,128)} %copy-done.56), channel_id=1, source_target_pairs={{0,4},{1,5},{2,6},{3,7},{4,0},{5,1},{6,2},{7,3},{8,12},{9,13},{10,... | collective-permute-start | bytes 1572872 | tf_op jit(solution)/shard_map/grad_gated_4/ppermute | solution.py:496
  349.9 22.9 %collective-permute-start.23 = (f32[128,1024]{1,0:T(8,128)}, f32[128,1024]{1,0:T(8,128)}, u32[]{:S(2)}, u32[]{:S(2)}) collective-permute-start(f32[128,1024]{1,0:T(8,128)} %copy-done.55), channel_id=1, source_target_pairs={{0,7},{1,6},{2,5},{3,4},{4,3},{5,2},{6,1},{7,0},{8,15},{9,14},{10,... | collective-permute-start | bytes 1572872 | tf_op jit(solution)/shard_map/grad_gated_7/ppermute | solution.py:496
  356.5 17.8 %collective-permute-start.30 = (f32[32,1024]{1,0:T(8,128)S(1)}, f32[32,1024]{1,0:T(8,128)S(1)}, u32[]{:S(2)}, u32[]{:S(2)}) collective-permute-start(f32[32,1024]{1,0:T(8,128)S(1)} %get-tuple-element.142), channel_id=1, source_target_pairs={{0,6},{2,4},{4,2},{6,0},{1,7},{3,5},{5,3},{7,1},{8,14},{10,12},{12... | collective-permute-start | bytes 393224 | tf_op jit(solution)/shard_map/rows_sum/ppermute | solution.py:496
  359.7 49.0 %collective-permute-start.25 = (f32[128,1024]{1,0:T(8,128)}, f32[128,1024]{1,0:T(8,128)S(1)}, u32[]{:S(2)}, u32[]{:S(2)}) collective-permute-start(f32[128,1024]{1,0:T(8,128)} %copy-done.51), channel_id=1, source_target_pairs={{0,3},{1,2},{2,1},{3,0},{4,7},{5,6},{6,5},{7,4},{8,11},{9,10},{10,... | collective-permute-start | bytes 1572872 | tf_op jit(solution)/shard_map/grad_gated_3/ppermute | solution.py:496
  359.9 50.7 %collective-permute-start.26 = (f32[128,1024]{1,0:T(8,128)}, f32[128,1024]{1,0:T(8,128)S(1)}, u32[]{:S(2)}, u32[]{:S(2)}) collective-permute-start(f32[128,1024]{1,0:T(8,128)} %copy-done.50), channel_id=1, source_target_pairs={{0,2},{1,3},{2,0},{3,1},{4,6},{5,7},{6,4},{7,5},{8,10},{9,11},{10,... | collective-permute-start | bytes 1572872 | tf_op jit(solution)/shard_map/grad_gated_2/ppermute | solution.py:496
  372.8 19.8 %collective-permute-start.29 = (f32[32,1024]{1,0:T(8,128)S(1)}, f32[32,1024]{1,0:T(8,128)S(1)}, u32[]{:S(2)}, u32[]{:S(2)}) collective-permute-start(f32[32,1024]{1,0:T(8,128)S(1)} %get-tuple-element.143), channel_id=1, source_target_pairs={{0,4},{2,6},{4,0},{6,2},{1,5},{3,7},{5,1},{7,3},{8,12},{10,14},{12... | collective-permute-start | bytes 393224 | tf_op jit(solution)/shard_map/rows_sum/ppermute | solution.py:496
  372.8 50.5 %collective-permute-start.27 = (f32[128,1024]{1,0:T(8,128)}, f32[128,1024]{1,0:T(8,128)}, u32[]{:S(2)}, u32[]{:S(2)}) collective-permute-start(f32[128,1024]{1,0:T(8,128)} %copy-done.49), channel_id=1, source_target_pairs={{0,1},{1,0},{2,3},{3,2},{4,5},{5,4},{6,7},{7,6},{8,9},{9,8},{10,11... | collective-permute-start | bytes 1572872 | tf_op jit(solution)/shard_map/grad_gated_1/ppermute | solution.py:496
  374.3 53.1 %collective-permute-start.24 = (f32[128,1024]{1,0:T(8,128)}, f32[128,1024]{1,0:T(8,128)}, u32[]{:S(2)}, u32[]{:S(2)}) collective-permute-start(f32[128,1024]{1,0:T(8,128)} %copy-done.48), channel_id=1, source_target_pairs={{0,5},{1,4},{2,7},{3,6},{4,1},{5,0},{6,3},{7,2},{8,13},{9,12},{10,... | collective-permute-start | bytes 1572872 | tf_op jit(solution)/shard_map/grad_gated_5/ppermute | solution.py:496
  407.6 21.7 %collective-permute-start.33 = (f32[32,1024]{1,0:T(8,128)S(1)}, f32[32,1024]{1,0:T(8,128)S(1)}, u32[]{:S(2)}, u32[]{:S(2)}) collective-permute-start(f32[32,1024]{1,0:T(8,128)S(1)} %fusion.4), channel_id=1, source_target_pairs={{0,24},{8,16},{16,8},{24,0},{1,25},{9,17},{17,9},{25,1},{2,26},{10... | collective-permute-start | bytes 393224 | tf_op jit(solution)/shard_map/parts_gather/ppermute | solution.py:496
  409.5 19.9 %collective-permute-start.32 = (f32[32,1024]{1,0:T(8,128)S(1)}, f32[32,1024]{1,0:T(8,128)S(1)}, u32[]{:S(2)}, u32[]{:S(2)}) collective-permute-start(f32[32,1024]{1,0:T(8,128)S(1)} %fusion.4), channel_id=1, source_target_pairs={{0,16},{8,24},{16,0},{24,8},{1,17},{9,25},{17,1},{25,9},{2,18},{10... | collective-permute-start | bytes 393224 | tf_op jit(solution)/shard_map/parts_gather/ppermute | solution.py:496
  411.3 18.0 %collective-permute-start.31 = (f32[32,1024]{1,0:T(8,128)S(1)}, f32[32,1024]{1,0:T(8,128)}, u32[]{:S(2)}, u32[]{:S(2)}) collective-permute-start(f32[32,1024]{1,0:T(8,128)S(1)} %fusion.4), channel_id=1, source_target_pairs={{0,8},{8,0},{16,24},{24,16},{1,9},{9,1},{17,25},{25,17},{2,10},{10... | collective-permute-start | bytes 393224 | tf_op jit(solution)/shard_map/parts_gather/ppermute | solution.py:496
  (67 other events, 863.2 us)
Sparse Core Ops, SparseCore 0:
  115.3 35.7 all-gather.2
  306.4 49.0 reduce-scatter.1
where the time goes:
time: 442 us; the launch traced here: 438 us
  waiting for transfers between devices  225 us (51%)
  Pallas kernels  88.8 us (20%)
  starting transfers between devices  55.9 us (13%)
  local copies, waits for them, and re-layouts  38.3 us (9%)
  other arithmetic  15.4 us (3%)
  between operations  14.6 us (3%)
    ppermute x34, waiting for transfers between devices, pairwise(): lax.ppermute(block, axis, [(i, i ^ step) for i in range(lax.axis_size(axi...  207 us
    pallas_call x3, Pallas kernels, call_kernel(): pl.pallas_call(kernel, out_shape=out_shape, in_specs=in_specs, out_specs=...  79.3 us
    ppermute x34, starting transfers between devices, pairwise(): lax.ppermute(block, axis, [(i, i ^ step) for i in range(lax.axis_size(axi...  55.8 us
    unnamed x126, local copies, waits for them, and re-layouts  37.1 us
    all_gather x1, waiting for transfers between devices, channel_shards(): over_all = [lax.all_gather(over_row, ('dp', 'col'))]  16.6 us
    pallas_call x3, Pallas kernels, gated_by(): pl.pallas_call(functools.partial(gate_kernel, steps, len(gates)), grid_sp...  9.45 us
  transfers between devices with their start and end apart: 36, of which 15 were waited for; matrix products, arithmetic and copies ran while one was open for 3% of the time, Pallas kernels for 20%

commit v1 on v0

--- a/solution.py
+++ b/solution.py
@@ -165,7 +165,7 @@
 
 
 VMEM_LIMIT = 18 * 1024 * 1024
-UNDER_WAY = 4
+UNDER_WAY = 3
 ROW_PAD = 16
 LANE_PAD = 128
 
@@ -379,20 +379,23 @@
     wait_all(start_all(((to, source) for source, to in views(me, outs, values)), sems))
 
 
-def grads_kernel(plan, views, term_views, count, me, filt, gated, *refs):
+def term_kernel(plan, views, term_views, count, me, gated, *refs):
     blocks, tables = refs[:count], refs[count : count + 6]
     into_even, into_odd, back_even, back_odd, turn, mix = tables
-    outs, term = refs[count + 6 : 2 * count + 6], refs[2 * count + 6]
-    values, mid, spec, sems, term_sems = refs[2 * count + 7 :]
+    spec, term, values, mid, sems, term_sems = refs[count + 6 :]
     wait_all(start_all(views(me, blocks, values), sems))
     to_spectrum(plan, values, into_even, into_odd, turn, mix, spec, mid)
+    inverse_rows(plan, True, gated, spec, turn, mix, mid)
+    inverse_columns(plan, back_even, back_odd, mid, values)
+    wait_all(start_all(((to, source) for source, to in term_views(me, [term], values)), term_sems))
+
+
+def grad_kernel(plan, views, count, me, filt, spec, back_even, back_odd, turn, mix, *refs):
+    outs = refs[:count]
+    values, mid, sems = refs[count:]
     inverse_rows(plan, True, filt, spec, turn, mix, mid)
     inverse_columns(plan, back_even, back_odd, mid, values)
-    copies = start_all(((to, source) for source, to in views(me, outs, values)), sems)
-    inverse_rows(plan, True, gated, spec, turn, mix, mid)
-    wait_all(copies)
-    inverse_columns(plan, back_even, back_odd, mid, values)
-    wait_all(start_all(((to, source) for source, to in term_views(me, [term], values)), term_sems))
+    wait_all(start_all(((to, source) for source, to in views(me, outs, values)), sems))
 
 
 def smem():
@@ -470,26 +473,41 @@
     return spec, outs
 
 
-def grads_of(plan, me, filt, gated, blocks, views, term_shape, term_views):
+def term_of(plan, me, gated, blocks, views, term_shape, term_views):
     count = len(blocks)
     shape = (2, plan.rows, plan.side)
-    *outs, term = call_kernel(
+    return call_kernel(
         plan,
-        functools.partial(grads_kernel, plan, views, term_views, count),
-        "grads_of",
-        (me, filt, gated, *blocks, *tables_of(plan)),
-        [smem(), vmem(), vmem()] + [vmem()] * count + [vmem()] * 6,
-        [float_array((plan.side // count, plan.side))] * count + [float_array(term_shape)],
-        [vmem()] * count + [anywhere()],
+        functools.partial(term_kernel, plan, views, term_views, count),
+        "term_of",
+        (me, gated, *blocks, *tables_of(plan)),
+        [smem(), vmem()] + [vmem()] * count + [vmem()] * 6,
+        [float_array(shape), float_array(term_shape)],
+        [vmem(), anywhere()],
         [
             pltpu.VMEM((plan.side, plan.side), jnp.float32),
-            pltpu.VMEM(shape, jnp.float32),
             pltpu.VMEM(shape, jnp.float32),
             pltpu.SemaphoreType.DMA((count,)),
             pltpu.SemaphoreType.DMA((math.prod(term_shape[:2]),)),
         ],
     )
-    return outs, term
+
+
+def grad_of(plan, me, filt, spec, count, views):
+    return call_kernel(
+        plan,
+        functools.partial(grad_kernel, plan, views, count),
+        "grad_of",
+        (me, filt, spec, *tables_of(plan)[2:]),
+        [smem()] + [vmem()] * 6,
+        [float_array((plan.side // count, plan.side))] * count,
+        [vmem()] * count,
+        [
+            pltpu.VMEM((plan.side, plan.side), jnp.float32),
+            pltpu.VMEM((2, plan.rows, plan.side), jnp.float32),
+            pltpu.SemaphoreType.DMA((count,)),
+        ],
+    )
 
 
 def pairwise(block, axis, step):
@@ -561,9 +579,10 @@
     )(me, *blocks, *gates, *done)
 
 
-def send_order(owners):
-    far = sorted(range(owners // 2, owners), key=lambda s: (s & 1, -s))
-    return far + sorted(range(1, owners // 2), reverse=True)
+def send_order(owners, cols):
+    far = sorted(range(owners // 2, owners), key=lambda s: (-s // cols, -s))
+    near = sorted(range(1, owners // 2), key=lambda s: (s % cols, -s))
+    return far, near
 
 
 def channel_shards(outer_gate, inner_gate, signal, grad_out, filter_weight):
@@ -573,10 +592,11 @@
     owners = rows * cols
     place = own_block()
     me = jnp.reshape(place, (1,)).astype(jnp.int32)
-    order = send_order(owners)
-    far, near = order[: owners // 2], order[owners // 2 :]
-    mixed_order = far[:1] + [step for pair in zip(far[1:], sorted(near, key=lambda s: s % cols)) for step in pair]
-    last_order = far[:-1] + near + far[-1:]
+    far, near = send_order(owners, cols)
+    order = far[:2]
+    for i in range(2, len(far)):
+        order = order + near[i - 2 : i - 1] + far[i : i + 1]
+    order = order[:-1] + near[len(far) - 2 :] + order[-1:]
     by_block = functools.partial(block_views, plan, owners)
     by_tile = functools.partial(tile_views, plan, (parts, rows, cols))
 
@@ -586,17 +606,25 @@
             jnp.float32
         ) * lax.dynamic_index_in_dim(right[0], at, 0, False).astype(jnp.float32)
 
-    sent = []
-
-    def exchange(blocks, what, order=order):
+    crossed, neared = [], []
+
+    def exchange(blocks, what, order, extra=None):
         got = [blocks[0]] + [None] * (owners - 1)
+        before, near_before = len(crossed), list(neared)
+        neared.clear()
         for step in order:
-            mine = blocks[step]
-            if len(sent) >= UNDER_WAY:
-                mine = after(sent[: len(sent) - UNDER_WAY + 1][-owners:], mine)
+            mine, waits = blocks[step], []
+            if step in far:
+                waits = crossed[max(0, len(crossed) - UNDER_WAY - 1) : max(0, len(crossed) - UNDER_WAY + 1)]
+                if len(crossed) - before >= len(far) // 2:
+                    waits = waits + near_before
+            elif before:
+                waits = crossed[before - 1 : before]
+            if waits:
+                mine = after(waits, mine)
             with jax.named_scope(f"{what}_{step}"):
                 got[step] = pairwise(mine, ("row", "col"), step)
-            sent.append(got[step])
+            (crossed if step in far else neared).append(got[step])
         return got
 
     height = block // parts
@@ -610,27 +638,30 @@
             gated[step] = jnp.concatenate([gated[step], own_part])
         if step == order[0]:
             inner, values = after(gated[step], [inner_gate, signal])
-    gated = exchange(gated, "gated", mixed_order)
+    gated = exchange(gated, "gated", order)
     over_row = jnp.stack([own_part] + [gated[i * cols][block:] for i in range(1, rows)])
-    over_row = after([gated[step] for step in far], over_row)
+    grad_conv = [gated_block(grad_out, outer_gate, step) for step in range(owners)]
+    over_row = after([gated[step] for step in far] + grad_conv, over_row)
     over_all = [lax.all_gather(over_row, ("dp", "col"))]
     filt = filter_spectrum(plan, me, over_all, by_tile, parts * owners)
 
-    grad_conv = [gated_block(grad_out, outer_gate, step) for step in range(owners)]
     spec, conv_out = conv_of(plan, me, filt, after(filt, gated), by_block)
-    for step in near:
-        grad_conv[step] = after(conv_out[0], grad_conv[step])
-    grad_conv = exchange(grad_conv, "grad_conv")
-    conv = exchange(conv_out, "conv")
+    grad_conv[near[-1]] = after(conv_out[0], grad_conv[near[-1]])
+    grad_conv = exchange(grad_conv, "grad_conv", order)
+    conv = exchange(conv_out, "conv", order)
     tile_shape = (parts * cols, rows, height, side)
-    back_out, term = grads_of(plan, me, filt, spec, grad_conv, by_block, tile_shape, by_tile)
-    grad_gated = exchange(back_out, "grad_gated", last_order)
-
-    term = after([conv[step] for step in far], term)
+    cot, term = term_of(plan, me, spec, grad_conv, by_block, tile_shape, by_tile)
+    back_out = grad_of(plan, me, filt, cot, owners, by_block)
+    grad_gated = exchange(back_out, "grad_gated", order)
+
+    term = after([conv[step] for step in far[:2]], term)
     term = lax.psum_scatter(term, ("dp", "col"), scatter_dimension=0, tiled=False)
     with jax.named_scope("rows_sum"):
         arrived = [pairwise(term[i], "row", i) for i in range(1, rows)]
     total = sum(arrived, term[0]) * (1.0 / side)
+    every = [0] + order
+    (grad_outer,) = gated_by(me, every, [conv[step] for step in every], [grad_out[0]])
+    total = after(grad_outer, total)
     with jax.named_scope("parts_gather"):
         others = [pairwise(total, "dp", i) for i in range(1, parts)]
     pieces = jnp.stack([total] + others)
@@ -642,8 +673,6 @@
         bit *= 2
     grad_filter = pieces.reshape(block, side)
 
-    every = [0] + last_order
-    (grad_outer,) = gated_by(me, every, [conv[step] for step in every], [grad_out[0]])
     gates = [signal[0], inner_gate[0]]
     early, late = every[:-1], every[-1:]
     done = gated_by(me, early, [grad_gated[step] for step in early], gates)

time: 442 us -> 426 us (0.964)
  waiting for transfers between devices: 225 us -> 136 us
  starting transfers between devices: 55.9 us -> 117 us
  local copies, waits for them, and re-layouts: 38.3 us -> 52.7 us
    ppermute x34, waiting for transfers between devices: 207 us -> 122 us  [pairwise(): lax.ppermute(block, axis, [(i, i ^ step) for i in range(lax.axis_size(axi...]
    ppermute x34, starting transfers between devices: 55.8 us -> 117 us  [pairwise(): lax.ppermute(block, axis, [(i, i ^ step) for i in range(lax.axis_size(axi...]
    all_gather x1, waiting for transfers between devices: 16.6 us -> 0.01 us  [channel_shards(): over_all = [lax.all_gather(over_row, ('dp', 'col'))]]
    unnamed x126 -> x134, local copies, waits for them, and re-layouts: 37.1 us -> 51.6 us
    reduce_scatter x1, waiting for transfers between devices: 2.12 us -> 13.2 us  [channel_shards(): lax.psum_scatter(term, ('dp', 'col'), scatter_dimension=0, tiled=False)]
    pallas_call x3 -> x4, Pallas kernels: 79.3 us -> 82.5 us  [call_kernel(): pl.pallas_call(kernel, out_shape=out_shape, in_specs=in_specs, out_specs=...]
  transfers between devices with their start and end apart: 36 -> 36, of which waited for: 15 -> 10; matrix products, arithmetic and copies ran while one was open for 3% -> 3% of each run, Pallas kernels for 20% -> 22%
where the time goes in v1:
time: 426 us; the launch traced here: 424 us
  waiting for transfers between devices  136 us (32%)
  starting transfers between devices  117 us (27%)
  Pallas kernels  92.2 us (22%)
  local copies, waits for them, and re-layouts  52.7 us (12%)
  between operations  14.6 us (3%)
  other arithmetic  11.9 us (3%)
    ppermute x34, waiting for transfers between devices, pairwise(): lax.ppermute(block, axis, [(i, i ^ step) for i in range(lax.axis_size(axi...  122 us
    ppermute x34, starting transfers between devices, pairwise(): lax.ppermute(block, axis, [(i, i ^ step) for i in range(lax.axis_size(axi...  117 us
    pallas_call x4, Pallas kernels, call_kernel(): pl.pallas_call(kernel, out_shape=out_shape, in_specs=in_specs, out_specs=...  82.5 us
    unnamed x134, local copies, waits for them, and re-layouts  51.6 us
    reduce_scatter x1, waiting for transfers between devices, channel_shards(): lax.psum_scatter(term, ('dp', 'col'), scatter_dimension=0, tiled=False)  13.2 us
    pallas_call x3, Pallas kernels, gated_by(): pl.pallas_call(functools.partial(gate_kernel, steps, len(gates)), grid_sp...  9.71 us
  transfers between devices with their start and end apart: 36, of which 10 were waited for; matrix products, arithmetic and copies ran while one was open for 3% of the time, Pallas kernels for 22%

profile of v1, /device:TPU:7, one launch (start us, length us, event | category | flops | bytes accessed | tf_op | source)
XLA Modules:
  0.0 424.2 jit_solution(3565198858998422239)
XLA Ops:
  8.3 3.9 collective-permute-start
  13.2 3.8 multiply_bitcast_fusion
  17.3 3.7 collective-permute-start.2
  22.0 2.9 collective-permute-done.refs_7_
  24.9 25.6 %collective-permute-start.3 = (f32[160,1024]{1,0:T(8,128)S(1)}, f32[160,1024]{1,0:T(8,128)S(1)}, u32[]{:S(2)}, u32[]{:S(2)}) collective-permute-start(f32[160,1024]{1,0:T(8,128)S(1)} %get-tuple-element.65), channel_id=1, source_target_pairs={{0,4},{1,5},{2,6},{3,7},{4,0},{5,1},{6,2},{7,3},{8,12},{9,13},{10,... | collective-permute-start | bytes 1966088 | tf_op jit(solution)/shard_map/gated_4/ppermute | solution.py:514
  50.5 2.2 multiply_bitcast_fusion.4
  54.5 59.2 %collective-permute-done.3.refs_4_ = f32[160,1024]{1,0:T(8,128)S(1)} collective-permute-done((f32[160,1024]{1,0:T(8,128)S(1)}, f32[160,1024]{1,0:T(8,128)S(1)}, u32[]{:S(2)}, u32[]{:S(2)}) %collective-permute-start.3) | collective-permute-done | bytes 655392 | tf_op jit(solution)/shard_map/gated_4/ppermute | solution.py:514
  116.0 2.2 collective-permute-start.7
  120.2 10.1 %collective-permute-done.6.refs_3_ = f32[128,1024]{1,0:T(8,128)S(1)} collective-permute-done((f32[128,1024]{1,0:T(8,128)}, f32[128,1024]{1,0:T(8,128)S(1)}, u32[]{:S(2)}, u32[]{:S(2)}) %collective-permute-start.6) | collective-permute-done | bytes 524320 | tf_op jit(solution)/shard_map/gated_3/ppermute | solution.py:514
  131.0 23.1 %collective-permute-start.10 = (f32[128,1024]{1,0:T(8,128)}, f32[128,1024]{1,0:T(8,128)}, u32[]{:S(2)}, u32[]{:S(2)}) collective-permute-start(f32[128,1024]{1,0:T(8,128)} %get-tuple-element.80), channel_id=1, source_target_pairs={{0,5},{1,4},{2,7},{3,6},{4,1},{5,0},{6,3},{7,2},{8,13},{9,12},{10,... | collective-permute-start | bytes 1572872 | tf_op jit(solution)/shard_map/grad_conv_5/ppermute | solution.py:514
  155.0 12.5 %collective-permute-start.12 = (f32[128,1024]{1,0:T(8,128)}, f32[128,1024]{1,0:T(8,128)}, u32[]{:S(2)}, u32[]{:S(2)}) collective-permute-start(f32[128,1024]{1,0:T(8,128)} %get-tuple-element.83), channel_id=1, source_target_pairs={{0,4},{1,5},{2,6},{3,7},{4,0},{5,1},{6,2},{7,3},{8,12},{9,13},{10,... | collective-permute-start | bytes 1572872 | tf_op jit(solution)/shard_map/grad_conv_4/ppermute | solution.py:514
  169.6 2.2 copy-done
  177.5 15.0 %filter_spectrum.1.filt = f32[2,528,1024]{2,1,0:T(8,128)S(1)} custom-call(s32[1]{0:T(128)} %bitcast.me, f32[8,4,32,1024]{3,2,1,0:T(8,128)S(1)} %bitcast.87, bf16[2,544,512]{2,1,0:T(8,128)(2,1)S(1)} %copy-done.11, bf16[2,512,512]{2,1,0:T(8,128)(2,1)S(1)} %copy-done.14, f32[2,528,1024]{2,1,0:T(8,128)S(1)} %copy-done, bf16[2,4,512,512]{3,2,1,0:T(8,128)(2,1)S(1)} %copy-done.2), custom_call_target="tpu_custom_call" | custom-call | flops 1048576 | bytes 1048576 | tf_op jit(solution)/shard_map/filter_spectrum/pallas_call | solution.py:418
  192.7 23.5 %conv_of.1 = (f32[2,528,1024]{2,1,0:T(8,128)S(1)}, f32[128,1024]{1,0:T(8,128)S(1)}, f32[128,1024]{1,0:T(8,128)}, f32[128,1024]{1,0:T(8,128)}, f32[128,1024]{1,0:...) custom-call(s32[1]{0:T(128)} %bitcast.me, ...), custom_call_target="tpu_custom_call" | custom-call | flops 1048576 | bytes 1048576 | tf_op jit(solution)/shard_map/conv_of/pallas_call | solution.py:418
  218.1 2.8 collective-permute-start.9
  221.0 30.4 %term_of.1 = (f32[2,528,1024]{2,1,0:T(8,128)S(1)}, f32[8,4,32,1024]{3,2,1,0:T(8,128)S(1)}) custom-call(s32[1]{0:T(128)} %bitcast.me, f32[2,528,1024]{2,1,0:T(8,128)S(1)} %get-tuple-element.98.gated, f32[128,1024]{1,0:T(8,128)S(1)} %copy-done.21, f32[128,1024]{1,0:T(8,128)S(1)} %collective-permute-done.16.refs_1_, ...), custom_call_target="tpu_custom_call" | custom-call | flops 1048576 | bytes 1048576 | tf_op jit(solution)/shard_map/term_of/pallas_call | solution.py:418
  256.3 8.9 %collective-permute-start.20 = (f32[128,1024]{1,0:T(8,128)}, f32[128,1024]{1,0:T(8,128)S(1)}, u32[]{:S(2)}, u32[]{:S(2)}) collective-permute-start(f32[128,1024]{1,0:T(8,128)} %get-tuple-element.97), channel_id=1, source_target_pairs={{0,4},{1,5},{2,6},{3,7},{4,0},{5,1},{6,2},{7,3},{8,12},{9,13},{10,... | collective-permute-start | bytes 1572872 | tf_op jit(solution)/shard_map/conv_4/ppermute | solution.py:514
  268.5 2.3 copy-done.1
  270.8 2.6 copy-done.4
  273.4 2.7 copy-done.6
  276.1 2.4 copy-done.18
  278.5 13.6 %grad_of.1 = (f32[128,1024]{1,0:T(8,128)S(1)}, f32[128,1024]{1,0:T(8,128)}, f32[128,1024]{1,0:T(8,128)S(1)}, f32[128,1024]{1,0:T(8,128)S(1)}, f32[128,1024]{1,0:...) custom-call(s32[1]{0:T(128)} %bitcast.me, f32[2,528,1024]{2,1,0:T(8,128)S(1)} %copy-done.6, ...), custom_call_target="tpu_custom_call" | custom-call | flops 1048576 | bytes 1048576 | tf_op jit(solution)/shard_map/grad_of/pallas_call | solution.py:418
  300.1 13.2 %reduce-scatter.2.cloned.1.call-done = f32[1,4,32,1024]{3,2,1,0:T(8,128)} async-done(((f32[8,4,32,1024]{3,2,1,0:T(8,128)}), f32[1,4,32,1024]{3,2,1,0:T(8,128)}) %reduce-scatter.2.cloned.1.call-update) | async-done | bytes 524304 | tf_op jit(solution)/shard_map/reduce_scatter | solution.py:658
  317.9 7.5 %collective-permute-done.21.refs_1_ = f32[128,1024]{1,0:T(8,128)S(1)} collective-permute-done((f32[128,1024]{1,0:T(8,128)}, f32[128,1024]{1,0:T(8,128)S(1)}, u32[]{:S(2)}, u32[]{:S(2)}) %collective-permute-start.21) | collective-permute-done | bytes 524320 | tf_op jit(solution)/shard_map/grad_gated_7/ppermute | solution.py:514
  326.3 15.5 %collective-permute-start.26 = (f32[128,1024]{1,0:T(8,128)}, f32[128,1024]{1,0:T(8,128)S(1)}, u32[]{:S(2)}, u32[]{:S(2)}) collective-permute-start(f32[128,1024]{1,0:T(8,128)} %copy-done.62), channel_id=1, source_target_pairs={{0,3},{1,2},{2,1},{3,0},{4,7},{5,6},{6,5},{7,4},{8,11},{9,10},{10,... | collective-permute-start | bytes 1572872 | tf_op jit(solution)/shard_map/grad_gated_3/ppermute | solution.py:514
  351.9 3.8 gate_out.3
  356.7 7.7 %collective-permute-done.26.refs_5_ = f32[128,1024]{1,0:T(8,128)S(1)} collective-permute-done((f32[128,1024]{1,0:T(8,128)}, f32[128,1024]{1,0:T(8,128)S(1)}, u32[]{:S(2)}, u32[]{:S(2)}) %collective-permute-start.26) | collective-permute-done | bytes 524320 | tf_op jit(solution)/shard_map/grad_gated_3/ppermute | solution.py:514
  365.5 3.7 collective-permute-done.25.refs_4_
  370.3 7.2 %collective-permute-done.24.refs_3_ = f32[128,1024]{1,0:T(8,128)S(1)} collective-permute-done((f32[128,1024]{1,0:T(8,128)}, f32[128,1024]{1,0:T(8,128)S(1)}, u32[]{:S(2)}, u32[]{:S(2)}) %collective-permute-start.24) | collective-permute-done | bytes 524320 | tf_op jit(solution)/shard_map/grad_gated_2/ppermute | solution.py:514
  378.6 10.8 %collective-permute-done.23.refs_2_ = f32[128,1024]{1,0:T(8,128)} collective-permute-done((f32[128,1024]{1,0:T(8,128)}, f32[128,1024]{1,0:T(8,128)}, u32[]{:S(2)}, u32[]{:S(2)}) %collective-permute-start.23) | collective-permute-done | bytes 524320 | tf_op jit(solution)/shard_map/grad_gated_6/ppermute | solution.py:514
  397.2 4.0 gate_out.4
  401.2 13.1 %collective-permute-done.22.refs_0_ = f32[128,1024]{1,0:T(8,128)} collective-permute-done((f32[128,1024]{1,0:T(8,128)}, f32[128,1024]{1,0:T(8,128)}, u32[]{:S(2)}, u32[]{:S(2)}) %collective-permute-start.22) | collective-permute-done | bytes 524320 | tf_op jit(solution)/shard_map/grad_gated_4/ppermute | solution.py:514
  (201 shorter events, 67.2 us)
Async XLA Ops:
  7.2 162.4 %all-gather.3.cloned.1.call-start = ((), (), s32[]{:S(2)}) async-start(), calls=%async_computation.2 | async-start | bytes 4718592 | tf_op jit(solution)/shard_map/all_gather | solution.py:645
  17.2 35.6 %collective-permute-start.1 = (f32[160,1024]{1,0:T(8,128)S(1)}, f32[160,1024]{1,0:T(8,128)S(1)}, u32[]{:S(2)}, u32[]{:S(2)}) collective-permute-start(f32[160,1024]{1,0:T(8,128)S(1)} %get-tuple-element.142), channel_id=1, source_target_pairs={{0,6},{1,7},{2,4},{3,5},{4,2},{5,3},{6,0},{7,1},{8,14},{9,15},{10,... | collective-permute-start | bytes 1966088 | tf_op jit(solution)/shard_map/gated_6/ppermute | solution.py:514
  17.3 36.4 %collective-permute-start.4 = (f32[160,1024]{1,0:T(8,128)S(1)}, f32[160,1024]{1,0:T(8,128)S(1)}, u32[]{:S(2)}, u32[]{:S(2)}) collective-permute-start(f32[160,1024]{1,0:T(8,128)S(1)} %get-tuple-element.140), channel_id=1, source_target_pairs={{0,2},{1,3},{2,0},{3,1},{4,6},{5,7},{6,4},{7,5},{8,10},{9,11},{10,... | collective-permute-start | bytes 1966088 | tf_op jit(solution)/shard_map/gated_2/ppermute | solution.py:514
  17.3 98.0 %collective-permute-start.2 = (f32[128,1024]{1,0:T(8,128)}, f32[128,1024]{1,0:T(8,128)S(1)}, u32[]{:S(2)}, u32[]{:S(2)}) collective-permute-start(f32[128,1024]{1,0:T(8,128)} %get-tuple-element.127), channel_id=1, source_target_pairs={{0,5},{1,4},{2,7},{3,6},{4,1},{5,0},{6,3},{7,2},{8,13},{9,12},{10,... | collective-permute-start | bytes 1572872 | tf_op jit(solution)/shard_map/gated_5/ppermute | solution.py:514
  24.9 88.8 %collective-permute-start.3 = (f32[160,1024]{1,0:T(8,128)S(1)}, f32[160,1024]{1,0:T(8,128)S(1)}, u32[]{:S(2)}, u32[]{:S(2)}) collective-permute-start(f32[160,1024]{1,0:T(8,128)S(1)} %get-tuple-element.65), channel_id=1, source_target_pairs={{0,4},{1,5},{2,6},{3,7},{4,0},{5,1},{6,2},{7,3},{8,12},{9,13},{10,... | collective-permute-start | bytes 1966088 | tf_op jit(solution)/shard_map/gated_4/ppermute | solution.py:514
  115.4 197.9 %reduce-scatter.2.cloned.1.call-start = ((), (), s32[]{:S(2)}) async-start(), calls=%async_computation.1 | async-start | bytes 4718592 | tf_op jit(solution)/shard_map/reduce_scatter | solution.py:658
  116.0 38.1 %collective-permute-start.7 = (f32[128,1024]{1,0:T(8,128)}, f32[128,1024]{1,0:T(8,128)S(1)}, u32[]{:S(2)}, u32[]{:S(2)}) collective-permute-start(f32[128,1024]{1,0:T(8,128)} %get-tuple-element.76), channel_id=1, source_target_pairs={{0,7},{1,6},{2,5},{3,4},{4,3},{5,2},{6,1},{7,0},{8,15},{9,14},{10,... | collective-permute-start | bytes 1572872 | tf_op jit(solution)/shard_map/grad_conv_7/ppermute | solution.py:514
  118.3 98.7 %collective-permute-start.8 = (f32[128,1024]{1,0:T(8,128)}, f32[128,1024]{1,0:T(8,128)}, u32[]{:S(2)}, u32[]{:S(2)}) collective-permute-start(f32[128,1024]{1,0:T(8,128)} %get-tuple-element.77), channel_id=1, source_target_pairs={{0,6},{1,7},{2,4},{3,5},{4,2},{5,3},{6,0},{7,1},{8,14},{9,15},{10,... | collective-permute-start | bytes 1572872 | tf_op jit(solution)/shard_map/grad_conv_6/ppermute | solution.py:514
  131.0 86.0 %collective-permute-start.10 = (f32[128,1024]{1,0:T(8,128)}, f32[128,1024]{1,0:T(8,128)}, u32[]{:S(2)}, u32[]{:S(2)}) collective-permute-start(f32[128,1024]{1,0:T(8,128)} %get-tuple-element.80), channel_id=1, source_target_pairs={{0,5},{1,4},{2,7},{3,6},{4,1},{5,0},{6,3},{7,2},{8,13},{9,12},{10,... | collective-permute-start | bytes 1572872 | tf_op jit(solution)/shard_map/grad_conv_5/ppermute | solution.py:514
  155.0 63.2 %collective-permute-start.12 = (f32[128,1024]{1,0:T(8,128)}, f32[128,1024]{1,0:T(8,128)}, u32[]{:S(2)}, u32[]{:S(2)}) collective-permute-start(f32[128,1024]{1,0:T(8,128)} %get-tuple-element.83), channel_id=1, source_target_pairs={{0,4},{1,5},{2,6},{3,7},{4,0},{5,1},{6,2},{7,3},{8,12},{9,13},{10,... | collective-permute-start | bytes 1572872 | tf_op jit(solution)/shard_map/grad_conv_4/ppermute | solution.py:514
  167.5 53.5 %collective-permute-start.14 = (f32[128,1024]{1,0:T(8,128)}, f32[128,1024]{1,0:T(8,128)}, u32[]{:S(2)}, u32[]{:S(2)}) collective-permute-start(f32[128,1024]{1,0:T(8,128)} %get-tuple-element.86), channel_id=1, source_target_pairs={{0,2},{1,3},{2,0},{3,1},{4,6},{5,7},{6,4},{7,5},{8,10},{9,11},{10,... | collective-permute-start | bytes 1572872 | tf_op jit(solution)/shard_map/grad_conv_2/ppermute | solution.py:514
  167.5 53.5 %collective-permute-start.15 = (f32[128,1024]{1,0:T(8,128)}, f32[128,1024]{1,0:T(8,128)}, u32[]{:S(2)}, u32[]{:S(2)}) collective-permute-start(f32[128,1024]{1,0:T(8,128)} %get-tuple-element.87), channel_id=1, source_target_pairs={{0,3},{1,2},{2,1},{3,0},{4,7},{5,6},{6,5},{7,4},{8,11},{9,10},{10,... | collective-permute-start | bytes 1572872 | tf_op jit(solution)/shard_map/grad_conv_3/ppermute | solution.py:514
  217.0 38.5 %collective-permute-start.11 = (f32[128,1024]{1,0:T(8,128)S(1)}, f32[128,1024]{1,0:T(8,128)S(1)}, u32[]{:S(2)}, u32[]{:S(2)}) collective-permute-start(f32[128,1024]{1,0:T(8,128)S(1)} %get-tuple-element.82), channel_id=1, source_target_pairs={{0,6},{1,7},{2,4},{3,5},{4,2},{5,3},{6,0},{7,1},{8,14},{9,15},{10,... | collective-permute-start | bytes 1572872 | tf_op jit(solution)/shard_map/conv_6/ppermute | solution.py:514
  218.1 37.4 %collective-permute-start.9 = (f32[128,1024]{1,0:T(8,128)S(1)}, f32[128,1024]{1,0:T(8,128)S(1)}, u32[]{:S(2)}, u32[]{:S(2)}) collective-permute-start(f32[128,1024]{1,0:T(8,128)S(1)} %get-tuple-element.79), channel_id=1, source_target_pairs={{0,7},{1,6},{2,5},{3,4},{4,3},{5,2},{6,1},{7,0},{8,15},{9,14},{10,... | collective-permute-start | bytes 1572872 | tf_op jit(solution)/shard_map/conv_7/ppermute | solution.py:514
  256.3 40.6 %collective-permute-start.20 = (f32[128,1024]{1,0:T(8,128)}, f32[128,1024]{1,0:T(8,128)S(1)}, u32[]{:S(2)}, u32[]{:S(2)}) collective-permute-start(f32[128,1024]{1,0:T(8,128)} %get-tuple-element.97), channel_id=1, source_target_pairs={{0,4},{1,5},{2,6},{3,7},{4,0},{5,1},{6,2},{7,3},{8,12},{9,13},{10,... | collective-permute-start | bytes 1572872 | tf_op jit(solution)/shard_map/conv_4/ppermute | solution.py:514
  265.3 33.8 %collective-permute-start.19 = (f32[128,1024]{1,0:T(8,128)}, f32[128,1024]{1,0:T(8,128)S(1)}, u32[]{:S(2)}, u32[]{:S(2)}) collective-permute-start(f32[128,1024]{1,0:T(8,128)} %get-tuple-element.95), channel_id=1, source_target_pairs={{0,1},{1,0},{2,3},{3,2},{4,5},{5,4},{6,7},{7,6},{8,9},{9,8},{10,11... | collective-permute-start | bytes 1572872 | tf_op jit(solution)/shard_map/conv_1/ppermute | solution.py:514
  265.6 48.7 %collective-permute-start.18 = (f32[128,1024]{1,0:T(8,128)}, f32[128,1024]{1,0:T(8,128)}, u32[]{:S(2)}, u32[]{:S(2)}) collective-permute-start(f32[128,1024]{1,0:T(8,128)} %get-tuple-element.93), channel_id=1, source_target_pairs={{0,3},{1,2},{2,1},{3,0},{4,7},{5,6},{6,5},{7,4},{8,11},{9,10},{10,... | collective-permute-start | bytes 1572872 | tf_op jit(solution)/shard_map/conv_3/ppermute | solution.py:514
  265.9 49.7 %collective-permute-start.13 = (f32[128,1024]{1,0:T(8,128)}, f32[128,1024]{1,0:T(8,128)}, u32[]{:S(2)}, u32[]{:S(2)}) collective-permute-start(f32[128,1024]{1,0:T(8,128)} %get-tuple-element.85), channel_id=1, source_target_pairs={{0,2},{1,3},{2,0},{3,1},{4,6},{5,7},{6,4},{7,5},{8,10},{9,11},{10,... | collective-permute-start | bytes 1572872 | tf_op jit(solution)/shard_map/conv_2/ppermute | solution.py:514
  267.1 48.5 %collective-permute-start.17 = (f32[128,1024]{1,0:T(8,128)}, f32[128,1024]{1,0:T(8,128)}, u32[]{:S(2)}, u32[]{:S(2)}) collective-permute-start(f32[128,1024]{1,0:T(8,128)} %get-tuple-element.91), channel_id=1, source_target_pairs={{0,5},{1,4},{2,7},{3,6},{4,1},{5,0},{6,3},{7,2},{8,13},{9,12},{10,... | collective-permute-start | bytes 1572872 | tf_op jit(solution)/shard_map/conv_5/ppermute | solution.py:514
  297.7 27.8 %collective-permute-start.21 = (f32[128,1024]{1,0:T(8,128)}, f32[128,1024]{1,0:T(8,128)S(1)}, u32[]{:S(2)}, u32[]{:S(2)}) collective-permute-start(f32[128,1024]{1,0:T(8,128)} %get-tuple-element.101), channel_id=1, source_target_pairs={{0,7},{1,6},{2,5},{3,4},{4,3},{5,2},{6,1},{7,0},{8,15},{9,14},{10,... | collective-permute-start | bytes 1572872 | tf_op jit(solution)/shard_map/grad_gated_7/ppermute | solution.py:514
  299.9 41.9 %collective-permute-start.27 = (f32[128,1024]{1,0:T(8,128)}, f32[128,1024]{1,0:T(8,128)S(1)}, u32[]{:S(2)}, u32[]{:S(2)}) collective-permute-start(f32[128,1024]{1,0:T(8,128)} %get-tuple-element.114), channel_id=1, source_target_pairs={{0,1},{1,0},{2,3},{3,2},{4,5},{5,4},{6,7},{7,6},{8,9},{9,8},{10,11... | collective-permute-start | bytes 1572872 | tf_op jit(solution)/shard_map/grad_gated_1/ppermute | solution.py:514
  314.3 28.9 %collective-permute-start.28 = (f32[32,1024]{1,0:T(8,128)S(1)}, f32[32,1024]{1,0:T(8,128)S(1)}, u32[]{:S(2)}, u32[]{:S(2)}) collective-permute-start(f32[32,1024]{1,0:T(8,128)S(1)} %get-tuple-element.137), channel_id=1, source_target_pairs={{0,2},{2,0},{4,6},{6,4},{1,3},{3,1},{5,7},{7,5},{8,10},{10,8},{12,... | collective-permute-start | bytes 393224 | tf_op jit(solution)/shard_map/rows_sum/ppermute | solution.py:514
  315.6 29.6 %collective-permute-start.29 = (f32[32,1024]{1,0:T(8,128)S(1)}, f32[32,1024]{1,0:T(8,128)S(1)}, u32[]{:S(2)}, u32[]{:S(2)}) collective-permute-start(f32[32,1024]{1,0:T(8,128)S(1)} %get-tuple-element.139), channel_id=1, source_target_pairs={{0,4},{2,6},{4,0},{6,2},{1,5},{3,7},{5,1},{7,3},{8,12},{10,14},{12... | collective-permute-start | bytes 393224 | tf_op jit(solution)/shard_map/rows_sum/ppermute | solution.py:514
  317.7 29.4 %collective-permute-start.30 = (f32[32,1024]{1,0:T(8,128)S(1)}, f32[32,1024]{1,0:T(8,128)S(1)}, u32[]{:S(2)}, u32[]{:S(2)}) collective-permute-start(f32[32,1024]{1,0:T(8,128)S(1)} %get-tuple-element.138), channel_id=1, source_target_pairs={{0,6},{2,4},{4,2},{6,0},{1,7},{3,5},{5,3},{7,1},{8,14},{10,12},{12... | collective-permute-start | bytes 393224 | tf_op jit(solution)/shard_map/rows_sum/ppermute | solution.py:514
  326.3 38.1 %collective-permute-start.26 = (f32[128,1024]{1,0:T(8,128)}, f32[128,1024]{1,0:T(8,128)S(1)}, u32[]{:S(2)}, u32[]{:S(2)}) collective-permute-start(f32[128,1024]{1,0:T(8,128)} %copy-done.62), channel_id=1, source_target_pairs={{0,3},{1,2},{2,1},{3,0},{4,7},{5,6},{6,5},{7,4},{8,11},{9,10},{10,... | collective-permute-start | bytes 1572872 | tf_op jit(solution)/shard_map/grad_gated_3/ppermute | solution.py:514
  342.6 26.6 %collective-permute-start.25 = (f32[128,1024]{1,0:T(8,128)}, f32[128,1024]{1,0:T(8,128)S(1)}, u32[]{:S(2)}, u32[]{:S(2)}) collective-permute-start(f32[128,1024]{1,0:T(8,128)} %copy-done.61), channel_id=1, source_target_pairs={{0,5},{1,4},{2,7},{3,6},{4,1},{5,0},{6,3},{7,2},{8,13},{9,12},{10,... | collective-permute-start | bytes 1572872 | tf_op jit(solution)/shard_map/grad_gated_5/ppermute | solution.py:514
  343.2 34.4 %collective-permute-start.24 = (f32[128,1024]{1,0:T(8,128)}, f32[128,1024]{1,0:T(8,128)S(1)}, u32[]{:S(2)}, u32[]{:S(2)}) collective-permute-start(f32[128,1024]{1,0:T(8,128)} %copy-done.60), channel_id=1, source_target_pairs={{0,2},{1,3},{2,0},{3,1},{4,6},{5,7},{6,4},{7,5},{8,10},{9,11},{10,... | collective-permute-start | bytes 1572872 | tf_op jit(solution)/shard_map/grad_gated_2/ppermute | solution.py:514
  345.1 44.2 %collective-permute-start.23 = (f32[128,1024]{1,0:T(8,128)}, f32[128,1024]{1,0:T(8,128)}, u32[]{:S(2)}, u32[]{:S(2)}) collective-permute-start(f32[128,1024]{1,0:T(8,128)} %copy-done.59), channel_id=1, source_target_pairs={{0,6},{1,7},{2,4},{3,5},{4,2},{5,3},{6,0},{7,1},{8,14},{9,15},{10,... | collective-permute-start | bytes 1572872 | tf_op jit(solution)/shard_map/grad_gated_6/ppermute | solution.py:514
  347.1 67.2 %collective-permute-start.22 = (f32[128,1024]{1,0:T(8,128)}, f32[128,1024]{1,0:T(8,128)}, u32[]{:S(2)}, u32[]{:S(2)}) collective-permute-start(f32[128,1024]{1,0:T(8,128)} %copy-done.58), channel_id=1, source_target_pairs={{0,4},{1,5},{2,6},{3,7},{4,0},{5,1},{6,2},{7,3},{8,12},{9,13},{10,... | collective-permute-start | bytes 1572872 | tf_op jit(solution)/shard_map/grad_gated_4/ppermute | solution.py:514
  365.2 51.0 %collective-permute-start.31 = (f32[32,1024]{1,0:T(8,128)S(1)}, f32[32,1024]{1,0:T(8,128)S(1)}, u32[]{:S(2)}, u32[]{:S(2)}) collective-permute-start(f32[32,1024]{1,0:T(8,128)S(1)} %fusion.4), channel_id=1, source_target_pairs={{0,8},{8,0},{16,24},{24,16},{1,9},{9,1},{17,25},{25,17},{2,10},{10... | collective-permute-start | bytes 393224 | tf_op jit(solution)/shard_map/parts_gather/ppermute | solution.py:514
  370.0 46.2 %collective-permute-start.32 = (f32[32,1024]{1,0:T(8,128)S(1)}, f32[32,1024]{1,0:T(8,128)S(1)}, u32[]{:S(2)}, u32[]{:S(2)}) collective-permute-start(f32[32,1024]{1,0:T(8,128)S(1)} %fusion.4), channel_id=1, source_target_pairs={{0,16},{8,24},{16,0},{24,8},{1,17},{9,25},{17,1},{25,9},{2,18},{10... | collective-permute-start | bytes 393224 | tf_op jit(solution)/shard_map/parts_gather/ppermute | solution.py:514
  378.3 37.9 %collective-permute-start.33 = (f32[32,1024]{1,0:T(8,128)S(1)}, f32[32,1024]{1,0:T(8,128)S(1)}, u32[]{:S(2)}, u32[]{:S(2)}) collective-permute-start(f32[32,1024]{1,0:T(8,128)S(1)} %fusion.4), channel_id=1, source_target_pairs={{0,24},{8,16},{16,8},{24,0},{1,25},{9,17},{17,9},{25,1},{2,26},{10... | collective-permute-start | bytes 393224 | tf_op jit(solution)/shard_map/parts_gather/ppermute | solution.py:514
  (71 other events, 843.8 us)
Sparse Core Ops, SparseCore 0:
  115.5 36.1 all-gather.2
  256.5 56.7 reduce-scatter.1

commit v2 on v1

--- a/solution.py
+++ b/solution.py
@@ -165,7 +165,6 @@
 
 
 VMEM_LIMIT = 18 * 1024 * 1024
-UNDER_WAY = 3
 ROW_PAD = 16
 LANE_PAD = 128
 
@@ -608,18 +607,18 @@
 
     crossed, neared = [], []
 
-    def exchange(blocks, what, order, extra=None):
+    def exchange(blocks, what, order, deep=3, near_wait=0):
         got = [blocks[0]] + [None] * (owners - 1)
         before, near_before = len(crossed), list(neared)
         neared.clear()
         for step in order:
             mine, waits = blocks[step], []
             if step in far:
-                waits = crossed[max(0, len(crossed) - UNDER_WAY - 1) : max(0, len(crossed) - UNDER_WAY + 1)]
+                waits = crossed[max(0, len(crossed) - deep - 1) : max(0, len(crossed) - deep + 1)]
                 if len(crossed) - before >= len(far) // 2:
                     waits = waits + near_before
             elif before:
-                waits = crossed[before - 1 : before]
+                waits = crossed[before - 1 + near_wait : before + near_wait]
             if waits:
                 mine = after(waits, mine)
             with jax.named_scope(f"{what}_{step}"):
@@ -641,18 +640,19 @@
     gated = exchange(gated, "gated", order)
     over_row = jnp.stack([own_part] + [gated[i * cols][block:] for i in range(1, rows)])
     grad_conv = [gated_block(grad_out, outer_gate, step) for step in range(owners)]
-    over_row = after([gated[step] for step in far] + grad_conv, over_row)
+    over_row = after(gated + grad_conv, over_row)
     over_all = [lax.all_gather(over_row, ("dp", "col"))]
     filt = filter_spectrum(plan, me, over_all, by_tile, parts * owners)
 
     spec, conv_out = conv_of(plan, me, filt, after(filt, gated), by_block)
-    grad_conv[near[-1]] = after(conv_out[0], grad_conv[near[-1]])
-    grad_conv = exchange(grad_conv, "grad_conv", order)
-    conv = exchange(conv_out, "conv", order)
+    for step in near[1:]:
+        grad_conv[step] = after(conv_out[0], grad_conv[step])
+    grad_conv = exchange(grad_conv, "grad_conv", order, 4)
+    conv = exchange(conv_out, "conv", order, 4)
     tile_shape = (parts * cols, rows, height, side)
     cot, term = term_of(plan, me, spec, grad_conv, by_block, tile_shape, by_tile)
     back_out = grad_of(plan, me, filt, cot, owners, by_block)
-    grad_gated = exchange(back_out, "grad_gated", order)
+    grad_gated = exchange(back_out, "grad_gated", order, 3, 2)
 
     term = after([conv[step] for step in far[:2]], term)
     term = lax.psum_scatter(term, ("dp", "col"), scatter_dimension=0, tiled=False)

time: 426 us -> 458 us (1.075)
  waiting for transfers between devices: 136 us -> 156 us
  starting transfers between devices: 117 us -> 128 us
    all_gather x1, waiting for transfers between devices: 0.01 us -> 29.7 us  [channel_shards(): over_all = [lax.all_gather(over_row, ('dp', 'col'))]]
    ppermute x34, starting transfers between devices: 117 us -> 128 us  [pairwise(): lax.ppermute(block, axis, [(i, i ^ step) for i in range(lax.axis_size(axi...]
    ppermute x34, waiting for transfers between devices: 122 us -> 116 us  [pairwise(): lax.ppermute(block, axis, [(i, i ^ step) for i in range(lax.axis_size(axi...]
    unnamed x134 -> x128, local copies, waits for them, and re-layouts: 51.6 us -> 50 us
  transfers between devices with their start and end apart: 36 -> 36, of which waited for: 10 -> 10; matrix products, arithmetic and copies ran while one was open for 3% -> 2% of each run, Pallas kernels for 22% -> 21%
where the time goes in v2:
time: 458 us; the launch traced here: 455 us
  waiting for transfers between devices  156 us (34%)
  starting transfers between devices  128 us (28%)
  Pallas kernels  93.5 us (20%)
  local copies, waits for them, and re-layouts  51.2 us (11%)
  between operations  14.6 us (3%)
  other arithmetic  11.9 us (3%)
    ppermute x34, starting transfers between devices, pairwise(): lax.ppermute(block, axis, [(i, i ^ step) for i in range(lax.axis_size(axi...  128 us
    ppermute x34, waiting for transfers between devices, pairwise(): lax.ppermute(block, axis, [(i, i ^ step) for i in range(lax.axis_size(axi...  116 us
    pallas_call x4, Pallas kernels, call_kernel(): pl.pallas_call(kernel, out_shape=out_shape, in_specs=in_specs, out_specs=...  84.2 us
    unnamed x128, local copies, waits for them, and re-layouts  50 us
    all_gather x1, waiting for transfers between devices, channel_shards(): over_all = [lax.all_gather(over_row, ('dp', 'col'))]  29.7 us
    reduce_scatter x1, waiting for transfers between devices, channel_shards(): lax.psum_scatter(term, ('dp', 'col'), scatter_dimension=0, tiled=False)  10.4 us
    pallas_call x3, Pallas kernels, gated_by(): pl.pallas_call(functools.partial(gate_kernel, steps, len(gates)), grid_sp...  9.33 us
  transfers between devices with their start and end apart: 36, of which 10 were waited for; matrix products, arithmetic and copies ran while one was open for 2% of the time, Pallas kernels for 21%

profile of v2, /device:TPU:7, one launch (start us, length us, event | category | flops | bytes accessed | tf_op | source)
XLA Modules:
  0.0 455.3 jit_solution(13114042867980136320)
XLA Ops:
  8.3 3.9 collective-permute-start.3
  13.2 3.8 multiply_bitcast_fusion.8
  20.3 4.6 %collective-permute-done.3.refs_7_ = f32[128,1024]{1,0:T(8,128)S(1)} collective-permute-done((f32[128,1024]{1,0:T(8,128)S(1)}, f32[128,1024]{1,0:T(8,128)S(1)}, u32[]{:S(2)}, u32[]{:S(2)}) %collective-permute-start.3) | collective-permute-done | bytes 524320 | tf_op jit(solution)/shard_map/gated_7/ppermute | solution.py:513
  24.9 25.6 %collective-permute-start.4 = (f32[160,1024]{1,0:T(8,128)S(1)}, f32[160,1024]{1,0:T(8,128)S(1)}, u32[]{:S(2)}, u32[]{:S(2)}) collective-permute-start(f32[160,1024]{1,0:T(8,128)S(1)} %get-tuple-element.66), channel_id=1, source_target_pairs={{0,4},{1,5},{2,6},{3,7},{4,0},{5,1},{6,2},{7,3},{8,12},{9,13},{10,... | collective-permute-start | bytes 1966088 | tf_op jit(solution)/shard_map/gated_4/ppermute | solution.py:513
  52.7 12.1 %collective-permute-start.5 = (f32[128,1024]{1,0:T(8,128)}, f32[128,1024]{1,0:T(8,128)S(1)}, u32[]{:S(2)}, u32[]{:S(2)}) collective-permute-start(f32[128,1024]{1,0:T(8,128)} %get-tuple-element.133), channel_id=1, source_target_pairs={{0,5},{1,4},{2,7},{3,6},{4,1},{5,0},{6,3},{7,2},{8,13},{9,12},{10,... | collective-permute-start | bytes 1572872 | tf_op jit(solution)/shard_map/gated_5/ppermute | solution.py:513
  66.5 35.9 %collective-permute-done.4.refs_4_ = f32[160,1024]{1,0:T(8,128)S(1)} collective-permute-done((f32[160,1024]{1,0:T(8,128)S(1)}, f32[160,1024]{1,0:T(8,128)S(1)}, u32[]{:S(2)}, u32[]{:S(2)}) %collective-permute-start.4) | collective-permute-done | bytes 655392 | tf_op jit(solution)/shard_map/gated_4/ppermute | solution.py:513
  104.1 9.5 %collective-permute-done.5.refs_5_ = f32[128,1024]{1,0:T(8,128)S(1)} collective-permute-done((f32[128,1024]{1,0:T(8,128)}, f32[128,1024]{1,0:T(8,128)S(1)}, u32[]{:S(2)}, u32[]{:S(2)}) %collective-permute-start.5) | collective-permute-done | bytes 524320 | tf_op jit(solution)/shard_map/gated_5/ppermute | solution.py:513
  114.5 2.7 collective-permute-start.7
  118.2 2.6 collective-permute-start.11
  121.1 29.7 %all-gather.3.cloned.1.call-done = f32[32,32,1024]{2,1,0:T(8,128)} async-done(((f32[4,32,1024]{2,1,0:T(8,128)}), f32[32,32,1024]{2,1,0:T(8,128)}) %all-gather.3.cloned.1.call-update) | async-done | bytes 4194320 | tf_op jit(solution)/shard_map/all_gather | solution.py:644
  158.7 15.0 %filter_spectrum.1.filt = f32[2,528,1024]{2,1,0:T(8,128)S(1)} custom-call(s32[1]{0:T(128)} %bitcast.me, f32[8,4,32,1024]{3,2,1,0:T(8,128)S(1)} %bitcast.87, bf16[2,544,512]{2,1,0:T(8,128)(2,1)S(1)} %copy-done.11, bf16[2,512,512]{2,1,0:T(8,128)(2,1)S(1)} %copy-done.14, f32[2,528,1024]{2,1,0:T(8,128)S(1)} %copy-done, bf16[2,4,512,512]{3,2,1,0:T(8,128)(2,1)S(1)} %copy-done.2), custom_call_target="tpu_custom_call" | custom-call | flops 1048576 | bytes 1048576 | tf_op jit(solution)/shard_map/filter_spectrum/pallas_call | solution.py:417
  173.9 25.2 %conv_of.1 = (f32[2,528,1024]{2,1,0:T(8,128)S(1)}, f32[128,1024]{1,0:T(8,128)S(1)}, f32[128,1024]{1,0:T(8,128)}, f32[128,1024]{1,0:T(8,128)}, f32[128,1024]{1,0:...) custom-call(s32[1]{0:T(128)} %bitcast.me, ...), custom_call_target="tpu_custom_call" | custom-call | flops 1048576 | bytes 1048576 | tf_op jit(solution)/shard_map/conv_of/pallas_call | solution.py:417
  203.6 3.3 collective-permute-done.11.refs_4_
  208.7 32.0 %collective-permute-done.15.refs_3_ = f32[128,1024]{1,0:T(8,128)S(1)} collective-permute-done((f32[128,1024]{1,0:T(8,128)S(1)}, f32[128,1024]{1,0:T(8,128)S(1)}, u32[]{:S(2)}, u32[]{:S(2)}) %collective-permute-start.15) | collective-permute-done | bytes 524320 | tf_op jit(solution)/shard_map/grad_conv_3/ppermute | solution.py:513
  240.7 30.4 %term_of.1 = (f32[2,528,1024]{2,1,0:T(8,128)S(1)}, f32[8,4,32,1024]{3,2,1,0:T(8,128)S(1)}) custom-call(s32[1]{0:T(128)} %bitcast.me, f32[2,528,1024]{2,1,0:T(8,128)S(1)} %get-tuple-element.100.gated, f32[128,1024]{1,0:T(8,128)S(1)} %copy-done.21, f32[128,1024]{1,0:T(8,128)S(1)} %collective-permute-done.16.refs_1_, ...), custom_call_target="tpu_custom_call" | custom-call | flops 1048576 | bytes 1048576 | tf_op jit(solution)/shard_map/term_of/pallas_call | solution.py:417
  278.1 2.5 collective-permute-start.20
  280.7 2.3 copy-done.1
  283.0 2.7 copy-done.4
  285.7 2.7 copy-done.6
  288.4 2.4 copy-done.18
  290.8 13.6 %grad_of.1 = (f32[128,1024]{1,0:T(8,128)S(1)}, f32[128,1024]{1,0:T(8,128)S(1)}, f32[128,1024]{1,0:T(8,128)S(1)}, f32[128,1024]{1,0:T(8,128)S(1)}, f32[128,1024]{...) custom-call(s32[1]{0:T(128)} %bitcast.me, f32[2,528,1024]{2,1,0:T(8,128)S(1)} %copy-done.6, ...), custom_call_target="tpu_custom_call" | custom-call | flops 1048576 | bytes 1048576 | tf_op jit(solution)/shard_map/grad_of/pallas_call | solution.py:417
  311.7 3.2 collective-permute-start.21
  314.9 10.4 %reduce-scatter.2.cloned.1.call-done = f32[1,4,32,1024]{3,2,1,0:T(8,128)} async-done(((f32[8,4,32,1024]{3,2,1,0:T(8,128)}), f32[1,4,32,1024]{3,2,1,0:T(8,128)}) %reduce-scatter.2.cloned.1.call-update) | async-done | bytes 524304 | tf_op jit(solution)/shard_map/reduce_scatter | solution.py:658
  327.6 20.0 %collective-permute-start.25 = (f32[128,1024]{1,0:T(8,128)}, f32[128,1024]{1,0:T(8,128)S(1)}, u32[]{:S(2)}, u32[]{:S(2)}) collective-permute-start(f32[128,1024]{1,0:T(8,128)} %copy-done.58), channel_id=1, source_target_pairs={{0,5},{1,4},{2,7},{3,6},{4,1},{5,0},{6,3},{7,2},{8,13},{9,12},{10,... | collective-permute-start | bytes 1572872 | tf_op jit(solution)/shard_map/grad_gated_5/ppermute | solution.py:513
  348.4 4.4 collective-permute-start.30
  353.6 33.8 %collective-permute-start.26 = (f32[128,1024]{1,0:T(8,128)}, f32[128,1024]{1,0:T(8,128)S(1)}, u32[]{:S(2)}, u32[]{:S(2)}) collective-permute-start(f32[128,1024]{1,0:T(8,128)} %copy-done.56), channel_id=1, source_target_pairs={{0,3},{1,2},{2,1},{3,0},{4,7},{5,6},{6,5},{7,4},{8,11},{9,10},{10,... | collective-permute-start | bytes 1572872 | tf_op jit(solution)/shard_map/grad_gated_3/ppermute | solution.py:513
  387.4 12.6 %collective-permute-done.29 = f32[32,1024]{1,0:T(8,128)S(1)} collective-permute-done((f32[32,1024]{1,0:T(8,128)S(1)}, f32[32,1024]{1,0:T(8,128)S(1)}, u32[]{:S(2)}, u32[]{:S(2)}) %collective-permute-start.29) | collective-permute-done | bytes 131104 | tf_op jit(solution)/shard_map/rows_sum/ppermute | solution.py:513
  400.0 3.5 collective-permute-start.22
  408.2 3.8 gate_out.3
  415.1 5.8 %collective-permute-done.26.refs_5_ = f32[128,1024]{1,0:T(8,128)S(1)} collective-permute-done((f32[128,1024]{1,0:T(8,128)}, f32[128,1024]{1,0:T(8,128)S(1)}, u32[]{:S(2)}, u32[]{:S(2)}) %collective-permute-start.26) | collective-permute-done | bytes 524320 | tf_op jit(solution)/shard_map/grad_gated_3/ppermute | solution.py:513
  421.9 12.0 %collective-permute-done.24.refs_3_ = f32[128,1024]{1,0:T(8,128)} collective-permute-done((f32[128,1024]{1,0:T(8,128)}, f32[128,1024]{1,0:T(8,128)}, u32[]{:S(2)}, u32[]{:S(2)}) %collective-permute-start.24) | collective-permute-done | bytes 524320 | tf_op jit(solution)/shard_map/grad_gated_2/ppermute | solution.py:513
  441.8 3.6 gate_out.4
  (195 shorter events, 65.0 us)
Async XLA Ops:
  7.2 143.6 %all-gather.3.cloned.1.call-start = ((), (), s32[]{:S(2)}) async-start(), calls=%async_computation.2 | async-start | bytes 4718592 | tf_op jit(solution)/shard_map/all_gather | solution.py:644
  17.2 35.5 %collective-permute-start.6 = (f32[160,1024]{1,0:T(8,128)S(1)}, f32[160,1024]{1,0:T(8,128)S(1)}, u32[]{:S(2)}, u32[]{:S(2)}) collective-permute-start(f32[160,1024]{1,0:T(8,128)S(1)} %get-tuple-element.142), channel_id=1, source_target_pairs={{0,6},{1,7},{2,4},{3,5},{4,2},{5,3},{6,0},{7,1},{8,14},{9,15},{10,... | collective-permute-start | bytes 1966088 | tf_op jit(solution)/shard_map/gated_6/ppermute | solution.py:513
  17.3 48.4 %collective-permute-start.1 = (f32[160,1024]{1,0:T(8,128)S(1)}, f32[160,1024]{1,0:T(8,128)S(1)}, u32[]{:S(2)}, u32[]{:S(2)}) collective-permute-start(f32[160,1024]{1,0:T(8,128)S(1)} %get-tuple-element.144), channel_id=1, source_target_pairs={{0,2},{1,3},{2,0},{3,1},{4,6},{5,7},{6,4},{7,5},{8,10},{9,11},{10,... | collective-permute-start | bytes 1966088 | tf_op jit(solution)/shard_map/gated_2/ppermute | solution.py:513
  17.3 86.8 %collective-permute-start = (f32[128,1024]{1,0:T(8,128)}, f32[128,1024]{1,0:T(8,128)S(1)}, u32[]{:S(2)}, u32[]{:S(2)}) collective-permute-start(f32[128,1024]{1,0:T(8,128)} %get-tuple-element.137), channel_id=1, source_target_pairs={{0,1},{1,0},{2,3},{3,2},{4,5},{5,4},{6,7},{7,6},{8,9},{9,8},{10,11... | collective-permute-start | bytes 1572872 | tf_op jit(solution)/shard_map/gated_1/ppermute | solution.py:513
  17.7 86.4 %collective-permute-start.2 = (f32[128,1024]{1,0:T(8,128)}, f32[128,1024]{1,0:T(8,128)}, u32[]{:S(2)}, u32[]{:S(2)}) collective-permute-start(f32[128,1024]{1,0:T(8,128)} %get-tuple-element.135), channel_id=1, source_target_pairs={{0,3},{1,2},{2,1},{3,0},{4,7},{5,6},{6,5},{7,4},{8,11},{9,10},{10,... | collective-permute-start | bytes 1572872 | tf_op jit(solution)/shard_map/gated_3/ppermute | solution.py:513
  24.9 77.6 %collective-permute-start.4 = (f32[160,1024]{1,0:T(8,128)S(1)}, f32[160,1024]{1,0:T(8,128)S(1)}, u32[]{:S(2)}, u32[]{:S(2)}) collective-permute-start(f32[160,1024]{1,0:T(8,128)S(1)} %get-tuple-element.66), channel_id=1, source_target_pairs={{0,4},{1,5},{2,6},{3,7},{4,0},{5,1},{6,2},{7,3},{8,12},{9,13},{10,... | collective-permute-start | bytes 1966088 | tf_op jit(solution)/shard_map/gated_4/ppermute | solution.py:513
  52.7 60.9 %collective-permute-start.5 = (f32[128,1024]{1,0:T(8,128)}, f32[128,1024]{1,0:T(8,128)S(1)}, u32[]{:S(2)}, u32[]{:S(2)}) collective-permute-start(f32[128,1024]{1,0:T(8,128)} %get-tuple-element.133), channel_id=1, source_target_pairs={{0,5},{1,4},{2,7},{3,6},{4,1},{5,0},{6,3},{7,2},{8,13},{9,12},{10,... | collective-permute-start | bytes 1572872 | tf_op jit(solution)/shard_map/gated_5/ppermute | solution.py:513
  114.5 210.8 %reduce-scatter.2.cloned.1.call-start = ((), (), s32[]{:S(2)}) async-start(), calls=%async_computation.1 | async-start | bytes 4718592 | tf_op jit(solution)/shard_map/reduce_scatter | solution.py:658
  114.5 85.4 %collective-permute-start.7 = (f32[128,1024]{1,0:T(8,128)}, f32[128,1024]{1,0:T(8,128)}, u32[]{:S(2)}, u32[]{:S(2)}) collective-permute-start(f32[128,1024]{1,0:T(8,128)} %get-tuple-element.77), channel_id=1, source_target_pairs={{0,7},{1,6},{2,5},{3,4},{4,3},{5,2},{6,1},{7,0},{8,15},{9,14},{10,... | collective-permute-start | bytes 1572872 | tf_op jit(solution)/shard_map/grad_conv_7/ppermute | solution.py:513
  117.2 82.9 %collective-permute-start.9 = (f32[128,1024]{1,0:T(8,128)}, f32[128,1024]{1,0:T(8,128)}, u32[]{:S(2)}, u32[]{:S(2)}) collective-permute-start(f32[128,1024]{1,0:T(8,128)} %get-tuple-element.80), channel_id=1, source_target_pairs={{0,6},{1,7},{2,4},{3,5},{4,2},{5,3},{6,0},{7,1},{8,14},{9,15},{10,... | collective-permute-start | bytes 1572872 | tf_op jit(solution)/shard_map/grad_conv_6/ppermute | solution.py:513
  118.2 83.3 %collective-permute-start.13 = (f32[128,1024]{1,0:T(8,128)}, f32[128,1024]{1,0:T(8,128)}, u32[]{:S(2)}, u32[]{:S(2)}) collective-permute-start(f32[128,1024]{1,0:T(8,128)} %get-tuple-element.86), channel_id=1, source_target_pairs={{0,5},{1,4},{2,7},{3,6},{4,1},{5,0},{6,3},{7,2},{8,13},{9,12},{10,... | collective-permute-start | bytes 1572872 | tf_op jit(solution)/shard_map/grad_conv_5/ppermute | solution.py:513
  118.2 88.7 %collective-permute-start.11 = (f32[128,1024]{1,0:T(8,128)}, f32[128,1024]{1,0:T(8,128)}, u32[]{:S(2)}, u32[]{:S(2)}) collective-permute-start(f32[128,1024]{1,0:T(8,128)} %get-tuple-element.83), channel_id=1, source_target_pairs={{0,4},{1,5},{2,6},{3,7},{4,0},{5,1},{6,2},{7,3},{8,12},{9,13},{10,... | collective-permute-start | bytes 1572872 | tf_op jit(solution)/shard_map/grad_conv_4/ppermute | solution.py:513
  120.8 87.9 %collective-permute-start.14 = (f32[128,1024]{1,0:T(8,128)}, f32[128,1024]{1,0:T(8,128)}, u32[]{:S(2)}, u32[]{:S(2)}) collective-permute-start(f32[128,1024]{1,0:T(8,128)} %get-tuple-element.87), channel_id=1, source_target_pairs={{0,2},{1,3},{2,0},{3,1},{4,6},{5,7},{6,4},{7,5},{8,10},{9,11},{10,... | collective-permute-start | bytes 1572872 | tf_op jit(solution)/shard_map/grad_conv_2/ppermute | solution.py:513
  200.2 40.6 %collective-permute-start.15 = (f32[128,1024]{1,0:T(8,128)S(1)}, f32[128,1024]{1,0:T(8,128)S(1)}, u32[]{:S(2)}, u32[]{:S(2)}) collective-permute-start(f32[128,1024]{1,0:T(8,128)S(1)} %copy-done.60), channel_id=1, source_target_pairs={{0,3},{1,2},{2,1},{3,0},{4,7},{5,6},{6,5},{7,4},{8,11},{9,10},{10,... | collective-permute-start | bytes 1572872 | tf_op jit(solution)/shard_map/grad_conv_3/ppermute | solution.py:513
  201.5 73.7 %collective-permute-start.10 = (f32[128,1024]{1,0:T(8,128)S(1)}, f32[128,1024]{1,0:T(8,128)S(1)}, u32[]{:S(2)}, u32[]{:S(2)}) collective-permute-start(f32[128,1024]{1,0:T(8,128)S(1)} %get-tuple-element.82), channel_id=1, source_target_pairs={{0,6},{1,7},{2,4},{3,5},{4,2},{5,3},{6,0},{7,1},{8,14},{9,15},{10,... | collective-permute-start | bytes 1572872 | tf_op jit(solution)/shard_map/conv_6/ppermute | solution.py:513
  206.9 68.3 %collective-permute-start.8 = (f32[128,1024]{1,0:T(8,128)S(1)}, f32[128,1024]{1,0:T(8,128)S(1)}, u32[]{:S(2)}, u32[]{:S(2)}) collective-permute-start(f32[128,1024]{1,0:T(8,128)S(1)} %get-tuple-element.79), channel_id=1, source_target_pairs={{0,7},{1,6},{2,5},{3,4},{4,3},{5,2},{6,1},{7,0},{8,15},{9,14},{10,... | collective-permute-start | bytes 1572872 | tf_op jit(solution)/shard_map/conv_7/ppermute | solution.py:513
  276.1 33.2 %collective-permute-start.17 = (f32[128,1024]{1,0:T(8,128)}, f32[128,1024]{1,0:T(8,128)S(1)}, u32[]{:S(2)}, u32[]{:S(2)}) collective-permute-start(f32[128,1024]{1,0:T(8,128)} %get-tuple-element.93), channel_id=1, source_target_pairs={{0,5},{1,4},{2,7},{3,6},{4,1},{5,0},{6,3},{7,2},{8,13},{9,12},{10,... | collective-permute-start | bytes 1572872 | tf_op jit(solution)/shard_map/conv_5/ppermute | solution.py:513
  276.2 34.8 %collective-permute-start.19 = (f32[128,1024]{1,0:T(8,128)}, f32[128,1024]{1,0:T(8,128)S(1)}, u32[]{:S(2)}, u32[]{:S(2)}) collective-permute-start(f32[128,1024]{1,0:T(8,128)} %get-tuple-element.97), channel_id=1, source_target_pairs={{0,1},{1,0},{2,3},{3,2},{4,5},{5,4},{6,7},{7,6},{8,9},{9,8},{10,11... | collective-permute-start | bytes 1572872 | tf_op jit(solution)/shard_map/conv_1/ppermute | solution.py:513
  276.6 49.7 %collective-permute-start.18 = (f32[128,1024]{1,0:T(8,128)}, f32[128,1024]{1,0:T(8,128)}, u32[]{:S(2)}, u32[]{:S(2)}) collective-permute-start(f32[128,1024]{1,0:T(8,128)} %get-tuple-element.95), channel_id=1, source_target_pairs={{0,3},{1,2},{2,1},{3,0},{4,7},{5,6},{6,5},{7,4},{8,11},{9,10},{10,... | collective-permute-start | bytes 1572872 | tf_op jit(solution)/shard_map/conv_3/ppermute | solution.py:513
  278.1 49.5 %collective-permute-start.12 = (f32[128,1024]{1,0:T(8,128)}, f32[128,1024]{1,0:T(8,128)}, u32[]{:S(2)}, u32[]{:S(2)}) collective-permute-start(f32[128,1024]{1,0:T(8,128)} %get-tuple-element.85), channel_id=1, source_target_pairs={{0,2},{1,3},{2,0},{3,1},{4,6},{5,7},{6,4},{7,5},{8,10},{9,11},{10,... | collective-permute-start | bytes 1572872 | tf_op jit(solution)/shard_map/conv_2/ppermute | solution.py:513
  278.1 49.5 %collective-permute-start.20 = (f32[128,1024]{1,0:T(8,128)}, f32[128,1024]{1,0:T(8,128)}, u32[]{:S(2)}, u32[]{:S(2)}) collective-permute-start(f32[128,1024]{1,0:T(8,128)} %get-tuple-element.99), channel_id=1, source_target_pairs={{0,4},{1,5},{2,6},{3,7},{4,0},{5,1},{6,2},{7,3},{8,12},{9,13},{10,... | collective-permute-start | bytes 1572872 | tf_op jit(solution)/shard_map/conv_4/ppermute | solution.py:513
  310.1 37.5 %collective-permute-start.23 = (f32[128,1024]{1,0:T(8,128)}, f32[128,1024]{1,0:T(8,128)S(1)}, u32[]{:S(2)}, u32[]{:S(2)}) collective-permute-start(f32[128,1024]{1,0:T(8,128)} %get-tuple-element.108), channel_id=1, source_target_pairs={{0,6},{1,7},{2,4},{3,5},{4,2},{5,3},{6,0},{7,1},{8,14},{9,15},{10,... | collective-permute-start | bytes 1572872 | tf_op jit(solution)/shard_map/grad_gated_6/ppermute | solution.py:513
  311.7 41.1 %collective-permute-start.21 = (f32[128,1024]{1,0:T(8,128)}, f32[128,1024]{1,0:T(8,128)S(1)}, u32[]{:S(2)}, u32[]{:S(2)}) collective-permute-start(f32[128,1024]{1,0:T(8,128)} %get-tuple-element.103), channel_id=1, source_target_pairs={{0,7},{1,6},{2,5},{3,4},{4,3},{5,2},{6,1},{7,0},{8,15},{9,14},{10,... | collective-permute-start | bytes 1572872 | tf_op jit(solution)/shard_map/grad_gated_7/ppermute | solution.py:513
  327.6 85.4 %collective-permute-start.25 = (f32[128,1024]{1,0:T(8,128)}, f32[128,1024]{1,0:T(8,128)S(1)}, u32[]{:S(2)}, u32[]{:S(2)}) collective-permute-start(f32[128,1024]{1,0:T(8,128)} %copy-done.58), channel_id=1, source_target_pairs={{0,5},{1,4},{2,7},{3,6},{4,1},{5,0},{6,3},{7,2},{8,13},{9,12},{10,... | collective-permute-start | bytes 1572872 | tf_op jit(solution)/shard_map/grad_gated_5/ppermute | solution.py:513
  347.6 52.4 %collective-permute-start.29 = (f32[32,1024]{1,0:T(8,128)S(1)}, f32[32,1024]{1,0:T(8,128)S(1)}, u32[]{:S(2)}, u32[]{:S(2)}) collective-permute-start(f32[32,1024]{1,0:T(8,128)S(1)} %get-tuple-element.141), channel_id=1, source_target_pairs={{0,4},{2,6},{4,0},{6,2},{1,5},{3,7},{5,1},{7,3},{8,12},{10,14},{12... | collective-permute-start | bytes 393224 | tf_op jit(solution)/shard_map/rows_sum/ppermute | solution.py:513
  348.4 51.6 %collective-permute-start.30 = (f32[32,1024]{1,0:T(8,128)S(1)}, f32[32,1024]{1,0:T(8,128)S(1)}, u32[]{:S(2)}, u32[]{:S(2)}) collective-permute-start(f32[32,1024]{1,0:T(8,128)S(1)} %get-tuple-element.140), channel_id=1, source_target_pairs={{0,6},{2,4},{4,2},{6,0},{1,7},{3,5},{5,3},{7,1},{8,14},{10,12},{12... | collective-permute-start | bytes 393224 | tf_op jit(solution)/shard_map/rows_sum/ppermute | solution.py:513
  353.6 60.4 %collective-permute-start.27 = (f32[128,1024]{1,0:T(8,128)}, f32[128,1024]{1,0:T(8,128)S(1)}, u32[]{:S(2)}, u32[]{:S(2)}) collective-permute-start(f32[128,1024]{1,0:T(8,128)} %copy-done.57), channel_id=1, source_target_pairs={{0,1},{1,0},{2,3},{3,2},{4,5},{5,4},{6,7},{7,6},{8,9},{9,8},{10,11... | collective-permute-start | bytes 1572872 | tf_op jit(solution)/shard_map/grad_gated_1/ppermute | solution.py:513
  353.6 67.2 %collective-permute-start.26 = (f32[128,1024]{1,0:T(8,128)}, f32[128,1024]{1,0:T(8,128)S(1)}, u32[]{:S(2)}, u32[]{:S(2)}) collective-permute-start(f32[128,1024]{1,0:T(8,128)} %copy-done.56), channel_id=1, source_target_pairs={{0,3},{1,2},{2,1},{3,0},{4,7},{5,6},{6,5},{7,4},{8,11},{9,10},{10,... | collective-permute-start | bytes 1572872 | tf_op jit(solution)/shard_map/grad_gated_3/ppermute | solution.py:513
  400.0 33.9 %collective-permute-start.24 = (f32[128,1024]{1,0:T(8,128)}, f32[128,1024]{1,0:T(8,128)}, u32[]{:S(2)}, u32[]{:S(2)}) collective-permute-start(f32[128,1024]{1,0:T(8,128)} %copy-done.55), channel_id=1, source_target_pairs={{0,2},{1,3},{2,0},{3,1},{4,6},{5,7},{6,4},{7,5},{8,10},{9,11},{10,... | collective-permute-start | bytes 1572872 | tf_op jit(solution)/shard_map/grad_gated_2/ppermute | solution.py:513
  400.0 45.4 %collective-permute-start.22 = (f32[128,1024]{1,0:T(8,128)}, f32[128,1024]{1,0:T(8,128)}, u32[]{:S(2)}, u32[]{:S(2)}) collective-permute-start(f32[128,1024]{1,0:T(8,128)} %copy-done.54), channel_id=1, source_target_pairs={{0,4},{1,5},{2,6},{3,7},{4,0},{5,1},{6,2},{7,3},{8,12},{9,13},{10,... | collective-permute-start | bytes 1572872 | tf_op jit(solution)/shard_map/grad_gated_4/ppermute | solution.py:513
  413.8 33.5 %collective-permute-start.31 = (f32[32,1024]{1,0:T(8,128)S(1)}, f32[32,1024]{1,0:T(8,128)S(1)}, u32[]{:S(2)}, u32[]{:S(2)}) collective-permute-start(f32[32,1024]{1,0:T(8,128)S(1)} %fusion.4), channel_id=1, source_target_pairs={{0,8},{8,0},{16,24},{24,16},{1,9},{9,1},{17,25},{25,17},{2,10},{10... | collective-permute-start | bytes 393224 | tf_op jit(solution)/shard_map/parts_gather/ppermute | solution.py:513
  414.8 32.5 %collective-permute-start.32 = (f32[32,1024]{1,0:T(8,128)S(1)}, f32[32,1024]{1,0:T(8,128)S(1)}, u32[]{:S(2)}, u32[]{:S(2)}) collective-permute-start(f32[32,1024]{1,0:T(8,128)S(1)} %fusion.4), channel_id=1, source_target_pairs={{0,16},{8,24},{16,0},{24,8},{1,17},{9,25},{17,1},{25,9},{2,18},{10... | collective-permute-start | bytes 393224 | tf_op jit(solution)/shard_map/parts_gather/ppermute | solution.py:513
  (68 other events, 873.4 us)
Sparse Core Ops, SparseCore 0:
  114.6 36.1 all-gather.2
  276.2 49.0 reduce-scatter.1

commit v3 on v2

--- a/solution.py
+++ b/solution.py
@@ -236,7 +236,7 @@
         yield blocks[step].at[pl.ds(0, size)], values.at[pl.ds(at, size)]
 
 
-def tile_views(plan, grid, me, tiles, values):
+def tile_views(plan, grid, natural, me, tiles, values):
     parts, rows, cols = grid
     block = plan.side // (rows * cols)
     height = block // parts
@@ -244,8 +244,10 @@
     for part in range(parts):
         for col in range(cols):
             for i in range(rows):
-                at = ((own_row ^ i) * cols + col) * block + part * height
-                yield tiles[0].at[part * cols + col, i], values.at[pl.ds(pl.multiple_of(at, height), height)]
+                row = i if natural else own_row ^ i
+                at = (row * cols + col) * block + part * height
+                at = at if natural else pl.multiple_of(at, height)
+                yield tiles[0].at[part * cols + col, i], values.at[pl.ds(at, height)]
 
 
 def start_all(pairs, sems):
@@ -596,8 +598,10 @@
     for i in range(2, len(far)):
         order = order + near[i - 2 : i - 1] + far[i : i + 1]
     order = order[:-1] + near[len(far) - 2 :] + order[-1:]
+    last_order = far + near[:1] + near[2:] + near[1:2]
     by_block = functools.partial(block_views, plan, owners)
-    by_tile = functools.partial(tile_views, plan, (parts, rows, cols))
+    by_tile = functools.partial(tile_views, plan, (parts, rows, cols), False)
+    by_row = functools.partial(tile_views, plan, (parts, rows, cols), True)
 
     def gated_block(left, right, step):
         at = place ^ step
@@ -644,22 +648,21 @@
     over_all = [lax.all_gather(over_row, ("dp", "col"))]
     filt = filter_spectrum(plan, me, over_all, by_tile, parts * owners)
 
-    spec, conv_out = conv_of(plan, me, filt, after(filt, gated), by_block)
-    for step in near[1:]:
-        grad_conv[step] = after(conv_out[0], grad_conv[step])
-    grad_conv = exchange(grad_conv, "grad_conv", order, 4)
+    got = exchange(grad_conv, "grad_conv", [step for step in order if step != near[-1]], 4)
+    spec, conv_out = conv_of(plan, me, filt, after([filt] + [got[step] for step in far[:1]], gated), by_block)
+    with jax.named_scope(f"grad_conv_{near[-1]}"):
+        got[near[-1]] = pairwise(after(conv_out[0], grad_conv[near[-1]]), ("row", "col"), near[-1])
+    grad_conv = got
     conv = exchange(conv_out, "conv", order, 4)
     tile_shape = (parts * cols, rows, height, side)
-    cot, term = term_of(plan, me, spec, grad_conv, by_block, tile_shape, by_tile)
+    cot, term = term_of(plan, me, spec, grad_conv, by_block, tile_shape, by_row)
     back_out = grad_of(plan, me, filt, cot, owners, by_block)
-    grad_gated = exchange(back_out, "grad_gated", order, 3, 2)
+    grad_gated = exchange(back_out, "grad_gated", last_order, 2, 3)
 
     term = after([conv[step] for step in far[:2]], term)
     term = lax.psum_scatter(term, ("dp", "col"), scatter_dimension=0, tiled=False)
-    with jax.named_scope("rows_sum"):
-        arrived = [pairwise(term[i], "row", i) for i in range(1, rows)]
-    total = sum(arrived, term[0]) * (1.0 / side)
-    every = [0] + order
+    total = lax.psum_scatter(term, "row", scatter_dimension=0, tiled=False) * (1.0 / side)
+    every = [0] + last_order
     (grad_outer,) = gated_by(me, every, [conv[step] for step in every], [grad_out[0]])
     total = after(grad_outer, total)
     with jax.named_scope("parts_gather"):

time: 458 us -> 444 us (0.969); the launches traced: 455 us -> 437 us
  starting transfers between devices: 128 us -> 110 us
  waiting for transfers between devices: 156 us -> 163 us
  local copies, waits for them, and re-layouts: 51.2 us -> 45.4 us
    ppermute x34 -> x31, starting transfers between devices: 128 us -> 110 us  [pairwise(): lax.ppermute(block, axis, [(i, i ^ step) for i in range(lax.axis_size(axi...]
    unnamed x128 -> x118, local copies, waits for them, and re-layouts: 50 us -> 45.2 us
    ppermute x34 -> x31, waiting for transfers between devices: 116 us -> 119 us  [pairwise(): lax.ppermute(block, axis, [(i, i ^ step) for i in range(lax.axis_size(axi...]
  transfers between devices with their start and end apart: 36 -> 34, of which waited for: 10 -> 9; matrix products, arithmetic and copies ran while one was open for 2% -> 2% of each run, Pallas kernels for 21% -> 21%
where the time goes in v3:
time: 444 us; the launch traced here: 437 us
  waiting for transfers between devices  163 us (37%)
  starting transfers between devices  110 us (25%)
  Pallas kernels  92.1 us (21%)
  local copies, waits for them, and re-layouts  45.4 us (10%)
  between operations  14.3 us (3%)
  other arithmetic  11.8 us (3%)
    ppermute x31, waiting for transfers between devices, pairwise(): lax.ppermute(block, axis, [(i, i ^ step) for i in range(lax.axis_size(axi...  119 us
    ppermute x31, starting transfers between devices, pairwise(): lax.ppermute(block, axis, [(i, i ^ step) for i in range(lax.axis_size(axi...  110 us
    pallas_call x4, Pallas kernels, call_kernel(): pl.pallas_call(kernel, out_shape=out_shape, in_specs=in_specs, out_specs=...  83.3 us
    unnamed x118, local copies, waits for them, and re-layouts  45.2 us
    all_gather x1, waiting for transfers between devices, channel_shards(): over_all = [lax.all_gather(over_row, ('dp', 'col'))]  29.7 us
    reduce_scatter x1, waiting for transfers between devices, channel_shards(): lax.psum_scatter(term, ('dp', 'col'), scatter_dimension=0, tiled=False)  13.9 us
  transfers between devices with their start and end apart: 34, of which 9 were waited for; matrix products, arithmetic and copies ran while one was open for 2% of the time, Pallas kernels for 21%

profile of v3, /device:TPU:7, one launch (start us, length us, event | category | flops | bytes accessed | tf_op | source)
XLA Modules:
  0.0 436.6 jit_solution(10264070424629059910)
XLA Ops:
  8.3 3.9 collective-permute-start.3
  13.2 3.8 multiply_bitcast_fusion.8
  17.3 3.8 collective-permute-start.5
  22.0 2.9 collective-permute-done.3.refs_7_
  24.9 25.6 %collective-permute-start.4 = (f32[160,1024]{1,0:T(8,128)S(1)}, f32[160,1024]{1,0:T(8,128)S(1)}, u32[]{:S(2)}, u32[]{:S(2)}) collective-permute-start(f32[160,1024]{1,0:T(8,128)S(1)} %get-tuple-element.64), channel_id=1, source_target_pairs={{0,4},{1,5},{2,6},{3,7},{4,0},{5,1},{6,2},{7,3},{8,12},{9,13},{10,... | collective-permute-start | bytes 1966088 | tf_op jit(solution)/shard_map/gated_4/ppermute | solution.py:515
  50.5 2.2 multiply_bitcast_fusion
  55.1 58.5 %collective-permute-done.4.refs_4_ = f32[160,1024]{1,0:T(8,128)S(1)} collective-permute-done((f32[160,1024]{1,0:T(8,128)S(1)}, f32[160,1024]{1,0:T(8,128)S(1)}, u32[]{:S(2)}, u32[]{:S(2)}) %collective-permute-start.4) | collective-permute-done | bytes 655392 | tf_op jit(solution)/shard_map/gated_4/ppermute | solution.py:515
  116.3 2.7 collective-permute-start.7
  120.1 2.7 collective-permute-start.12
  122.9 29.7 %all-gather.3.cloned.1.call-done = f32[32,32,1024]{2,1,0:T(8,128)} async-done(((f32[4,32,1024]{2,1,0:T(8,128)}), f32[32,32,1024]{2,1,0:T(8,128)}) %all-gather.3.cloned.1.call-update) | async-done | bytes 4194320 | tf_op jit(solution)/shard_map/all_gather | solution.py:648
  152.6 2.2 copy-done
  154.8 2.2 copy-done.2
  160.5 15.0 %filter_spectrum.1.filt = f32[2,528,1024]{2,1,0:T(8,128)S(1)} custom-call(s32[1]{0:T(128)} %bitcast.me, f32[8,4,32,1024]{3,2,1,0:T(8,128)S(1)} %bitcast.74, bf16[2,544,512]{2,1,0:T(8,128)(2,1)S(1)} %copy-done.11, bf16[2,512,512]{2,1,0:T(8,128)(2,1)S(1)} %copy-done.14, f32[2,528,1024]{2,1,0:T(8,128)S(1)} %copy-done, bf16[2,4,512,512]{3,2,1,0:T(8,128)(2,1)S(1)} %copy-done.2), custom_call_target="tpu_custom_call" | custom-call | flops 1048576 | bytes 1048576 | tf_op jit(solution)/shard_map/filter_spectrum/pallas_call | solution.py:419
  175.5 2.2 collective-permute-start.15
  177.8 24.5 %conv_of.1 = (f32[2,528,1024]{2,1,0:T(8,128)S(1)}, f32[128,1024]{1,0:T(8,128)S(1)}, f32[128,1024]{1,0:T(8,128)}, f32[128,1024]{1,0:T(8,128)}, f32[128,1024]{1,0:...) custom-call(s32[1]{0:T(128)} %bitcast.me, ...), custom_call_target="tpu_custom_call" | custom-call | flops 1048576 | bytes 1048576 | tf_op jit(solution)/shard_map/conv_of/pallas_call | solution.py:419
  207.2 23.7 %collective-permute-done.15.refs_4_ = f32[128,1024]{1,0:T(8,128)S(1)} collective-permute-done((f32[128,1024]{1,0:T(8,128)S(1)}, f32[128,1024]{1,0:T(8,128)S(1)}, u32[]{:S(2)}, u32[]{:S(2)}) %collective-permute-start.15) | collective-permute-done | bytes 524320 | tf_op jit(solution)/shard_map/grad_conv_4/ppermute | solution.py:515
  230.9 30.4 %term_of.1 = (f32[2,528,1024]{2,1,0:T(8,128)S(1)}, f32[8,4,32,1024]{3,2,1,0:T(8,128)S(1)}) custom-call(s32[1]{0:T(128)} %bitcast.me, f32[2,528,1024]{2,1,0:T(8,128)S(1)} %get-tuple-element.95.gated, f32[128,1024]{1,0:T(8,128)S(1)} %copy-done.21, f32[128,1024]{1,0:T(8,128)S(1)} %collective-permute-done.20.refs_1_, ...), custom_call_target="tpu_custom_call" | custom-call | flops 1048576 | bytes 1048576 | tf_op jit(solution)/shard_map/term_of/pallas_call | solution.py:419
  268.7 2.7 collective-permute-start.16
  271.4 2.5 copy-done.1
  273.9 2.6 copy-done.4
  276.5 2.6 copy-done.6
  279.2 2.3 copy-done.18
  281.5 13.4 %grad_of.1 = (f32[128,1024]{1,0:T(8,128)S(1)}, f32[128,1024]{1,0:T(8,128)S(1)}, f32[128,1024]{1,0:T(8,128)S(1)}, f32[128,1024]{1,0:T(8,128)S(1)}, f32[128,1024]{...) custom-call(s32[1]{0:T(128)} %bitcast.me, f32[2,528,1024]{2,1,0:T(8,128)S(1)} %copy-done.6, ...), custom_call_target="tpu_custom_call" | custom-call | flops 1048576 | bytes 1048576 | tf_op jit(solution)/shard_map/grad_of/pallas_call | solution.py:419
  301.3 13.9 %reduce-scatter.3.cloned.1.call-done = f32[1,4,32,1024]{3,2,1,0:T(8,128)} async-done(((f32[8,4,32,1024]{3,2,1,0:T(8,128)}), f32[1,4,32,1024]{3,2,1,0:T(8,128)}) %reduce-scatter.3.cloned.1.call-update) | async-done | bytes 524304 | tf_op jit(solution)/shard_map/reduce_scatter | solution.py:663
  315.2 3.1 collective-permute-start.24
  318.4 25.3 %collective-permute-done.17.refs_5_ = f32[128,1024]{1,0:T(8,128)} collective-permute-done((f32[128,1024]{1,0:T(8,128)}, f32[128,1024]{1,0:T(8,128)}, u32[]{:S(2)}, u32[]{:S(2)}) %collective-permute-start.17) | collective-permute-done | bytes 524320 | tf_op jit(solution)/shard_map/conv_2/ppermute | solution.py:515
  344.5 13.9 %collective-permute-start.22 = (f32[128,1024]{1,0:T(8,128)}, f32[128,1024]{1,0:T(8,128)S(1)}, u32[]{:S(2)}, u32[]{:S(2)}) collective-permute-start(f32[128,1024]{1,0:T(8,128)} %copy-done.52), channel_id=1, source_target_pairs={{0,5},{1,4},{2,7},{3,6},{4,1},{5,0},{6,3},{7,2},{8,13},{9,12},{10,... | collective-permute-start | bytes 1572872 | tf_op jit(solution)/shard_map/grad_gated_5/ppermute | solution.py:515
  359.1 21.4 %collective-permute-start.25 = (f32[128,1024]{1,0:T(8,128)}, f32[128,1024]{1,0:T(8,128)}, u32[]{:S(2)}, u32[]{:S(2)}) collective-permute-start(f32[128,1024]{1,0:T(8,128)} %copy-done.51), channel_id=1, source_target_pairs={{0,4},{1,5},{2,6},{3,7},{4,0},{5,1},{6,2},{7,3},{8,12},{9,13},{10,... | collective-permute-start | bytes 1572872 | tf_op jit(solution)/shard_map/grad_gated_4/ppermute | solution.py:515
  382.5 18.7 %collective-permute-start.26 = (f32[128,1024]{1,0:T(8,128)}, f32[128,1024]{1,0:T(8,128)}, u32[]{:S(2)}, u32[]{:S(2)}) collective-permute-start(f32[128,1024]{1,0:T(8,128)} %copy-done.50), channel_id=1, source_target_pairs={{0,2},{1,3},{2,0},{3,1},{4,6},{5,7},{6,4},{7,5},{8,10},{9,11},{10,... | collective-permute-start | bytes 1572872 | tf_op jit(solution)/shard_map/grad_gated_2/ppermute | solution.py:515
  405.6 3.4 gate_out.3
  410.1 5.7 %collective-permute-done.26.refs_5_ = f32[128,1024]{1,0:T(8,128)} collective-permute-done((f32[128,1024]{1,0:T(8,128)}, f32[128,1024]{1,0:T(8,128)}, u32[]{:S(2)}, u32[]{:S(2)}) %collective-permute-start.26) | collective-permute-done | bytes 524320 | tf_op jit(solution)/shard_map/grad_gated_2/ppermute | solution.py:515
  421.5 3.6 gate_out.4
  (181 shorter events, 51.2 us)
Async XLA Ops:
  7.2 145.4 %all-gather.3.cloned.1.call-start = ((), (), s32[]{:S(2)}) async-start(), calls=%async_computation.4 | async-start | bytes 4718592 | tf_op jit(solution)/shard_map/all_gather | solution.py:648
  8.3 16.5 %collective-permute-start.3 = (f32[128,1024]{1,0:T(8,128)S(1)}, f32[128,1024]{1,0:T(8,128)S(1)}, u32[]{:S(2)}, u32[]{:S(2)}) collective-permute-start(f32[128,1024]{1,0:T(8,128)S(1)} %multiply_bitcast_fusion.15), channel_id=1, source_target_pairs={{0,7},{1,6},{2,5},{3,4},{4,3},{5,2},{6,1},{7,0},{8,15},{9,14},{10,... | collective-permute-start | bytes 1572872 | tf_op jit(solution)/shard_map/gated_7/ppermute | solution.py:515
  17.2 35.6 %collective-permute-start.6 = (f32[160,1024]{1,0:T(8,128)S(1)}, f32[160,1024]{1,0:T(8,128)S(1)}, u32[]{:S(2)}, u32[]{:S(2)}) collective-permute-start(f32[160,1024]{1,0:T(8,128)S(1)} %get-tuple-element.135), channel_id=1, source_target_pairs={{0,6},{1,7},{2,4},{3,5},{4,2},{5,3},{6,0},{7,1},{8,14},{9,15},{10,... | collective-permute-start | bytes 1966088 | tf_op jit(solution)/shard_map/gated_6/ppermute | solution.py:515
  17.2 37.1 %collective-permute-start.1 = (f32[160,1024]{1,0:T(8,128)S(1)}, f32[160,1024]{1,0:T(8,128)S(1)}, u32[]{:S(2)}, u32[]{:S(2)}) collective-permute-start(f32[160,1024]{1,0:T(8,128)S(1)} %get-tuple-element.137), channel_id=1, source_target_pairs={{0,2},{1,3},{2,0},{3,1},{4,6},{5,7},{6,4},{7,5},{8,10},{9,11},{10,... | collective-permute-start | bytes 1966088 | tf_op jit(solution)/shard_map/gated_2/ppermute | solution.py:515
  17.3 98.1 %collective-permute-start.5 = (f32[128,1024]{1,0:T(8,128)}, f32[128,1024]{1,0:T(8,128)S(1)}, u32[]{:S(2)}, u32[]{:S(2)}) collective-permute-start(f32[128,1024]{1,0:T(8,128)} %get-tuple-element.129), channel_id=1, source_target_pairs={{0,5},{1,4},{2,7},{3,6},{4,1},{5,0},{6,3},{7,2},{8,13},{9,12},{10,... | collective-permute-start | bytes 1572872 | tf_op jit(solution)/shard_map/gated_5/ppermute | solution.py:515
  21.1 94.3 %collective-permute-start.2 = (f32[128,1024]{1,0:T(8,128)}, f32[128,1024]{1,0:T(8,128)}, u32[]{:S(2)}, u32[]{:S(2)}) collective-permute-start(f32[128,1024]{1,0:T(8,128)} %get-tuple-element.131), channel_id=1, source_target_pairs={{0,3},{1,2},{2,1},{3,0},{4,7},{5,6},{6,5},{7,4},{8,11},{9,10},{10,... | collective-permute-start | bytes 1572872 | tf_op jit(solution)/shard_map/gated_3/ppermute | solution.py:515
  24.9 88.8 %collective-permute-start.4 = (f32[160,1024]{1,0:T(8,128)S(1)}, f32[160,1024]{1,0:T(8,128)S(1)}, u32[]{:S(2)}, u32[]{:S(2)}) collective-permute-start(f32[160,1024]{1,0:T(8,128)S(1)} %get-tuple-element.64), channel_id=1, source_target_pairs={{0,4},{1,5},{2,6},{3,7},{4,0},{5,1},{6,2},{7,3},{8,12},{9,13},{10,... | collective-permute-start | bytes 1966088 | tf_op jit(solution)/shard_map/gated_4/ppermute | solution.py:515
  52.7 62.6 %collective-permute-start = (f32[128,1024]{1,0:T(8,128)}, f32[128,1024]{1,0:T(8,128)S(1)}, u32[]{:S(2)}, u32[]{:S(2)}) collective-permute-start(f32[128,1024]{1,0:T(8,128)} %get-tuple-element.133), channel_id=1, source_target_pairs={{0,1},{1,0},{2,3},{3,2},{4,5},{5,4},{6,7},{7,6},{8,9},{9,8},{10,11... | collective-permute-start | bytes 1572872 | tf_op jit(solution)/shard_map/gated_1/ppermute | solution.py:515
  116.3 198.9 %reduce-scatter.3.cloned.1.call-start = ((), (), s32[]{:S(2)}) async-start(), calls=%async_computation.2 | async-start | bytes 4718592 | tf_op jit(solution)/shard_map/reduce_scatter | solution.py:663
  116.3 59.2 %collective-permute-start.7 = (f32[128,1024]{1,0:T(8,128)}, f32[128,1024]{1,0:T(8,128)}, u32[]{:S(2)}, u32[]{:S(2)}) collective-permute-start(f32[128,1024]{1,0:T(8,128)} %get-tuple-element.66), channel_id=1, source_target_pairs={{0,7},{1,6},{2,5},{3,4},{4,3},{5,2},{6,1},{7,0},{8,15},{9,14},{10,... | collective-permute-start | bytes 1572872 | tf_op jit(solution)/shard_map/grad_conv_7/ppermute | solution.py:515
  119.0 84.2 %collective-permute-start.9 = (f32[128,1024]{1,0:T(8,128)}, f32[128,1024]{1,0:T(8,128)}, u32[]{:S(2)}, u32[]{:S(2)}) collective-permute-start(f32[128,1024]{1,0:T(8,128)} %get-tuple-element.78), channel_id=1, source_target_pairs={{0,6},{1,7},{2,4},{3,5},{4,2},{5,3},{6,0},{7,1},{8,14},{9,15},{10,... | collective-permute-start | bytes 1572872 | tf_op jit(solution)/shard_map/grad_conv_6/ppermute | solution.py:515
  120.1 83.7 %collective-permute-start.11 = (f32[128,1024]{1,0:T(8,128)}, f32[128,1024]{1,0:T(8,128)}, u32[]{:S(2)}, u32[]{:S(2)}) collective-permute-start(f32[128,1024]{1,0:T(8,128)} %get-tuple-element.81), channel_id=1, source_target_pairs={{0,5},{1,4},{2,7},{3,6},{4,1},{5,0},{6,3},{7,2},{8,13},{9,12},{10,... | collective-permute-start | bytes 1572872 | tf_op jit(solution)/shard_map/grad_conv_5/ppermute | solution.py:515
  120.1 85.5 %collective-permute-start.12 = (f32[128,1024]{1,0:T(8,128)}, f32[128,1024]{1,0:T(8,128)}, u32[]{:S(2)}, u32[]{:S(2)}) collective-permute-start(f32[128,1024]{1,0:T(8,128)} %get-tuple-element.82), channel_id=1, source_target_pairs={{0,2},{1,3},{2,0},{3,1},{4,6},{5,7},{6,4},{7,5},{8,10},{9,11},{10,... | collective-permute-start | bytes 1572872 | tf_op jit(solution)/shard_map/grad_conv_2/ppermute | solution.py:515
  122.8 84.4 %collective-permute-start.13 = (f32[128,1024]{1,0:T(8,128)}, f32[128,1024]{1,0:T(8,128)}, u32[]{:S(2)}, u32[]{:S(2)}) collective-permute-start(f32[128,1024]{1,0:T(8,128)} %get-tuple-element.83), channel_id=1, source_target_pairs={{0,3},{1,2},{2,1},{3,0},{4,7},{5,6},{6,5},{7,4},{8,11},{9,10},{10,... | collective-permute-start | bytes 1572872 | tf_op jit(solution)/shard_map/grad_conv_3/ppermute | solution.py:515
  175.5 55.4 %collective-permute-start.15 = (f32[128,1024]{1,0:T(8,128)S(1)}, f32[128,1024]{1,0:T(8,128)S(1)}, u32[]{:S(2)}, u32[]{:S(2)}) collective-permute-start(f32[128,1024]{1,0:T(8,128)S(1)} %copy-done.56), channel_id=1, source_target_pairs={{0,4},{1,5},{2,6},{3,7},{4,0},{5,1},{6,2},{7,3},{8,12},{9,13},{10,... | collective-permute-start | bytes 1572872 | tf_op jit(solution)/shard_map/grad_conv_4/ppermute | solution.py:515
  203.2 27.7 %collective-permute-start.20 = (f32[128,1024]{1,0:T(8,128)S(1)}, f32[128,1024]{1,0:T(8,128)S(1)}, u32[]{:S(2)}, u32[]{:S(2)}) collective-permute-start(f32[128,1024]{1,0:T(8,128)S(1)} %copy-done.55), channel_id=1, source_target_pairs={{0,1},{1,0},{2,3},{3,2},{4,5},{5,4},{6,7},{7,6},{8,9},{9,8},{10,11... | collective-permute-start | bytes 1572872 | tf_op jit(solution)/shard_map/grad_conv_1/ppermute | solution.py:515
  203.7 61.7 %collective-permute-start.10 = (f32[128,1024]{1,0:T(8,128)S(1)}, f32[128,1024]{1,0:T(8,128)S(1)}, u32[]{:S(2)}, u32[]{:S(2)}) collective-permute-start(f32[128,1024]{1,0:T(8,128)S(1)} %get-tuple-element.80), channel_id=1, source_target_pairs={{0,6},{1,7},{2,4},{3,5},{4,2},{5,3},{6,0},{7,1},{8,14},{9,15},{10,... | collective-permute-start | bytes 1572872 | tf_op jit(solution)/shard_map/conv_6/ppermute | solution.py:515
  205.6 59.8 %collective-permute-start.8 = (f32[128,1024]{1,0:T(8,128)S(1)}, f32[128,1024]{1,0:T(8,128)S(1)}, u32[]{:S(2)}, u32[]{:S(2)}) collective-permute-start(f32[128,1024]{1,0:T(8,128)S(1)} %get-tuple-element.77), channel_id=1, source_target_pairs={{0,7},{1,6},{2,5},{3,4},{4,3},{5,2},{6,1},{7,0},{8,15},{9,14},{10,... | collective-permute-start | bytes 1572872 | tf_op jit(solution)/shard_map/conv_7/ppermute | solution.py:515
  266.2 142.7 %reduce-scatter.5.cloned.1.call-start = ((), (), s32[]{:S(2)}) async-start(), calls=%async_computation.3 | async-start | bytes 655360 | tf_op jit(solution)/shard_map/reduce_scatter | solution.py:664
  266.3 34.2 %collective-permute-start.14 = (f32[128,1024]{1,0:T(8,128)}, f32[128,1024]{1,0:T(8,128)S(1)}, u32[]{:S(2)}, u32[]{:S(2)}) collective-permute-start(f32[128,1024]{1,0:T(8,128)} %get-tuple-element.85), channel_id=1, source_target_pairs={{0,5},{1,4},{2,7},{3,6},{4,1},{5,0},{6,3},{7,2},{8,13},{9,12},{10,... | collective-permute-start | bytes 1572872 | tf_op jit(solution)/shard_map/conv_5/ppermute | solution.py:515
  266.4 52.0 %collective-permute-start.19 = (f32[128,1024]{1,0:T(8,128)}, f32[128,1024]{1,0:T(8,128)}, u32[]{:S(2)}, u32[]{:S(2)}) collective-permute-start(f32[128,1024]{1,0:T(8,128)} %get-tuple-element.94), channel_id=1, source_target_pairs={{0,3},{1,2},{2,1},{3,0},{4,7},{5,6},{6,5},{7,4},{8,11},{9,10},{10,... | collective-permute-start | bytes 1572872 | tf_op jit(solution)/shard_map/conv_3/ppermute | solution.py:515
  266.4 51.9 %collective-permute-start.18 = (f32[128,1024]{1,0:T(8,128)}, f32[128,1024]{1,0:T(8,128)}, u32[]{:S(2)}, u32[]{:S(2)}) collective-permute-start(f32[128,1024]{1,0:T(8,128)} %get-tuple-element.92), channel_id=1, source_target_pairs={{0,1},{1,0},{2,3},{3,2},{4,5},{5,4},{6,7},{7,6},{8,9},{9,8},{10,11... | collective-permute-start | bytes 1572872 | tf_op jit(solution)/shard_map/conv_1/ppermute | solution.py:515
  267.4 76.3 %collective-permute-start.17 = (f32[128,1024]{1,0:T(8,128)}, f32[128,1024]{1,0:T(8,128)}, u32[]{:S(2)}, u32[]{:S(2)}) collective-permute-start(f32[128,1024]{1,0:T(8,128)} %get-tuple-element.90), channel_id=1, source_target_pairs={{0,2},{1,3},{2,0},{3,1},{4,6},{5,7},{6,4},{7,5},{8,10},{9,11},{10,... | collective-permute-start | bytes 1572872 | tf_op jit(solution)/shard_map/conv_2/ppermute | solution.py:515
  268.7 46.5 %collective-permute-start.16 = (f32[128,1024]{1,0:T(8,128)}, f32[128,1024]{1,0:T(8,128)}, u32[]{:S(2)}, u32[]{:S(2)}) collective-permute-start(f32[128,1024]{1,0:T(8,128)} %get-tuple-element.88), channel_id=1, source_target_pairs={{0,4},{1,5},{2,6},{3,7},{4,0},{5,1},{6,2},{7,3},{8,12},{9,13},{10,... | collective-permute-start | bytes 1572872 | tf_op jit(solution)/shard_map/conv_4/ppermute | solution.py:515
  301.3 42.4 %collective-permute-start.21 = (f32[128,1024]{1,0:T(8,128)}, f32[128,1024]{1,0:T(8,128)S(1)}, u32[]{:S(2)}, u32[]{:S(2)}) collective-permute-start(f32[128,1024]{1,0:T(8,128)} %get-tuple-element.99), channel_id=1, source_target_pairs={{0,7},{1,6},{2,5},{3,4},{4,3},{5,2},{6,1},{7,0},{8,15},{9,14},{10,... | collective-permute-start | bytes 1572872 | tf_op jit(solution)/shard_map/grad_gated_7/ppermute | solution.py:515
  315.2 43.1 %collective-permute-start.24 = (f32[128,1024]{1,0:T(8,128)}, f32[128,1024]{1,0:T(8,128)S(1)}, u32[]{:S(2)}, u32[]{:S(2)}) collective-permute-start(f32[128,1024]{1,0:T(8,128)} %copy-done.53), channel_id=1, source_target_pairs={{0,6},{1,7},{2,4},{3,5},{4,2},{5,3},{6,0},{7,1},{8,14},{9,15},{10,... | collective-permute-start | bytes 1572872 | tf_op jit(solution)/shard_map/grad_gated_6/ppermute | solution.py:515
  344.5 37.2 %collective-permute-start.22 = (f32[128,1024]{1,0:T(8,128)}, f32[128,1024]{1,0:T(8,128)S(1)}, u32[]{:S(2)}, u32[]{:S(2)}) collective-permute-start(f32[128,1024]{1,0:T(8,128)} %copy-done.52), channel_id=1, source_target_pairs={{0,5},{1,4},{2,7},{3,6},{4,1},{5,0},{6,3},{7,2},{8,13},{9,12},{10,... | collective-permute-start | bytes 1572872 | tf_op jit(solution)/shard_map/grad_gated_5/ppermute | solution.py:515
  359.1 50.8 %collective-permute-start.25 = (f32[128,1024]{1,0:T(8,128)}, f32[128,1024]{1,0:T(8,128)}, u32[]{:S(2)}, u32[]{:S(2)}) collective-permute-start(f32[128,1024]{1,0:T(8,128)} %copy-done.51), channel_id=1, source_target_pairs={{0,4},{1,5},{2,6},{3,7},{4,0},{5,1},{6,2},{7,3},{8,12},{9,13},{10,... | collective-permute-start | bytes 1572872 | tf_op jit(solution)/shard_map/grad_gated_4/ppermute | solution.py:515
  382.5 33.3 %collective-permute-start.26 = (f32[128,1024]{1,0:T(8,128)}, f32[128,1024]{1,0:T(8,128)}, u32[]{:S(2)}, u32[]{:S(2)}) collective-permute-start(f32[128,1024]{1,0:T(8,128)} %copy-done.50), channel_id=1, source_target_pairs={{0,2},{1,3},{2,0},{3,1},{4,6},{5,7},{6,4},{7,5},{8,10},{9,11},{10,... | collective-permute-start | bytes 1572872 | tf_op jit(solution)/shard_map/grad_gated_2/ppermute | solution.py:515
  401.9 25.1 %collective-permute-start.23 = (f32[128,1024]{1,0:T(8,128)}, f32[128,1024]{1,0:T(8,128)}, u32[]{:S(2)}, u32[]{:S(2)}) collective-permute-start(f32[128,1024]{1,0:T(8,128)} %copy-done.48), channel_id=1, source_target_pairs={{0,3},{1,2},{2,1},{3,0},{4,7},{5,6},{6,5},{7,4},{8,11},{9,10},{10,... | collective-permute-start | bytes 1572872 | tf_op jit(solution)/shard_map/grad_gated_3/ppermute | solution.py:515
  409.9 19.0 %collective-permute-start.30 = (f32[32,1024]{1,0:T(8,128)S(1)}, f32[32,1024]{1,0:T(8,128)S(1)}, u32[]{:S(2)}, u32[]{:S(2)}) collective-permute-start(f32[32,1024]{1,0:T(8,128)S(1)} %multiply_bitcast_fusion.16), channel_id=1, source_target_pairs={{0,24},{8,16},{16,8},{24,0},{1,25},{9,17},{17,9},{25,1},{2,26},{10... | collective-permute-start | bytes 393224 | tf_op jit(solution)/shard_map/parts_gather/ppermute | solution.py:515
  410.0 18.9 %collective-permute-start.29 = (f32[32,1024]{1,0:T(8,128)S(1)}, f32[32,1024]{1,0:T(8,128)S(1)}, u32[]{:S(2)}, u32[]{:S(2)}) collective-permute-start(f32[32,1024]{1,0:T(8,128)S(1)} %multiply_bitcast_fusion.16), channel_id=1, source_target_pairs={{0,16},{8,24},{16,0},{24,8},{1,17},{9,25},{17,1},{25,9},{2,18},{10... | collective-permute-start | bytes 393224 | tf_op jit(solution)/shard_map/parts_gather/ppermute | solution.py:515
  (61 other events, 809.9 us)
Sparse Core Ops, SparseCore 0:
  116.4 36.1 all-gather.2
  266.3 48.8 reduce-scatter.2
  317.6 30.5 reduce-scatter.4

commit v4 on v3

--- a/solution.py
+++ b/solution.py
@@ -598,7 +598,7 @@
     for i in range(2, len(far)):
         order = order + near[i - 2 : i - 1] + far[i : i + 1]
     order = order[:-1] + near[len(far) - 2 :] + order[-1:]
-    last_order = far + near[:1] + near[2:] + near[1:2]
+    last_order = far[:-1] + near + far[-1:]
     by_block = functools.partial(block_views, plan, owners)
     by_tile = functools.partial(tile_views, plan, (parts, rows, cols), False)
     by_row = functools.partial(tile_views, plan, (parts, rows, cols), True)
@@ -657,14 +657,14 @@
     tile_shape = (parts * cols, rows, height, side)
     cot, term = term_of(plan, me, spec, grad_conv, by_block, tile_shape, by_row)
     back_out = grad_of(plan, me, filt, cot, owners, by_block)
-    grad_gated = exchange(back_out, "grad_gated", last_order, 2, 3)
+    grad_gated = exchange(back_out, "grad_gated", [step for step in last_order if step != near[-1]], 3, 2)
+    every = [0] + order
+    (grad_outer,) = gated_by(me, every, [conv[step] for step in every], [grad_out[0]])
 
     term = after([conv[step] for step in far[:2]], term)
     term = lax.psum_scatter(term, ("dp", "col"), scatter_dimension=0, tiled=False)
+    term = after([grad_outer] + [grad_gated[step] for step in far[:1]], term)
     total = lax.psum_scatter(term, "row", scatter_dimension=0, tiled=False) * (1.0 / side)
-    every = [0] + last_order
-    (grad_outer,) = gated_by(me, every, [conv[step] for step in every], [grad_out[0]])
-    total = after(grad_outer, total)
     with jax.named_scope("parts_gather"):
         others = [pairwise(total, "dp", i) for i in range(1, parts)]
     pieces = jnp.stack([total] + others)
@@ -675,7 +675,10 @@
         pieces = jnp.where(upper, swapped.reshape(pieces.shape), pieces)
         bit *= 2
     grad_filter = pieces.reshape(block, side)
-
+    with jax.named_scope(f"grad_gated_{near[-1]}"):
+        grad_gated[near[-1]] = pairwise(back_out[near[-1]], ("row", "col"), near[-1])
+
+    every = [0] + near + far
     gates = [signal[0], inner_gate[0]]
     early, late = every[:-1], every[-1:]
     done = gated_by(me, early, [grad_gated[step] for step in early], gates)

time: 444 us -> 439 us (0.989); the launches traced: 437 us -> 438 us
  waiting for transfers between devices: 163 us -> 204 us
  starting transfers between devices: 110 us -> 82.2 us
  local copies, waits for them, and re-layouts: 45.4 us -> 32.3 us
    ppermute x31, waiting for transfers between devices: 119 us -> 175 us  [pairwise(): lax.ppermute(block, axis, [(i, i ^ step) for i in range(lax.axis_size(axi...]
    ppermute x31, starting transfers between devices: 110 us -> 82.1 us  [pairwise(): lax.ppermute(block, axis, [(i, i ^ step) for i in range(lax.axis_size(axi...]
    reduce_scatter x1, waiting for transfers between devices: 13.9 us -> 0.02 us  [channel_shards(): lax.psum_scatter(term, ('dp', 'col'), scatter_dimension=0, tiled=False)]
    unnamed x118 -> x110, local copies, waits for them, and re-layouts: 45.2 us -> 32.2 us
  transfers between devices with their start and end apart: 34 -> 34, of which waited for: 9 -> 11; matrix products, arithmetic and copies ran while one was open for 2% -> 2% of each run, Pallas kernels for 21% -> 21%
where the time goes in v4:
time: 439 us; the launch traced here: 438 us
  waiting for transfers between devices  204 us (46%)
  Pallas kernels  91.9 us (21%)
  starting transfers between devices  82.2 us (19%)
  local copies, waits for them, and re-layouts  32.3 us (7%)
  between operations  14.4 us (3%)
  other arithmetic  12.8 us (3%)
    ppermute x31, waiting for transfers between devices, pairwise(): lax.ppermute(block, axis, [(i, i ^ step) for i in range(lax.axis_size(axi...  175 us
    pallas_call x4, Pallas kernels, call_kernel(): pl.pallas_call(kernel, out_shape=out_shape, in_specs=in_specs, out_specs=...  82.3 us
    ppermute x31, starting transfers between devices, pairwise(): lax.ppermute(block, axis, [(i, i ^ step) for i in range(lax.axis_size(axi...  82.1 us
    unnamed x110, local copies, waits for them, and re-layouts  32.2 us
    all_gather x1, waiting for transfers between devices, channel_shards(): over_all = [lax.all_gather(over_row, ('dp', 'col'))]  29.7 us
    pallas_call x3, Pallas kernels, gated_by(): pl.pallas_call(functools.partial(gate_kernel, steps, len(gates)), grid_sp...  9.6 us
  transfers between devices with their start and end apart: 34, of which 11 were waited for; matrix products, arithmetic and copies ran while one was open for 2% of the time, Pallas kernels for 21%

profile of v4, /device:TPU:7, one launch (start us, length us, event | category | flops | bytes accessed | tf_op | source)
XLA Modules:
  0.0 438.0 jit_solution(5155347717982705120)
XLA Ops:
  8.3 3.9 collective-permute-start.3
  13.2 3.8 multiply_bitcast_fusion.8
  17.3 3.8 collective-permute-start.5
  22.0 2.9 collective-permute-done.3.refs_7_
  24.9 25.6 %collective-permute-start.4 = (f32[160,1024]{1,0:T(8,128)S(1)}, f32[160,1024]{1,0:T(8,128)S(1)}, u32[]{:S(2)}, u32[]{:S(2)}) collective-permute-start(f32[160,1024]{1,0:T(8,128)S(1)} %get-tuple-element.63), channel_id=1, source_target_pairs={{0,4},{1,5},{2,6},{3,7},{4,0},{5,1},{6,2},{7,3},{8,12},{9,13},{10,... | collective-permute-start | bytes 1966088 | tf_op jit(solution)/shard_map/gated_4/ppermute | solution.py:515
  50.5 2.2 multiply_bitcast_fusion
  55.2 58.5 %collective-permute-done.4.refs_4_ = f32[160,1024]{1,0:T(8,128)S(1)} collective-permute-done((f32[160,1024]{1,0:T(8,128)S(1)}, f32[160,1024]{1,0:T(8,128)S(1)}, u32[]{:S(2)}, u32[]{:S(2)}) %collective-permute-start.4) | collective-permute-done | bytes 655392 | tf_op jit(solution)/shard_map/gated_4/ppermute | solution.py:515
  116.3 2.7 collective-permute-start.7
  120.0 2.7 collective-permute-start.14
  122.8 29.7 %all-gather.3.cloned.1.call-done = f32[32,32,1024]{2,1,0:T(8,128)} async-done(((f32[4,32,1024]{2,1,0:T(8,128)}), f32[32,32,1024]{2,1,0:T(8,128)}) %all-gather.3.cloned.1.call-update) | async-done | bytes 4194320 | tf_op jit(solution)/shard_map/all_gather | solution.py:648
  152.5 2.2 copy-done
  154.7 2.2 copy-done.2
  160.4 15.0 %filter_spectrum.1.filt = f32[2,528,1024]{2,1,0:T(8,128)S(1)} custom-call(s32[1]{0:T(128)} %bitcast.me, f32[8,4,32,1024]{3,2,1,0:T(8,128)S(1)} %bitcast.73, bf16[2,544,512]{2,1,0:T(8,128)(2,1)S(1)} %copy-done.11, bf16[2,512,512]{2,1,0:T(8,128)(2,1)S(1)} %copy-done.14, f32[2,528,1024]{2,1,0:T(8,128)S(1)} %copy-done, bf16[2,4,512,512]{3,2,1,0:T(8,128)(2,1)S(1)} %copy-done.2), custom_call_target="tpu_custom_call" | custom-call | flops 1048576 | bytes 1048576 | tf_op jit(solution)/shard_map/filter_spectrum/pallas_call | solution.py:419
  175.5 2.2 collective-permute-start.11
  177.8 24.3 %conv_of.1 = (f32[2,528,1024]{2,1,0:T(8,128)S(1)}, f32[128,1024]{1,0:T(8,128)S(1)}, f32[128,1024]{1,0:T(8,128)}, f32[128,1024]{1,0:T(8,128)}, f32[128,1024]{1,0:...) custom-call(s32[1]{0:T(128)} %bitcast.me, ...), custom_call_target="tpu_custom_call" | custom-call | flops 1048576 | bytes 1048576 | tf_op jit(solution)/shard_map/conv_of/pallas_call | solution.py:419
  207.1 23.8 %collective-permute-done.11.refs_4_ = f32[128,1024]{1,0:T(8,128)S(1)} collective-permute-done((f32[128,1024]{1,0:T(8,128)S(1)}, f32[128,1024]{1,0:T(8,128)S(1)}, u32[]{:S(2)}, u32[]{:S(2)}) %collective-permute-start.11) | collective-permute-done | bytes 524320 | tf_op jit(solution)/shard_map/grad_conv_4/ppermute | solution.py:515
  230.9 30.4 %term_of.1 = (f32[2,528,1024]{2,1,0:T(8,128)S(1)}, f32[8,4,32,1024]{3,2,1,0:T(8,128)S(1)}) custom-call(s32[1]{0:T(128)} %bitcast.me, f32[2,528,1024]{2,1,0:T(8,128)S(1)} %get-tuple-element.94.gated, f32[128,1024]{1,0:T(8,128)S(1)} %copy-done.21, f32[128,1024]{1,0:T(8,128)S(1)} %collective-permute-done.20.refs_1_, ...), custom_call_target="tpu_custom_call" | custom-call | flops 1048576 | bytes 1048576 | tf_op jit(solution)/shard_map/term_of/pallas_call | solution.py:419
  269.0 2.5 collective-permute-start.16
  273.4 2.7 copy-done.1
  276.1 2.6 copy-done.4
  278.7 2.4 copy-done.6
  281.1 2.2 copy-done.18
  283.3 12.6 %grad_of.1 = (f32[128,1024]{1,0:T(8,128)S(1)}, f32[128,1024]{1,0:T(8,128)S(1)}, f32[128,1024]{1,0:T(8,128)S(1)}, f32[128,1024]{1,0:T(8,128)S(1)}, f32[128,1024]{...) custom-call(s32[1]{0:T(128)} %bitcast.me, ...), custom_call_target="tpu_custom_call" | custom-call | flops 1048576 | bytes 1048576 | tf_op jit(solution)/shard_map/grad_of/pallas_call | solution.py:419
  297.4 9.2 %collective-permute-done.16.refs_4_ = f32[128,1024]{1,0:T(8,128)S(1)} collective-permute-done((f32[128,1024]{1,0:T(8,128)}, f32[128,1024]{1,0:T(8,128)S(1)}, u32[]{:S(2)}, u32[]{:S(2)}) %collective-permute-start.16) | collective-permute-done | bytes 524320 | tf_op jit(solution)/shard_map/conv_5/ppermute | solution.py:515
  306.6 21.2 %collective-permute-done.12.refs_3_ = f32[128,1024]{1,0:T(8,128)S(1)} collective-permute-done((f32[128,1024]{1,0:T(8,128)}, f32[128,1024]{1,0:T(8,128)S(1)}, u32[]{:S(2)}, u32[]{:S(2)}) %collective-permute-start.12) | collective-permute-done | bytes 524320 | tf_op jit(solution)/shard_map/conv_2/ppermute | solution.py:515
  327.8 3.6 gate_out.3
  332.7 17.4 %collective-permute-done.23.refs_5_ = f32[128,1024]{1,0:T(8,128)S(1)} collective-permute-done((f32[128,1024]{1,0:T(8,128)}, f32[128,1024]{1,0:T(8,128)S(1)}, u32[]{:S(2)}, u32[]{:S(2)}) %collective-permute-start.23) | collective-permute-done | bytes 524320 | tf_op jit(solution)/shard_map/grad_gated_6/ppermute | solution.py:515
  350.9 24.9 %collective-permute-start.24 = (f32[128,1024]{1,0:T(8,128)}, f32[128,1024]{1,0:T(8,128)}, u32[]{:S(2)}, u32[]{:S(2)}) collective-permute-start(f32[128,1024]{1,0:T(8,128)} %copy-done.46), channel_id=1, source_target_pairs={{0,2},{1,3},{2,0},{3,1},{4,6},{5,7},{6,4},{7,5},{8,10},{9,11},{10,... | collective-permute-start | bytes 1572872 | tf_op jit(solution)/shard_map/grad_gated_2/ppermute | solution.py:515
  380.1 7.6 %collective-permute-done.27.refs_6_ = f32[128,1024]{1,0:T(8,128)} collective-permute-done((f32[128,1024]{1,0:T(8,128)}, f32[128,1024]{1,0:T(8,128)}, u32[]{:S(2)}, u32[]{:S(2)}) %collective-permute-start.27) | collective-permute-done | bytes 524320 | tf_op jit(solution)/shard_map/grad_gated_5/ppermute | solution.py:515
  387.7 21.7 %collective-permute-done.24.refs_1_ = f32[128,1024]{1,0:T(8,128)} collective-permute-done((f32[128,1024]{1,0:T(8,128)}, f32[128,1024]{1,0:T(8,128)}, u32[]{:S(2)}, u32[]{:S(2)}) %collective-permute-start.24) | collective-permute-done | bytes 524320 | tf_op jit(solution)/shard_map/grad_gated_2/ppermute | solution.py:515
  409.4 11.2 %collective-permute-done.25.refs_2_ = f32[128,1024]{1,0:T(8,128)} collective-permute-done((f32[128,1024]{1,0:T(8,128)}, f32[128,1024]{1,0:T(8,128)}, u32[]{:S(2)}, u32[]{:S(2)}) %collective-permute-start.25) | collective-permute-done | bytes 524320 | tf_op jit(solution)/shard_map/grad_gated_3/ppermute | solution.py:515
  423.3 4.1 gate_out.4
  (173 shorter events, 41.7 us)
Async XLA Ops:
  7.2 145.3 %all-gather.3.cloned.1.call-start = ((), (), s32[]{:S(2)}) async-start(), calls=%async_computation.4 | async-start | bytes 4718592 | tf_op jit(solution)/shard_map/all_gather | solution.py:648
  17.2 35.6 %collective-permute-start.6 = (f32[160,1024]{1,0:T(8,128)S(1)}, f32[160,1024]{1,0:T(8,128)S(1)}, u32[]{:S(2)}, u32[]{:S(2)}) collective-permute-start(f32[160,1024]{1,0:T(8,128)S(1)} %get-tuple-element.135), channel_id=1, source_target_pairs={{0,6},{1,7},{2,4},{3,5},{4,2},{5,3},{6,0},{7,1},{8,14},{9,15},{10,... | collective-permute-start | bytes 1966088 | tf_op jit(solution)/shard_map/gated_6/ppermute | solution.py:515
  17.2 37.1 %collective-permute-start.1 = (f32[160,1024]{1,0:T(8,128)S(1)}, f32[160,1024]{1,0:T(8,128)S(1)}, u32[]{:S(2)}, u32[]{:S(2)}) collective-permute-start(f32[160,1024]{1,0:T(8,128)S(1)} %get-tuple-element.137), channel_id=1, source_target_pairs={{0,2},{1,3},{2,0},{3,1},{4,6},{5,7},{6,4},{7,5},{8,10},{9,11},{10,... | collective-permute-start | bytes 1966088 | tf_op jit(solution)/shard_map/gated_2/ppermute | solution.py:515
  17.3 98.0 %collective-permute-start.5 = (f32[128,1024]{1,0:T(8,128)}, f32[128,1024]{1,0:T(8,128)S(1)}, u32[]{:S(2)}, u32[]{:S(2)}) collective-permute-start(f32[128,1024]{1,0:T(8,128)} %get-tuple-element.127), channel_id=1, source_target_pairs={{0,5},{1,4},{2,7},{3,6},{4,1},{5,0},{6,3},{7,2},{8,13},{9,12},{10,... | collective-permute-start | bytes 1572872 | tf_op jit(solution)/shard_map/gated_5/ppermute | solution.py:515
  21.1 94.3 %collective-permute-start.2 = (f32[128,1024]{1,0:T(8,128)}, f32[128,1024]{1,0:T(8,128)}, u32[]{:S(2)}, u32[]{:S(2)}) collective-permute-start(f32[128,1024]{1,0:T(8,128)} %get-tuple-element.129), channel_id=1, source_target_pairs={{0,3},{1,2},{2,1},{3,0},{4,7},{5,6},{6,5},{7,4},{8,11},{9,10},{10,... | collective-permute-start | bytes 1572872 | tf_op jit(solution)/shard_map/gated_3/ppermute | solution.py:515
  24.9 88.8 %collective-permute-start.4 = (f32[160,1024]{1,0:T(8,128)S(1)}, f32[160,1024]{1,0:T(8,128)S(1)}, u32[]{:S(2)}, u32[]{:S(2)}) collective-permute-start(f32[160,1024]{1,0:T(8,128)S(1)} %get-tuple-element.63), channel_id=1, source_target_pairs={{0,4},{1,5},{2,6},{3,7},{4,0},{5,1},{6,2},{7,3},{8,12},{9,13},{10,... | collective-permute-start | bytes 1966088 | tf_op jit(solution)/shard_map/gated_4/ppermute | solution.py:515
  52.7 62.6 %collective-permute-start = (f32[128,1024]{1,0:T(8,128)}, f32[128,1024]{1,0:T(8,128)S(1)}, u32[]{:S(2)}, u32[]{:S(2)}) collective-permute-start(f32[128,1024]{1,0:T(8,128)} %get-tuple-element.131), channel_id=1, source_target_pairs={{0,1},{1,0},{2,3},{3,2},{4,5},{5,4},{6,7},{7,6},{8,9},{9,8},{10,11... | collective-permute-start | bytes 1572872 | tf_op jit(solution)/shard_map/gated_1/ppermute | solution.py:515
  116.2 215.2 %reduce-scatter.3.cloned.1.call-start = ((), (), s32[]{:S(2)}) async-start(), calls=%async_computation.2 | async-start | bytes 4718592 | tf_op jit(solution)/shard_map/reduce_scatter | solution.py:665
  116.3 59.2 %collective-permute-start.7 = (f32[128,1024]{1,0:T(8,128)}, f32[128,1024]{1,0:T(8,128)}, u32[]{:S(2)}, u32[]{:S(2)}) collective-permute-start(f32[128,1024]{1,0:T(8,128)} %get-tuple-element.65), channel_id=1, source_target_pairs={{0,7},{1,6},{2,5},{3,4},{4,3},{5,2},{6,1},{7,0},{8,15},{9,14},{10,... | collective-permute-start | bytes 1572872 | tf_op jit(solution)/shard_map/grad_conv_7/ppermute | solution.py:515
  118.9 84.0 %collective-permute-start.9 = (f32[128,1024]{1,0:T(8,128)}, f32[128,1024]{1,0:T(8,128)}, u32[]{:S(2)}, u32[]{:S(2)}) collective-permute-start(f32[128,1024]{1,0:T(8,128)} %get-tuple-element.77), channel_id=1, source_target_pairs={{0,6},{1,7},{2,4},{3,5},{4,2},{5,3},{6,0},{7,1},{8,14},{9,15},{10,... | collective-permute-start | bytes 1572872 | tf_op jit(solution)/shard_map/grad_conv_6/ppermute | solution.py:515
  120.0 83.5 %collective-permute-start.13 = (f32[128,1024]{1,0:T(8,128)}, f32[128,1024]{1,0:T(8,128)}, u32[]{:S(2)}, u32[]{:S(2)}) collective-permute-start(f32[128,1024]{1,0:T(8,128)} %get-tuple-element.83), channel_id=1, source_target_pairs={{0,5},{1,4},{2,7},{3,6},{4,1},{5,0},{6,3},{7,2},{8,13},{9,12},{10,... | collective-permute-start | bytes 1572872 | tf_op jit(solution)/shard_map/grad_conv_5/ppermute | solution.py:515
  120.0 85.4 %collective-permute-start.14 = (f32[128,1024]{1,0:T(8,128)}, f32[128,1024]{1,0:T(8,128)}, u32[]{:S(2)}, u32[]{:S(2)}) collective-permute-start(f32[128,1024]{1,0:T(8,128)} %get-tuple-element.84), channel_id=1, source_target_pairs={{0,2},{1,3},{2,0},{3,1},{4,6},{5,7},{6,4},{7,5},{8,10},{9,11},{10,... | collective-permute-start | bytes 1572872 | tf_op jit(solution)/shard_map/grad_conv_2/ppermute | solution.py:515
  122.8 84.3 %collective-permute-start.15 = (f32[128,1024]{1,0:T(8,128)}, f32[128,1024]{1,0:T(8,128)}, u32[]{:S(2)}, u32[]{:S(2)}) collective-permute-start(f32[128,1024]{1,0:T(8,128)} %get-tuple-element.85), channel_id=1, source_target_pairs={{0,3},{1,2},{2,1},{3,0},{4,7},{5,6},{6,5},{7,4},{8,11},{9,10},{10,... | collective-permute-start | bytes 1572872 | tf_op jit(solution)/shard_map/grad_conv_3/ppermute | solution.py:515
  175.5 55.4 %collective-permute-start.11 = (f32[128,1024]{1,0:T(8,128)S(1)}, f32[128,1024]{1,0:T(8,128)S(1)}, u32[]{:S(2)}, u32[]{:S(2)}) collective-permute-start(f32[128,1024]{1,0:T(8,128)S(1)} %copy-done.52), channel_id=1, source_target_pairs={{0,4},{1,5},{2,6},{3,7},{4,0},{5,1},{6,2},{7,3},{8,12},{9,13},{10,... | collective-permute-start | bytes 1572872 | tf_op jit(solution)/shard_map/grad_conv_4/ppermute | solution.py:515
  202.9 27.9 %collective-permute-start.20 = (f32[128,1024]{1,0:T(8,128)S(1)}, f32[128,1024]{1,0:T(8,128)S(1)}, u32[]{:S(2)}, u32[]{:S(2)}) collective-permute-start(f32[128,1024]{1,0:T(8,128)S(1)} %copy-done.51), channel_id=1, source_target_pairs={{0,1},{1,0},{2,3},{3,2},{4,5},{5,4},{6,7},{7,6},{8,9},{9,8},{10,11... | collective-permute-start | bytes 1572872 | tf_op jit(solution)/shard_map/grad_conv_1/ppermute | solution.py:515
  203.5 61.9 %collective-permute-start.10 = (f32[128,1024]{1,0:T(8,128)S(1)}, f32[128,1024]{1,0:T(8,128)S(1)}, u32[]{:S(2)}, u32[]{:S(2)}) collective-permute-start(f32[128,1024]{1,0:T(8,128)S(1)} %get-tuple-element.79), channel_id=1, source_target_pairs={{0,6},{1,7},{2,4},{3,5},{4,2},{5,3},{6,0},{7,1},{8,14},{9,15},{10,... | collective-permute-start | bytes 1572872 | tf_op jit(solution)/shard_map/conv_6/ppermute | solution.py:515
  205.4 60.8 %collective-permute-start.8 = (f32[128,1024]{1,0:T(8,128)S(1)}, f32[128,1024]{1,0:T(8,128)S(1)}, u32[]{:S(2)}, u32[]{:S(2)}) collective-permute-start(f32[128,1024]{1,0:T(8,128)S(1)} %get-tuple-element.76), channel_id=1, source_target_pairs={{0,7},{1,6},{2,5},{3,4},{4,3},{5,2},{6,1},{7,0},{8,15},{9,14},{10,... | collective-permute-start | bytes 1572872 | tf_op jit(solution)/shard_map/conv_7/ppermute | solution.py:515
  267.0 112.1 %reduce-scatter.5.cloned.1.call-start = ((), (), s32[]{:S(2)}) async-start(), calls=%async_computation.3 | async-start | bytes 655360 | tf_op jit(solution)/shard_map/reduce_scatter | solution.py:667
  268.0 28.0 %collective-permute-start.19 = (f32[128,1024]{1,0:T(8,128)S(1)}, f32[128,1024]{1,0:T(8,128)S(1)}, u32[]{:S(2)}, u32[]{:S(2)}) collective-permute-start(f32[128,1024]{1,0:T(8,128)S(1)} %copy-done.45), channel_id=1, source_target_pairs={{0,4},{1,5},{2,6},{3,7},{4,0},{5,1},{6,2},{7,3},{8,12},{9,13},{10,... | collective-permute-start | bytes 1572872 | tf_op jit(solution)/shard_map/conv_4/ppermute | solution.py:515
  268.0 28.3 %collective-permute-start.18 = (f32[128,1024]{1,0:T(8,128)}, f32[128,1024]{1,0:T(8,128)S(1)}, u32[]{:S(2)}, u32[]{:S(2)}) collective-permute-start(f32[128,1024]{1,0:T(8,128)} %get-tuple-element.91), channel_id=1, source_target_pairs={{0,1},{1,0},{2,3},{3,2},{4,5},{5,4},{6,7},{7,6},{8,9},{9,8},{10,11... | collective-permute-start | bytes 1572872 | tf_op jit(solution)/shard_map/conv_1/ppermute | solution.py:515
  269.0 28.5 %collective-permute-start.17 = (f32[128,1024]{1,0:T(8,128)}, f32[128,1024]{1,0:T(8,128)S(1)}, u32[]{:S(2)}, u32[]{:S(2)}) collective-permute-start(f32[128,1024]{1,0:T(8,128)} %get-tuple-element.89), channel_id=1, source_target_pairs={{0,3},{1,2},{2,1},{3,0},{4,7},{5,6},{6,5},{7,4},{8,11},{9,10},{10,... | collective-permute-start | bytes 1572872 | tf_op jit(solution)/shard_map/conv_3/ppermute | solution.py:515
  269.0 37.6 %collective-permute-start.16 = (f32[128,1024]{1,0:T(8,128)}, f32[128,1024]{1,0:T(8,128)S(1)}, u32[]{:S(2)}, u32[]{:S(2)}) collective-permute-start(f32[128,1024]{1,0:T(8,128)} %get-tuple-element.87), channel_id=1, source_target_pairs={{0,5},{1,4},{2,7},{3,6},{4,1},{5,0},{6,3},{7,2},{8,13},{9,12},{10,... | collective-permute-start | bytes 1572872 | tf_op jit(solution)/shard_map/conv_5/ppermute | solution.py:515
  271.5 56.3 %collective-permute-start.12 = (f32[128,1024]{1,0:T(8,128)}, f32[128,1024]{1,0:T(8,128)S(1)}, u32[]{:S(2)}, u32[]{:S(2)}) collective-permute-start(f32[128,1024]{1,0:T(8,128)} %get-tuple-element.82), channel_id=1, source_target_pairs={{0,2},{1,3},{2,0},{3,1},{4,6},{5,7},{6,4},{7,5},{8,10},{9,11},{10,... | collective-permute-start | bytes 1572872 | tf_op jit(solution)/shard_map/conv_2/ppermute | solution.py:515
  296.1 35.4 %collective-permute-start.21 = (f32[128,1024]{1,0:T(8,128)S(1)}, f32[128,1024]{1,0:T(8,128)S(1)}, u32[]{:S(2)}, u32[]{:S(2)}) collective-permute-start(f32[128,1024]{1,0:T(8,128)S(1)} %get-tuple-element.98), channel_id=1, source_target_pairs={{0,7},{1,6},{2,5},{3,4},{4,3},{5,2},{6,1},{7,0},{8,15},{9,14},{10,... | collective-permute-start | bytes 1572872 | tf_op jit(solution)/shard_map/grad_gated_7/ppermute | solution.py:515
  331.6 48.5 %collective-permute-start.26 = (f32[128,1024]{1,0:T(8,128)}, f32[128,1024]{1,0:T(8,128)}, u32[]{:S(2)}, u32[]{:S(2)}) collective-permute-start(f32[128,1024]{1,0:T(8,128)} %copy-done.48), channel_id=1, source_target_pairs={{0,1},{1,0},{2,3},{3,2},{4,5},{5,4},{6,7},{7,6},{8,9},{9,8},{10,11... | collective-permute-start | bytes 1572872 | tf_op jit(solution)/shard_map/grad_gated_1/ppermute | solution.py:515
  332.1 55.6 %collective-permute-start.27 = (f32[128,1024]{1,0:T(8,128)}, f32[128,1024]{1,0:T(8,128)}, u32[]{:S(2)}, u32[]{:S(2)}) collective-permute-start(f32[128,1024]{1,0:T(8,128)} %copy-done.47), channel_id=1, source_target_pairs={{0,5},{1,4},{2,7},{3,6},{4,1},{5,0},{6,3},{7,2},{8,13},{9,12},{10,... | collective-permute-start | bytes 1572872 | tf_op jit(solution)/shard_map/grad_gated_5/ppermute | solution.py:515
  350.9 58.5 %collective-permute-start.24 = (f32[128,1024]{1,0:T(8,128)}, f32[128,1024]{1,0:T(8,128)}, u32[]{:S(2)}, u32[]{:S(2)}) collective-permute-start(f32[128,1024]{1,0:T(8,128)} %copy-done.46), channel_id=1, source_target_pairs={{0,2},{1,3},{2,0},{3,1},{4,6},{5,7},{6,4},{7,5},{8,10},{9,11},{10,... | collective-permute-start | bytes 1572872 | tf_op jit(solution)/shard_map/grad_gated_2/ppermute | solution.py:515
  375.9 44.8 %collective-permute-start.25 = (f32[128,1024]{1,0:T(8,128)}, f32[128,1024]{1,0:T(8,128)}, u32[]{:S(2)}, u32[]{:S(2)}) collective-permute-start(f32[128,1024]{1,0:T(8,128)} %copy-done.43), channel_id=1, source_target_pairs={{0,3},{1,2},{2,1},{3,0},{4,7},{5,6},{6,5},{7,4},{8,11},{9,10},{10,... | collective-permute-start | bytes 1572872 | tf_op jit(solution)/shard_map/grad_gated_3/ppermute | solution.py:515
  378.0 49.4 %collective-permute-start.22 = (f32[128,1024]{1,0:T(8,128)}, f32[128,1024]{1,0:T(8,128)}, u32[]{:S(2)}, u32[]{:S(2)}) collective-permute-start(f32[128,1024]{1,0:T(8,128)} %copy-done.42), channel_id=1, source_target_pairs={{0,4},{1,5},{2,6},{3,7},{4,0},{5,1},{6,2},{7,3},{8,12},{9,13},{10,... | collective-permute-start | bytes 1572872 | tf_op jit(solution)/shard_map/grad_gated_4/ppermute | solution.py:515
  380.0 49.3 %collective-permute-start.30 = (f32[32,1024]{1,0:T(8,128)S(1)}, f32[32,1024]{1,0:T(8,128)S(1)}, u32[]{:S(2)}, u32[]{:S(2)}) collective-permute-start(f32[32,1024]{1,0:T(8,128)S(1)} %get-tuple-element.134), channel_id=1, source_target_pairs={{0,24},{8,16},{16,8},{24,0},{1,25},{9,17},{17,9},{25,1},{2,26},{10... | collective-permute-start | bytes 393224 | tf_op jit(solution)/shard_map/parts_gather/ppermute | solution.py:515
  387.7 41.6 %collective-permute-start.29 = (f32[32,1024]{1,0:T(8,128)S(1)}, f32[32,1024]{1,0:T(8,128)}, u32[]{:S(2)}, u32[]{:S(2)}) collective-permute-start(f32[32,1024]{1,0:T(8,128)S(1)} %get-tuple-element.134), channel_id=1, source_target_pairs={{0,16},{8,24},{16,0},{24,8},{1,17},{9,25},{17,1},{25,9},{2,18},{10... | collective-permute-start | bytes 393224 | tf_op jit(solution)/shard_map/parts_gather/ppermute | solution.py:515
  409.4 20.0 %collective-permute-start.28 = (f32[32,1024]{1,0:T(8,128)S(1)}, f32[32,1024]{1,0:T(8,128)}, u32[]{:S(2)}, u32[]{:S(2)}) collective-permute-start(f32[32,1024]{1,0:T(8,128)S(1)} %get-tuple-element.134), channel_id=1, source_target_pairs={{0,8},{8,0},{16,24},{24,16},{1,9},{9,1},{17,25},{25,17},{2,10},{10... | collective-permute-start | bytes 393224 | tf_op jit(solution)/shard_map/parts_gather/ppermute | solution.py:515
  (57 other events, 1214.3 us)
Sparse Core Ops, SparseCore 0:
  116.3 36.1 all-gather.2
  267.1 48.7 reduce-scatter.2
  331.6 39.8 reduce-scatter.4

commit v5 on v2

--- a/solution.py
+++ b/solution.py
@@ -596,6 +596,7 @@
     for i in range(2, len(far)):
         order = order + near[i - 2 : i - 1] + far[i : i + 1]
     order = order[:-1] + near[len(far) - 2 :] + order[-1:]
+    last_order = far + near
     by_block = functools.partial(block_views, plan, owners)
     by_tile = functools.partial(tile_views, plan, (parts, rows, cols))
 
@@ -644,21 +645,28 @@
     over_all = [lax.all_gather(over_row, ("dp", "col"))]
     filt = filter_spectrum(plan, me, over_all, by_tile, parts * owners)
 
-    spec, conv_out = conv_of(plan, me, filt, after(filt, gated), by_block)
-    for step in near[1:]:
-        grad_conv[step] = after(conv_out[0], grad_conv[step])
-    grad_conv = exchange(grad_conv, "grad_conv", order, 4)
+    got = exchange(grad_conv, "grad_conv", [step for step in order if step != near[-1]], 4)
+    spec, conv_out = conv_of(plan, me, filt, after([filt] + [got[step] for step in far[:1]], gated), by_block)
+    with jax.named_scope(f"grad_conv_{near[-1]}"):
+        got[near[-1]] = pairwise(after(conv_out[0], grad_conv[near[-1]]), ("row", "col"), near[-1])
+    grad_conv = got
     conv = exchange(conv_out, "conv", order, 4)
     tile_shape = (parts * cols, rows, height, side)
     cot, term = term_of(plan, me, spec, grad_conv, by_block, tile_shape, by_tile)
     back_out = grad_of(plan, me, filt, cot, owners, by_block)
-    grad_gated = exchange(back_out, "grad_gated", order, 3, 2)
+    grad_gated = exchange(back_out, "grad_gated", last_order, 2, 3)
 
     term = after([conv[step] for step in far[:2]], term)
     term = lax.psum_scatter(term, ("dp", "col"), scatter_dimension=0, tiled=False)
     with jax.named_scope("rows_sum"):
-        arrived = [pairwise(term[i], "row", i) for i in range(1, rows)]
-    total = sum(arrived, term[0]) * (1.0 / side)
+        term = [term[i] for i in range(rows)]
+        bit = 1
+        while bit < rows:
+            arrived = pairwise(jnp.stack(term[bit::2 * bit]), "row", bit)
+            for j, i in enumerate(range(0, rows, 2 * bit)):
+                term[i] = term[i] + arrived[j]
+            bit *= 2
+    total = term[0] * (1.0 / side)
     every = [0] + order
     (grad_outer,) = gated_by(me, every, [conv[step] for step in every], [grad_out[0]])
     total = after(grad_outer, total)
@@ -673,6 +681,7 @@
         bit *= 2
     grad_filter = pieces.reshape(block, side)
 
+    every = [0] + far + near[::-1]
     gates = [signal[0], inner_gate[0]]
     early, late = every[:-1], every[-1:]
     done = gated_by(me, early, [grad_gated[step] for step in early], gates)

time: 458 us -> 441 us (0.963)
  starting transfers between devices: 128 us -> 74.1 us
  waiting for transfers between devices: 156 us -> 190 us
    ppermute x34 -> x33, starting transfers between devices: 128 us -> 74 us  [pairwise(): lax.ppermute(block, axis, [(i, i ^ step) for i in range(lax.axis_size(axi...]
    ppermute x34 -> x33, waiting for transfers between devices: 116 us -> 160 us  [pairwise(): lax.ppermute(block, axis, [(i, i ^ step) for i in range(lax.axis_size(axi...]
    reduce_scatter x1, waiting for transfers between devices: 10.4 us -> 0.01 us  [channel_shards(): lax.psum_scatter(term, ('dp', 'col'), scatter_dimension=0, tiled=False)]
    unnamed x128 -> x138, local copies, waits for them, and re-layouts: 50 us -> 54.6 us
  transfers between devices with their start and end apart: 36 -> 35, of which waited for: 10 -> 10; matrix products, arithmetic and copies ran while one was open for 2% -> 3% of each run, Pallas kernels for 21% -> 21%
where the time goes in v5:
time: 441 us; the launch traced here: 440 us
  waiting for transfers between devices  190 us (43%)
  Pallas kernels  92.5 us (21%)
  starting transfers between devices  74.1 us (17%)
  local copies, waits for them, and re-layouts  55.7 us (13%)
  between operations  14.7 us (3%)
  other arithmetic  12.8 us (3%)
    ppermute x33, waiting for transfers between devices, pairwise(): lax.ppermute(block, axis, [(i, i ^ step) for i in range(lax.axis_size(axi...  160 us
    pallas_call x4, Pallas kernels, call_kernel(): pl.pallas_call(kernel, out_shape=out_shape, in_specs=in_specs, out_specs=...  83.5 us
    ppermute x33, starting transfers between devices, pairwise(): lax.ppermute(block, axis, [(i, i ^ step) for i in range(lax.axis_size(axi...  74 us
    unnamed x138, local copies, waits for them, and re-layouts  54.6 us
    all_gather x1, waiting for transfers between devices, channel_shards(): over_all = [lax.all_gather(over_row, ('dp', 'col'))]  29.7 us
    pallas_call x3, Pallas kernels, gated_by(): pl.pallas_call(functools.partial(gate_kernel, steps, len(gates)), grid_sp...  9.01 us
  transfers between devices with their start and end apart: 35, of which 10 were waited for; matrix products, arithmetic and copies ran while one was open for 3% of the time, Pallas kernels for 21%

profile of v5, /device:TPU:7, one launch (start us, length us, event | category | flops | bytes accessed | tf_op | source)
XLA Modules:
  0.0 439.9 jit_solution(5954618230063042809)
XLA Ops:
  8.3 3.9 collective-permute-start.3
  13.2 3.8 multiply_bitcast_fusion.8
  17.3 3.7 collective-permute-start.5
  22.0 2.9 collective-permute-done.3.refs_7_
  24.9 25.6 %collective-permute-start.4 = (f32[160,1024]{1,0:T(8,128)S(1)}, f32[160,1024]{1,0:T(8,128)S(1)}, u32[]{:S(2)}, u32[]{:S(2)}) collective-permute-start(f32[160,1024]{1,0:T(8,128)S(1)} %get-tuple-element.64), channel_id=1, source_target_pairs={{0,4},{1,5},{2,6},{3,7},{4,0},{5,1},{6,2},{7,3},{8,12},{9,13},{10,... | collective-permute-start | bytes 1966088 | tf_op jit(solution)/shard_map/gated_4/ppermute | solution.py:513
  50.5 2.2 multiply_bitcast_fusion
  55.2 58.5 %collective-permute-done.4.refs_4_ = f32[160,1024]{1,0:T(8,128)S(1)} collective-permute-done((f32[160,1024]{1,0:T(8,128)S(1)}, f32[160,1024]{1,0:T(8,128)S(1)}, u32[]{:S(2)}, u32[]{:S(2)}) %collective-permute-start.4) | collective-permute-done | bytes 655392 | tf_op jit(solution)/shard_map/gated_4/ppermute | solution.py:513
  116.3 2.7 collective-permute-start.7
  120.1 2.7 collective-permute-start.14
  122.9 29.7 %all-gather.3.cloned.1.call-done = f32[32,32,1024]{2,1,0:T(8,128)} async-done(((f32[4,32,1024]{2,1,0:T(8,128)}), f32[32,32,1024]{2,1,0:T(8,128)}) %all-gather.3.cloned.1.call-update) | async-done | bytes 4194320 | tf_op jit(solution)/shard_map/all_gather | solution.py:645
  152.6 2.2 copy-done
  154.8 2.2 copy-done.2
  160.5 15.0 %filter_spectrum.1.filt = f32[2,528,1024]{2,1,0:T(8,128)S(1)} custom-call(s32[1]{0:T(128)} %bitcast.me, f32[8,4,32,1024]{3,2,1,0:T(8,128)S(1)} %bitcast.93, bf16[2,544,512]{2,1,0:T(8,128)(2,1)S(1)} %copy-done.11, bf16[2,512,512]{2,1,0:T(8,128)(2,1)S(1)} %copy-done.14, f32[2,528,1024]{2,1,0:T(8,128)S(1)} %copy-done, bf16[2,4,512,512]{3,2,1,0:T(8,128)(2,1)S(1)} %copy-done.2), custom_call_target="tpu_custom_call" | custom-call | flops 1048576 | bytes 1048576 | tf_op jit(solution)/shard_map/filter_spectrum/pallas_call | solution.py:417
  177.8 24.5 %conv_of.1 = (f32[2,528,1024]{2,1,0:T(8,128)S(1)}, f32[128,1024]{1,0:T(8,128)S(1)}, f32[128,1024]{1,0:T(8,128)}, f32[128,1024]{1,0:T(8,128)}, f32[128,1024]{1,0:...) custom-call(s32[1]{0:T(128)} %bitcast.me, ...), custom_call_target="tpu_custom_call" | custom-call | flops 1048576 | bytes 1048576 | tf_op jit(solution)/shard_map/conv_of/pallas_call | solution.py:417
  207.2 23.7 %collective-permute-done.11.refs_4_ = f32[128,1024]{1,0:T(8,128)S(1)} collective-permute-done((f32[128,1024]{1,0:T(8,128)S(1)}, f32[128,1024]{1,0:T(8,128)S(1)}, u32[]{:S(2)}, u32[]{:S(2)}) %collective-permute-start.11) | collective-permute-done | bytes 524320 | tf_op jit(solution)/shard_map/grad_conv_4/ppermute | solution.py:513
  230.9 30.4 %term_of.1 = (f32[2,528,1024]{2,1,0:T(8,128)S(1)}, f32[8,4,32,1024]{3,2,1,0:T(8,128)S(1)}) custom-call(s32[1]{0:T(128)} %bitcast.me, f32[2,528,1024]{2,1,0:T(8,128)S(1)} %get-tuple-element.95.gated, f32[128,1024]{1,0:T(8,128)S(1)} %copy-done.21, f32[128,1024]{1,0:T(8,128)S(1)} %collective-permute-done.20.refs_1_, ...), custom_call_target="tpu_custom_call" | custom-call | flops 1048576 | bytes 1048576 | tf_op jit(solution)/shard_map/term_of/pallas_call | solution.py:417
  266.3 3.2 collective-permute-start.19
  271.4 2.4 copy-done.1
  273.7 2.6 copy-done.4
  276.4 2.6 copy-done.6
  279.0 2.4 copy-done.18
  281.4 13.6 %grad_of.1 = (f32[128,1024]{1,0:T(8,128)S(1)}, f32[128,1024]{1,0:T(8,128)S(1)}, f32[128,1024]{1,0:T(8,128)S(1)}, f32[128,1024]{1,0:T(8,128)S(1)}, f32[128,1024]{...) custom-call(s32[1]{0:T(128)} %bitcast.me, f32[2,528,1024]{2,1,0:T(8,128)S(1)} %copy-done.6, ...), custom_call_target="tpu_custom_call" | custom-call | flops 1048576 | bytes 1048576 | tf_op jit(solution)/shard_map/grad_of/pallas_call | solution.py:417
  299.8 3.5 collective-permute-done.19.refs_7_
  304.9 23.8 %collective-permute-done.17.refs_5_ = f32[128,1024]{1,0:T(8,128)S(1)} collective-permute-done((f32[128,1024]{1,0:T(8,128)}, f32[128,1024]{1,0:T(8,128)S(1)}, u32[]{:S(2)}, u32[]{:S(2)}) %collective-permute-start.17) | collective-permute-done | bytes 524320 | tf_op jit(solution)/shard_map/conv_3/ppermute | solution.py:513
  329.6 10.4 %collective-permute-done.12.refs_3_ = f32[128,1024]{1,0:T(8,128)S(1)} collective-permute-done((f32[128,1024]{1,0:T(8,128)}, f32[128,1024]{1,0:T(8,128)S(1)}, u32[]{:S(2)}, u32[]{:S(2)}) %collective-permute-start.12) | collective-permute-done | bytes 524320 | tf_op jit(solution)/shard_map/conv_2/ppermute | solution.py:513
  343.4 17.0 %collective-permute-start.25 = (f32[128,1024]{1,0:T(8,128)}, f32[128,1024]{1,0:T(8,128)S(1)}, u32[]{:S(2)}, u32[]{:S(2)}) collective-permute-start(f32[128,1024]{1,0:T(8,128)} %copy-done.63), channel_id=1, source_target_pairs={{0,4},{1,5},{2,6},{3,7},{4,0},{5,1},{6,2},{7,3},{8,12},{9,13},{10,... | collective-permute-start | bytes 1572872 | tf_op jit(solution)/shard_map/grad_gated_4/ppermute | solution.py:513
  360.4 21.5 %collective-permute-done.22.refs_3_ = f32[128,1024]{1,0:T(8,128)S(1)} collective-permute-done((f32[128,1024]{1,0:T(8,128)}, f32[128,1024]{1,0:T(8,128)S(1)}, u32[]{:S(2)}, u32[]{:S(2)}) %collective-permute-start.22) | collective-permute-done | bytes 524320 | tf_op jit(solution)/shard_map/grad_gated_5/ppermute | solution.py:513
  393.7 3.5 gate_out.3
  397.2 11.0 %collective-permute-done.29 = f32[1,32,1024]{2,1,0:T(8,128)S(1)} collective-permute-done((f32[1,32,1024]{2,1,0:T(8,128)S(1)}, f32[1,32,1024]{2,1,0:T(8,128)S(1)}, u32[]{:S(2)}, u32[]{:S(2)}) %collective-permute-start.29) | collective-permute-done | bytes 131104 | tf_op jit(solution)/shard_map/rows_sum/ppermute | solution.py:513
  410.8 2.6 collective-permute-start.30
  413.5 5.1 %collective-permute-done.27.refs_6_ = f32[128,1024]{1,0:T(8,128)} collective-permute-done((f32[128,1024]{1,0:T(8,128)}, f32[128,1024]{1,0:T(8,128)}, u32[]{:S(2)}, u32[]{:S(2)}) %collective-permute-start.27) | collective-permute-done | bytes 524320 | tf_op jit(solution)/shard_map/grad_gated_3/ppermute | solution.py:513
  426.4 3.6 gate_out.4
  (205 shorter events, 62.7 us)
Async XLA Ops:
  7.2 145.4 %all-gather.3.cloned.1.call-start = ((), (), s32[]{:S(2)}) async-start(), calls=%async_computation.2 | async-start | bytes 4718592 | tf_op jit(solution)/shard_map/all_gather | solution.py:645
  17.2 35.6 %collective-permute-start.6 = (f32[160,1024]{1,0:T(8,128)S(1)}, f32[160,1024]{1,0:T(8,128)S(1)}, u32[]{:S(2)}, u32[]{:S(2)}) collective-permute-start(f32[160,1024]{1,0:T(8,128)S(1)} %get-tuple-element.137), channel_id=1, source_target_pairs={{0,6},{1,7},{2,4},{3,5},{4,2},{5,3},{6,0},{7,1},{8,14},{9,15},{10,... | collective-permute-start | bytes 1966088 | tf_op jit(solution)/shard_map/gated_6/ppermute | solution.py:513
  17.2 37.1 %collective-permute-start.1 = (f32[160,1024]{1,0:T(8,128)S(1)}, f32[160,1024]{1,0:T(8,128)S(1)}, u32[]{:S(2)}, u32[]{:S(2)}) collective-permute-start(f32[160,1024]{1,0:T(8,128)S(1)} %get-tuple-element.139), channel_id=1, source_target_pairs={{0,2},{1,3},{2,0},{3,1},{4,6},{5,7},{6,4},{7,5},{8,10},{9,11},{10,... | collective-permute-start | bytes 1966088 | tf_op jit(solution)/shard_map/gated_2/ppermute | solution.py:513
  17.3 98.0 %collective-permute-start.5 = (f32[128,1024]{1,0:T(8,128)}, f32[128,1024]{1,0:T(8,128)S(1)}, u32[]{:S(2)}, u32[]{:S(2)}) collective-permute-start(f32[128,1024]{1,0:T(8,128)} %get-tuple-element.129), channel_id=1, source_target_pairs={{0,5},{1,4},{2,7},{3,6},{4,1},{5,0},{6,3},{7,2},{8,13},{9,12},{10,... | collective-permute-start | bytes 1572872 | tf_op jit(solution)/shard_map/gated_5/ppermute | solution.py:513
  21.1 94.3 %collective-permute-start.2 = (f32[128,1024]{1,0:T(8,128)}, f32[128,1024]{1,0:T(8,128)}, u32[]{:S(2)}, u32[]{:S(2)}) collective-permute-start(f32[128,1024]{1,0:T(8,128)} %get-tuple-element.131), channel_id=1, source_target_pairs={{0,3},{1,2},{2,1},{3,0},{4,7},{5,6},{6,5},{7,4},{8,11},{9,10},{10,... | collective-permute-start | bytes 1572872 | tf_op jit(solution)/shard_map/gated_3/ppermute | solution.py:513
  24.9 88.8 %collective-permute-start.4 = (f32[160,1024]{1,0:T(8,128)S(1)}, f32[160,1024]{1,0:T(8,128)S(1)}, u32[]{:S(2)}, u32[]{:S(2)}) collective-permute-start(f32[160,1024]{1,0:T(8,128)S(1)} %get-tuple-element.64), channel_id=1, source_target_pairs={{0,4},{1,5},{2,6},{3,7},{4,0},{5,1},{6,2},{7,3},{8,12},{9,13},{10,... | collective-permute-start | bytes 1966088 | tf_op jit(solution)/shard_map/gated_4/ppermute | solution.py:513
  52.8 62.6 %collective-permute-start = (f32[128,1024]{1,0:T(8,128)}, f32[128,1024]{1,0:T(8,128)S(1)}, u32[]{:S(2)}, u32[]{:S(2)}) collective-permute-start(f32[128,1024]{1,0:T(8,128)} %get-tuple-element.133), channel_id=1, source_target_pairs={{0,1},{1,0},{2,3},{3,2},{4,5},{5,4},{6,7},{7,6},{8,9},{9,8},{10,11... | collective-permute-start | bytes 1572872 | tf_op jit(solution)/shard_map/gated_1/ppermute | solution.py:513
  116.3 225.3 %reduce-scatter.2.cloned.1.call-start = ((), (), s32[]{:S(2)}) async-start(), calls=%async_computation.1 | async-start | bytes 4718592 | tf_op jit(solution)/shard_map/reduce_scatter | solution.py:660
  116.3 59.2 %collective-permute-start.7 = (f32[128,1024]{1,0:T(8,128)}, f32[128,1024]{1,0:T(8,128)}, u32[]{:S(2)}, u32[]{:S(2)}) collective-permute-start(f32[128,1024]{1,0:T(8,128)} %get-tuple-element.66), channel_id=1, source_target_pairs={{0,7},{1,6},{2,5},{3,4},{4,3},{5,2},{6,1},{7,0},{8,15},{9,14},{10,... | collective-permute-start | bytes 1572872 | tf_op jit(solution)/shard_map/grad_conv_7/ppermute | solution.py:513
  119.0 84.2 %collective-permute-start.9 = (f32[128,1024]{1,0:T(8,128)}, f32[128,1024]{1,0:T(8,128)}, u32[]{:S(2)}, u32[]{:S(2)}) collective-permute-start(f32[128,1024]{1,0:T(8,128)} %get-tuple-element.78), channel_id=1, source_target_pairs={{0,6},{1,7},{2,4},{3,5},{4,2},{5,3},{6,0},{7,1},{8,14},{9,15},{10,... | collective-permute-start | bytes 1572872 | tf_op jit(solution)/shard_map/grad_conv_6/ppermute | solution.py:513
  120.1 83.6 %collective-permute-start.13 = (f32[128,1024]{1,0:T(8,128)}, f32[128,1024]{1,0:T(8,128)}, u32[]{:S(2)}, u32[]{:S(2)}) collective-permute-start(f32[128,1024]{1,0:T(8,128)} %get-tuple-element.84), channel_id=1, source_target_pairs={{0,5},{1,4},{2,7},{3,6},{4,1},{5,0},{6,3},{7,2},{8,13},{9,12},{10,... | collective-permute-start | bytes 1572872 | tf_op jit(solution)/shard_map/grad_conv_5/ppermute | solution.py:513
  120.1 85.5 %collective-permute-start.14 = (f32[128,1024]{1,0:T(8,128)}, f32[128,1024]{1,0:T(8,128)}, u32[]{:S(2)}, u32[]{:S(2)}) collective-permute-start(f32[128,1024]{1,0:T(8,128)} %get-tuple-element.85), channel_id=1, source_target_pairs={{0,2},{1,3},{2,0},{3,1},{4,6},{5,7},{6,4},{7,5},{8,10},{9,11},{10,... | collective-permute-start | bytes 1572872 | tf_op jit(solution)/shard_map/grad_conv_2/ppermute | solution.py:513
  122.8 84.4 %collective-permute-start.15 = (f32[128,1024]{1,0:T(8,128)}, f32[128,1024]{1,0:T(8,128)}, u32[]{:S(2)}, u32[]{:S(2)}) collective-permute-start(f32[128,1024]{1,0:T(8,128)} %get-tuple-element.86), channel_id=1, source_target_pairs={{0,3},{1,2},{2,1},{3,0},{4,7},{5,6},{6,5},{7,4},{8,11},{9,10},{10,... | collective-permute-start | bytes 1572872 | tf_op jit(solution)/shard_map/grad_conv_3/ppermute | solution.py:513
  175.5 55.4 %collective-permute-start.11 = (f32[128,1024]{1,0:T(8,128)S(1)}, f32[128,1024]{1,0:T(8,128)S(1)}, u32[]{:S(2)}, u32[]{:S(2)}) collective-permute-start(f32[128,1024]{1,0:T(8,128)S(1)} %copy-done.66), channel_id=1, source_target_pairs={{0,4},{1,5},{2,6},{3,7},{4,0},{5,1},{6,2},{7,3},{8,12},{9,13},{10,... | collective-permute-start | bytes 1572872 | tf_op jit(solution)/shard_map/grad_conv_4/ppermute | solution.py:513
  203.2 27.7 %collective-permute-start.20 = (f32[128,1024]{1,0:T(8,128)S(1)}, f32[128,1024]{1,0:T(8,128)S(1)}, u32[]{:S(2)}, u32[]{:S(2)}) collective-permute-start(f32[128,1024]{1,0:T(8,128)S(1)} %copy-done.65), channel_id=1, source_target_pairs={{0,1},{1,0},{2,3},{3,2},{4,5},{5,4},{6,7},{7,6},{8,9},{9,8},{10,11... | collective-permute-start | bytes 1572872 | tf_op jit(solution)/shard_map/grad_conv_1/ppermute | solution.py:513
  203.7 61.7 %collective-permute-start.10 = (f32[128,1024]{1,0:T(8,128)S(1)}, f32[128,1024]{1,0:T(8,128)S(1)}, u32[]{:S(2)}, u32[]{:S(2)}) collective-permute-start(f32[128,1024]{1,0:T(8,128)S(1)} %get-tuple-element.80), channel_id=1, source_target_pairs={{0,6},{1,7},{2,4},{3,5},{4,2},{5,3},{6,0},{7,1},{8,14},{9,15},{10,... | collective-permute-start | bytes 1572872 | tf_op jit(solution)/shard_map/conv_6/ppermute | solution.py:513
  205.6 59.8 %collective-permute-start.8 = (f32[128,1024]{1,0:T(8,128)S(1)}, f32[128,1024]{1,0:T(8,128)S(1)}, u32[]{:S(2)}, u32[]{:S(2)}) collective-permute-start(f32[128,1024]{1,0:T(8,128)S(1)} %get-tuple-element.77), channel_id=1, source_target_pairs={{0,7},{1,6},{2,5},{3,4},{4,3},{5,2},{6,1},{7,0},{8,15},{9,14},{10,... | collective-permute-start | bytes 1572872 | tf_op jit(solution)/shard_map/conv_7/ppermute | solution.py:513
  266.2 32.8 %collective-permute-start.16 = (f32[128,1024]{1,0:T(8,128)}, f32[128,1024]{1,0:T(8,128)S(1)}, u32[]{:S(2)}, u32[]{:S(2)}) collective-permute-start(f32[128,1024]{1,0:T(8,128)} %get-tuple-element.88), channel_id=1, source_target_pairs={{0,5},{1,4},{2,7},{3,6},{4,1},{5,0},{6,3},{7,2},{8,13},{9,12},{10,... | collective-permute-start | bytes 1572872 | tf_op jit(solution)/shard_map/conv_5/ppermute | solution.py:513
  266.3 37.0 %collective-permute-start.19 = (f32[128,1024]{1,0:T(8,128)}, f32[128,1024]{1,0:T(8,128)S(1)}, u32[]{:S(2)}, u32[]{:S(2)}) collective-permute-start(f32[128,1024]{1,0:T(8,128)} %get-tuple-element.94), channel_id=1, source_target_pairs={{0,4},{1,5},{2,6},{3,7},{4,0},{5,1},{6,2},{7,3},{8,12},{9,13},{10,... | collective-permute-start | bytes 1572872 | tf_op jit(solution)/shard_map/conv_4/ppermute | solution.py:513
  269.5 34.6 %collective-permute-start.18 = (f32[128,1024]{1,0:T(8,128)}, f32[128,1024]{1,0:T(8,128)S(1)}, u32[]{:S(2)}, u32[]{:S(2)}) collective-permute-start(f32[128,1024]{1,0:T(8,128)} %get-tuple-element.92), channel_id=1, source_target_pairs={{0,1},{1,0},{2,3},{3,2},{4,5},{5,4},{6,7},{7,6},{8,9},{9,8},{10,11... | collective-permute-start | bytes 1572872 | tf_op jit(solution)/shard_map/conv_1/ppermute | solution.py:513
  269.5 59.3 %collective-permute-start.17 = (f32[128,1024]{1,0:T(8,128)}, f32[128,1024]{1,0:T(8,128)S(1)}, u32[]{:S(2)}, u32[]{:S(2)}) collective-permute-start(f32[128,1024]{1,0:T(8,128)} %get-tuple-element.90), channel_id=1, source_target_pairs={{0,3},{1,2},{2,1},{3,0},{4,7},{5,6},{6,5},{7,4},{8,11},{9,10},{10,... | collective-permute-start | bytes 1572872 | tf_op jit(solution)/shard_map/conv_3/ppermute | solution.py:513
  269.5 70.4 %collective-permute-start.12 = (f32[128,1024]{1,0:T(8,128)}, f32[128,1024]{1,0:T(8,128)S(1)}, u32[]{:S(2)}, u32[]{:S(2)}) collective-permute-start(f32[128,1024]{1,0:T(8,128)} %get-tuple-element.83), channel_id=1, source_target_pairs={{0,2},{1,3},{2,0},{3,1},{4,6},{5,7},{6,4},{7,5},{8,10},{9,11},{10,... | collective-permute-start | bytes 1572872 | tf_op jit(solution)/shard_map/conv_2/ppermute | solution.py:513
  299.8 40.9 %collective-permute-start.21 = (f32[128,1024]{1,0:T(8,128)S(1)}, f32[128,1024]{1,0:T(8,128)S(1)}, u32[]{:S(2)}, u32[]{:S(2)}) collective-permute-start(f32[128,1024]{1,0:T(8,128)S(1)} %get-tuple-element.99), channel_id=1, source_target_pairs={{0,7},{1,6},{2,5},{3,4},{4,3},{5,2},{6,1},{7,0},{8,15},{9,14},{10,... | collective-permute-start | bytes 1572872 | tf_op jit(solution)/shard_map/grad_gated_7/ppermute | solution.py:513
  304.1 38.5 %collective-permute-start.24 = (f32[128,1024]{1,0:T(8,128)}, f32[128,1024]{1,0:T(8,128)S(1)}, u32[]{:S(2)}, u32[]{:S(2)}) collective-permute-start(f32[128,1024]{1,0:T(8,128)} %get-tuple-element.106), channel_id=1, source_target_pairs={{0,6},{1,7},{2,4},{3,5},{4,2},{5,3},{6,0},{7,1},{8,14},{9,15},{10,... | collective-permute-start | bytes 1572872 | tf_op jit(solution)/shard_map/grad_gated_6/ppermute | solution.py:513
  341.5 40.5 %collective-permute-start.22 = (f32[128,1024]{1,0:T(8,128)}, f32[128,1024]{1,0:T(8,128)S(1)}, u32[]{:S(2)}, u32[]{:S(2)}) collective-permute-start(f32[128,1024]{1,0:T(8,128)} %get-tuple-element.101), channel_id=1, source_target_pairs={{0,5},{1,4},{2,7},{3,6},{4,1},{5,0},{6,3},{7,2},{8,13},{9,12},{10,... | collective-permute-start | bytes 1572872 | tf_op jit(solution)/shard_map/grad_gated_5/ppermute | solution.py:513
  342.5 42.3 %collective-permute-start.28 = (f32[2,32,1024]{2,1,0:T(8,128)S(1)}, f32[2,32,1024]{2,1,0:T(8,128)S(1)}, u32[]{:S(2)}, u32[]{:S(2)}) collective-permute-start(f32[2,32,1024]{2,1,0:T(8,128)S(1)} %pad_maximum_fusion.5), channel_id=1, source_target_pairs={{0,2},{2,0},{4,6},{6,4},{1,3},{3,1},{5,7},{7,5},{8,10},{10,8},{12,... | collective-permute-start | bytes 786440 | tf_op jit(solution)/shard_map/rows_sum/ppermute | solution.py:513
  343.4 65.8 %collective-permute-start.25 = (f32[128,1024]{1,0:T(8,128)}, f32[128,1024]{1,0:T(8,128)S(1)}, u32[]{:S(2)}, u32[]{:S(2)}) collective-permute-start(f32[128,1024]{1,0:T(8,128)} %copy-done.63), channel_id=1, source_target_pairs={{0,4},{1,5},{2,6},{3,7},{4,0},{5,1},{6,2},{7,3},{8,12},{9,13},{10,... | collective-permute-start | bytes 1572872 | tf_op jit(solution)/shard_map/grad_gated_4/ppermute | solution.py:513
  382.8 47.2 %collective-permute-start.23 = (f32[128,1024]{1,0:T(8,128)}, f32[128,1024]{1,0:T(8,128)}, u32[]{:S(2)}, u32[]{:S(2)}) collective-permute-start(f32[128,1024]{1,0:T(8,128)} %copy-done.60), channel_id=1, source_target_pairs={{0,2},{1,3},{2,0},{3,1},{4,6},{5,7},{6,4},{7,5},{8,10},{9,11},{10,... | collective-permute-start | bytes 1572872 | tf_op jit(solution)/shard_map/grad_gated_2/ppermute | solution.py:513
  382.8 27.3 %collective-permute-start.26 = (f32[128,1024]{1,0:T(8,128)}, f32[128,1024]{1,0:T(8,128)S(1)}, u32[]{:S(2)}, u32[]{:S(2)}) collective-permute-start(f32[128,1024]{1,0:T(8,128)} %copy-done.62), channel_id=1, source_target_pairs={{0,1},{1,0},{2,3},{3,2},{4,5},{5,4},{6,7},{7,6},{8,9},{9,8},{10,11... | collective-permute-start | bytes 1572872 | tf_op jit(solution)/shard_map/grad_gated_1/ppermute | solution.py:513
  383.2 35.3 %collective-permute-start.27 = (f32[128,1024]{1,0:T(8,128)}, f32[128,1024]{1,0:T(8,128)}, u32[]{:S(2)}, u32[]{:S(2)}) collective-permute-start(f32[128,1024]{1,0:T(8,128)} %copy-done.61), channel_id=1, source_target_pairs={{0,3},{1,2},{2,1},{3,0},{4,7},{5,6},{6,5},{7,4},{8,11},{9,10},{10,... | collective-permute-start | bytes 1572872 | tf_op jit(solution)/shard_map/grad_gated_3/ppermute | solution.py:513
  385.8 22.4 %collective-permute-start.29 = (f32[1,32,1024]{2,1,0:T(8,128)S(1)}, f32[1,32,1024]{2,1,0:T(8,128)S(1)}, u32[]{:S(2)}, u32[]{:S(2)}) collective-permute-start(f32[1,32,1024]{2,1,0:T(8,128)S(1)} %slice_add_fusion), channel_id=1, source_target_pairs={{0,4},{2,6},{4,0},{6,2},{1,5},{3,7},{5,1},{7,3},{8,12},{10,14},{12... | collective-permute-start | bytes 393224 | tf_op jit(solution)/shard_map/rows_sum/ppermute | solution.py:513
  409.2 22.8 %collective-permute-start.32 = (f32[32,1024]{1,0:T(8,128)S(1)}, f32[32,1024]{1,0:T(8,128)S(1)}, u32[]{:S(2)}, u32[]{:S(2)}) collective-permute-start(f32[32,1024]{1,0:T(8,128)S(1)} %fusion.3), channel_id=1, source_target_pairs={{0,24},{8,16},{16,8},{24,0},{1,25},{9,17},{17,9},{25,1},{2,26},{10... | collective-permute-start | bytes 393224 | tf_op jit(solution)/shard_map/parts_gather/ppermute | solution.py:513
  (72 other events, 847.9 us)
Sparse Core Ops, SparseCore 0:
  116.4 36.1 all-gather.2
  266.4 48.8 reduce-scatter.1

commit v6 on v5

--- a/solution.py
+++ b/solution.py
@@ -654,19 +654,13 @@
     tile_shape = (parts * cols, rows, height, side)
     cot, term = term_of(plan, me, spec, grad_conv, by_block, tile_shape, by_tile)
     back_out = grad_of(plan, me, filt, cot, owners, by_block)
-    grad_gated = exchange(back_out, "grad_gated", last_order, 2, 3)
+    grad_gated = exchange(back_out, "grad_gated", last_order, 3, 2)
 
     term = after([conv[step] for step in far[:2]], term)
     term = lax.psum_scatter(term, ("dp", "col"), scatter_dimension=0, tiled=False)
     with jax.named_scope("rows_sum"):
-        term = [term[i] for i in range(rows)]
-        bit = 1
-        while bit < rows:
-            arrived = pairwise(jnp.stack(term[bit::2 * bit]), "row", bit)
-            for j, i in enumerate(range(0, rows, 2 * bit)):
-                term[i] = term[i] + arrived[j]
-            bit *= 2
-    total = term[0] * (1.0 / side)
+        arrived = [pairwise(term[i], "row", i) for i in range(1, rows)]
+    total = sum(arrived, term[0]) * (1.0 / side)
     every = [0] + order
     (grad_outer,) = gated_by(me, every, [conv[step] for step in every], [grad_out[0]])
     total = after(grad_outer, total)

time: 441 us -> 431 us (0.977)
  waiting for transfers between devices: 190 us -> 161 us
  starting transfers between devices: 74.1 us -> 94.3 us
  local copies, waits for them, and re-layouts: 55.7 us -> 51.2 us
    ppermute x33 -> x34, waiting for transfers between devices: 160 us -> 121 us  [pairwise(): lax.ppermute(block, axis, [(i, i ^ step) for i in range(lax.axis_size(axi...]
    ppermute x33 -> x34, starting transfers between devices: 74 us -> 94.2 us  [pairwise(): lax.ppermute(block, axis, [(i, i ^ step) for i in range(lax.axis_size(axi...]
    reduce_scatter x1, waiting for transfers between devices: 0.01 us -> 9.98 us  [channel_shards(): lax.psum_scatter(term, ('dp', 'col'), scatter_dimension=0, tiled=False)]
    unnamed x138 -> x128, local copies, waits for them, and re-layouts: 54.6 us -> 50 us
  transfers between devices with their start and end apart: 35 -> 36, of which waited for: 10 -> 10; matrix products, arithmetic and copies ran while one was open for 3% -> 3% of each run, Pallas kernels for 21% -> 22%
where the time goes in v6:
time: 431 us; the launch traced here: 426 us
  waiting for transfers between devices  161 us (37%)
  starting transfers between devices  94.3 us (22%)
  Pallas kernels  92.8 us (22%)
  local copies, waits for them, and re-layouts  51.2 us (12%)
  between operations  14.6 us (3%)
  other arithmetic  11.9 us (3%)
    ppermute x34, waiting for transfers between devices, pairwise(): lax.ppermute(block, axis, [(i, i ^ step) for i in range(lax.axis_size(axi...  121 us
    ppermute x34, starting transfers between devices, pairwise(): lax.ppermute(block, axis, [(i, i ^ step) for i in range(lax.axis_size(axi...  94.2 us
    pallas_call x4, Pallas kernels, call_kernel(): pl.pallas_call(kernel, out_shape=out_shape, in_specs=in_specs, out_specs=...  83.5 us
    unnamed x128, local copies, waits for them, and re-layouts  50 us
    all_gather x1, waiting for transfers between devices, channel_shards(): over_all = [lax.all_gather(over_row, ('dp', 'col'))]  29.7 us
    reduce_scatter x1, waiting for transfers between devices, channel_shards(): lax.psum_scatter(term, ('dp', 'col'), scatter_dimension=0, tiled=False)  9.98 us
    pallas_call x3, Pallas kernels, gated_by(): pl.pallas_call(functools.partial(gate_kernel, steps, len(gates)), grid_sp...  9.33 us
  transfers between devices with their start and end apart: 36, of which 10 were waited for; matrix products, arithmetic and copies ran while one was open for 3% of the time, Pallas kernels for 22%

profile of v6, /device:TPU:7, one launch (start us, length us, event | category | flops | bytes accessed | tf_op | source)
XLA Modules:
  0.0 425.5 jit_solution(4642833155607393579)
XLA Ops:
  8.3 3.9 collective-permute-start.3
  13.2 3.8 multiply_bitcast_fusion.8
  17.3 3.7 collective-permute-start.5
  22.0 2.9 collective-permute-done.3.refs_7_
  24.9 25.6 %collective-permute-start.4 = (f32[160,1024]{1,0:T(8,128)S(1)}, f32[160,1024]{1,0:T(8,128)S(1)}, u32[]{:S(2)}, u32[]{:S(2)}) collective-permute-start(f32[160,1024]{1,0:T(8,128)S(1)} %get-tuple-element.64), channel_id=1, source_target_pairs={{0,4},{1,5},{2,6},{3,7},{4,0},{5,1},{6,2},{7,3},{8,12},{9,13},{10,... | collective-permute-start | bytes 1966088 | tf_op jit(solution)/shard_map/gated_4/ppermute | solution.py:513
  50.5 2.2 multiply_bitcast_fusion
  55.2 58.5 %collective-permute-done.4.refs_4_ = f32[160,1024]{1,0:T(8,128)S(1)} collective-permute-done((f32[160,1024]{1,0:T(8,128)S(1)}, f32[160,1024]{1,0:T(8,128)S(1)}, u32[]{:S(2)}, u32[]{:S(2)}) %collective-permute-start.4) | collective-permute-done | bytes 655392 | tf_op jit(solution)/shard_map/gated_4/ppermute | solution.py:513
  116.3 2.7 collective-permute-start.7
  120.0 2.7 collective-permute-start.14
  122.8 29.7 %all-gather.3.cloned.1.call-done = f32[32,32,1024]{2,1,0:T(8,128)} async-done(((f32[4,32,1024]{2,1,0:T(8,128)}), f32[32,32,1024]{2,1,0:T(8,128)}) %all-gather.3.cloned.1.call-update) | async-done | bytes 4194320 | tf_op jit(solution)/shard_map/all_gather | solution.py:645
  152.5 2.2 copy-done
  160.5 15.0 %filter_spectrum.1.filt = f32[2,528,1024]{2,1,0:T(8,128)S(1)} custom-call(s32[1]{0:T(128)} %bitcast.me, f32[8,4,32,1024]{3,2,1,0:T(8,128)S(1)} %bitcast.87, bf16[2,544,512]{2,1,0:T(8,128)(2,1)S(1)} %copy-done.11, bf16[2,512,512]{2,1,0:T(8,128)(2,1)S(1)} %copy-done.14, f32[2,528,1024]{2,1,0:T(8,128)S(1)} %copy-done, bf16[2,4,512,512]{3,2,1,0:T(8,128)(2,1)S(1)} %copy-done.2), custom_call_target="tpu_custom_call" | custom-call | flops 1048576 | bytes 1048576 | tf_op jit(solution)/shard_map/filter_spectrum/pallas_call | solution.py:417
  177.8 24.5 %conv_of.1 = (f32[2,528,1024]{2,1,0:T(8,128)S(1)}, f32[128,1024]{1,0:T(8,128)S(1)}, f32[128,1024]{1,0:T(8,128)}, f32[128,1024]{1,0:T(8,128)}, f32[128,1024]{1,0:...) custom-call(s32[1]{0:T(128)} %bitcast.me, ...), custom_call_target="tpu_custom_call" | custom-call | flops 1048576 | bytes 1048576 | tf_op jit(solution)/shard_map/conv_of/pallas_call | solution.py:417
  207.2 23.6 %collective-permute-done.11.refs_4_ = f32[128,1024]{1,0:T(8,128)S(1)} collective-permute-done((f32[128,1024]{1,0:T(8,128)S(1)}, f32[128,1024]{1,0:T(8,128)S(1)}, u32[]{:S(2)}, u32[]{:S(2)}) %collective-permute-start.11) | collective-permute-done | bytes 524320 | tf_op jit(solution)/shard_map/grad_conv_4/ppermute | solution.py:513
  230.9 30.4 %term_of.1 = (f32[2,528,1024]{2,1,0:T(8,128)S(1)}, f32[8,4,32,1024]{3,2,1,0:T(8,128)S(1)}) custom-call(s32[1]{0:T(128)} %bitcast.me, f32[2,528,1024]{2,1,0:T(8,128)S(1)} %get-tuple-element.95.gated, f32[128,1024]{1,0:T(8,128)S(1)} %copy-done.21, f32[128,1024]{1,0:T(8,128)S(1)} %collective-permute-done.20.refs_1_, ...), custom_call_target="tpu_custom_call" | custom-call | flops 1048576 | bytes 1048576 | tf_op jit(solution)/shard_map/term_of/pallas_call | solution.py:417
  266.3 3.2 collective-permute-start.19
  271.4 2.4 copy-done.1
  273.7 2.6 copy-done.4
  276.4 2.6 copy-done.6
  279.0 2.4 copy-done.18
  281.4 13.6 %grad_of.1 = (f32[128,1024]{1,0:T(8,128)S(1)}, f32[128,1024]{1,0:T(8,128)S(1)}, f32[128,1024]{1,0:T(8,128)S(1)}, f32[128,1024]{1,0:T(8,128)S(1)}, f32[128,1024]{...) custom-call(s32[1]{0:T(128)} %bitcast.me, f32[2,528,1024]{2,1,0:T(8,128)S(1)} %copy-done.6, ...), custom_call_target="tpu_custom_call" | custom-call | flops 1048576 | bytes 1048576 | tf_op jit(solution)/shard_map/grad_of/pallas_call | solution.py:417
  300.7 2.6 collective-permute-done.19.refs_7_
  305.2 10.0 %reduce-scatter.2.cloned.1.call-done = f32[1,4,32,1024]{3,2,1,0:T(8,128)} async-done(((f32[8,4,32,1024]{3,2,1,0:T(8,128)}), f32[1,4,32,1024]{3,2,1,0:T(8,128)}) %reduce-scatter.2.cloned.1.call-update) | async-done | bytes 524304 | tf_op jit(solution)/shard_map/reduce_scatter | solution.py:660
  317.5 11.3 %collective-permute-done.17.refs_5_ = f32[128,1024]{1,0:T(8,128)} collective-permute-done((f32[128,1024]{1,0:T(8,128)}, f32[128,1024]{1,0:T(8,128)}, u32[]{:S(2)}, u32[]{:S(2)}) %collective-permute-start.17) | collective-permute-done | bytes 524320 | tf_op jit(solution)/shard_map/conv_3/ppermute | solution.py:513
  328.9 11.2 %collective-permute-done.12.refs_3_ = f32[128,1024]{1,0:T(8,128)} collective-permute-done((f32[128,1024]{1,0:T(8,128)}, f32[128,1024]{1,0:T(8,128)}, u32[]{:S(2)}, u32[]{:S(2)}) %collective-permute-start.12) | collective-permute-done | bytes 524320 | tf_op jit(solution)/shard_map/conv_2/ppermute | solution.py:513
  344.7 22.5 %collective-permute-start.27 = (f32[128,1024]{1,0:T(8,128)}, f32[128,1024]{1,0:T(8,128)S(1)}, u32[]{:S(2)}, u32[]{:S(2)}) collective-permute-start(f32[128,1024]{1,0:T(8,128)} %copy-done.56), channel_id=1, source_target_pairs={{0,3},{1,2},{2,1},{3,0},{4,7},{5,6},{6,5},{7,4},{8,11},{9,10},{10,... | collective-permute-start | bytes 1572872 | tf_op jit(solution)/shard_map/grad_gated_3/ppermute | solution.py:513
  367.1 11.6 %collective-permute-start.25 = (f32[128,1024]{1,0:T(8,128)}, f32[128,1024]{1,0:T(8,128)}, u32[]{:S(2)}, u32[]{:S(2)}) collective-permute-start(f32[128,1024]{1,0:T(8,128)} %copy-done.55), channel_id=1, source_target_pairs={{0,4},{1,5},{2,6},{3,7},{4,0},{5,1},{6,2},{7,3},{8,12},{9,13},{10,... | collective-permute-start | bytes 1572872 | tf_op jit(solution)/shard_map/grad_gated_4/ppermute | solution.py:513
  378.7 2.8 collective-permute-done.29
  386.3 3.8 gate_out.3
  393.5 2.6 collective-permute-start.31
  396.1 8.1 %collective-permute-done.25.refs_4_ = f32[128,1024]{1,0:T(8,128)} collective-permute-done((f32[128,1024]{1,0:T(8,128)}, f32[128,1024]{1,0:T(8,128)}, u32[]{:S(2)}, u32[]{:S(2)}) %collective-permute-start.25) | collective-permute-done | bytes 524320 | tf_op jit(solution)/shard_map/grad_gated_4/ppermute | solution.py:513
  412.0 3.6 gate_out.4
  (195 shorter events, 62.6 us)
Async XLA Ops:
  7.2 145.4 %all-gather.3.cloned.1.call-start = ((), (), s32[]{:S(2)}) async-start(), calls=%async_computation.2 | async-start | bytes 4718592 | tf_op jit(solution)/shard_map/all_gather | solution.py:645
  17.2 35.6 %collective-permute-start.6 = (f32[160,1024]{1,0:T(8,128)S(1)}, f32[160,1024]{1,0:T(8,128)S(1)}, u32[]{:S(2)}, u32[]{:S(2)}) collective-permute-start(f32[160,1024]{1,0:T(8,128)S(1)} %get-tuple-element.138), channel_id=1, source_target_pairs={{0,6},{1,7},{2,4},{3,5},{4,2},{5,3},{6,0},{7,1},{8,14},{9,15},{10,... | collective-permute-start | bytes 1966088 | tf_op jit(solution)/shard_map/gated_6/ppermute | solution.py:513
  17.2 37.1 %collective-permute-start.1 = (f32[160,1024]{1,0:T(8,128)S(1)}, f32[160,1024]{1,0:T(8,128)S(1)}, u32[]{:S(2)}, u32[]{:S(2)}) collective-permute-start(f32[160,1024]{1,0:T(8,128)S(1)} %get-tuple-element.140), channel_id=1, source_target_pairs={{0,2},{1,3},{2,0},{3,1},{4,6},{5,7},{6,4},{7,5},{8,10},{9,11},{10,... | collective-permute-start | bytes 1966088 | tf_op jit(solution)/shard_map/gated_2/ppermute | solution.py:513
  17.3 98.0 %collective-permute-start.5 = (f32[128,1024]{1,0:T(8,128)}, f32[128,1024]{1,0:T(8,128)S(1)}, u32[]{:S(2)}, u32[]{:S(2)}) collective-permute-start(f32[128,1024]{1,0:T(8,128)} %get-tuple-element.129), channel_id=1, source_target_pairs={{0,5},{1,4},{2,7},{3,6},{4,1},{5,0},{6,3},{7,2},{8,13},{9,12},{10,... | collective-permute-start | bytes 1572872 | tf_op jit(solution)/shard_map/gated_5/ppermute | solution.py:513
  21.1 94.3 %collective-permute-start.2 = (f32[128,1024]{1,0:T(8,128)}, f32[128,1024]{1,0:T(8,128)}, u32[]{:S(2)}, u32[]{:S(2)}) collective-permute-start(f32[128,1024]{1,0:T(8,128)} %get-tuple-element.131), channel_id=1, source_target_pairs={{0,3},{1,2},{2,1},{3,0},{4,7},{5,6},{6,5},{7,4},{8,11},{9,10},{10,... | collective-permute-start | bytes 1572872 | tf_op jit(solution)/shard_map/gated_3/ppermute | solution.py:513
  24.9 88.8 %collective-permute-start.4 = (f32[160,1024]{1,0:T(8,128)S(1)}, f32[160,1024]{1,0:T(8,128)S(1)}, u32[]{:S(2)}, u32[]{:S(2)}) collective-permute-start(f32[160,1024]{1,0:T(8,128)S(1)} %get-tuple-element.64), channel_id=1, source_target_pairs={{0,4},{1,5},{2,6},{3,7},{4,0},{5,1},{6,2},{7,3},{8,12},{9,13},{10,... | collective-permute-start | bytes 1966088 | tf_op jit(solution)/shard_map/gated_4/ppermute | solution.py:513
  52.8 62.6 %collective-permute-start = (f32[128,1024]{1,0:T(8,128)}, f32[128,1024]{1,0:T(8,128)S(1)}, u32[]{:S(2)}, u32[]{:S(2)}) collective-permute-start(f32[128,1024]{1,0:T(8,128)} %get-tuple-element.133), channel_id=1, source_target_pairs={{0,1},{1,0},{2,3},{3,2},{4,5},{5,4},{6,7},{7,6},{8,9},{9,8},{10,11... | collective-permute-start | bytes 1572872 | tf_op jit(solution)/shard_map/gated_1/ppermute | solution.py:513
  116.2 199.0 %reduce-scatter.2.cloned.1.call-start = ((), (), s32[]{:S(2)}) async-start(), calls=%async_computation.1 | async-start | bytes 4718592 | tf_op jit(solution)/shard_map/reduce_scatter | solution.py:660
  116.3 59.2 %collective-permute-start.7 = (f32[128,1024]{1,0:T(8,128)}, f32[128,1024]{1,0:T(8,128)}, u32[]{:S(2)}, u32[]{:S(2)}) collective-permute-start(f32[128,1024]{1,0:T(8,128)} %get-tuple-element.66), channel_id=1, source_target_pairs={{0,7},{1,6},{2,5},{3,4},{4,3},{5,2},{6,1},{7,0},{8,15},{9,14},{10,... | collective-permute-start | bytes 1572872 | tf_op jit(solution)/shard_map/grad_conv_7/ppermute | solution.py:513
  119.0 84.2 %collective-permute-start.9 = (f32[128,1024]{1,0:T(8,128)}, f32[128,1024]{1,0:T(8,128)}, u32[]{:S(2)}, u32[]{:S(2)}) collective-permute-start(f32[128,1024]{1,0:T(8,128)} %get-tuple-element.78), channel_id=1, source_target_pairs={{0,6},{1,7},{2,4},{3,5},{4,2},{5,3},{6,0},{7,1},{8,14},{9,15},{10,... | collective-permute-start | bytes 1572872 | tf_op jit(solution)/shard_map/grad_conv_6/ppermute | solution.py:513
  120.0 83.7 %collective-permute-start.13 = (f32[128,1024]{1,0:T(8,128)}, f32[128,1024]{1,0:T(8,128)}, u32[]{:S(2)}, u32[]{:S(2)}) collective-permute-start(f32[128,1024]{1,0:T(8,128)} %get-tuple-element.84), channel_id=1, source_target_pairs={{0,5},{1,4},{2,7},{3,6},{4,1},{5,0},{6,3},{7,2},{8,13},{9,12},{10,... | collective-permute-start | bytes 1572872 | tf_op jit(solution)/shard_map/grad_conv_5/ppermute | solution.py:513
  120.0 85.6 %collective-permute-start.14 = (f32[128,1024]{1,0:T(8,128)}, f32[128,1024]{1,0:T(8,128)}, u32[]{:S(2)}, u32[]{:S(2)}) collective-permute-start(f32[128,1024]{1,0:T(8,128)} %get-tuple-element.85), channel_id=1, source_target_pairs={{0,2},{1,3},{2,0},{3,1},{4,6},{5,7},{6,4},{7,5},{8,10},{9,11},{10,... | collective-permute-start | bytes 1572872 | tf_op jit(solution)/shard_map/grad_conv_2/ppermute | solution.py:513
  122.8 84.5 %collective-permute-start.15 = (f32[128,1024]{1,0:T(8,128)}, f32[128,1024]{1,0:T(8,128)}, u32[]{:S(2)}, u32[]{:S(2)}) collective-permute-start(f32[128,1024]{1,0:T(8,128)} %get-tuple-element.86), channel_id=1, source_target_pairs={{0,3},{1,2},{2,1},{3,0},{4,7},{5,6},{6,5},{7,4},{8,11},{9,10},{10,... | collective-permute-start | bytes 1572872 | tf_op jit(solution)/shard_map/grad_conv_3/ppermute | solution.py:513
  175.5 55.4 %collective-permute-start.11 = (f32[128,1024]{1,0:T(8,128)S(1)}, f32[128,1024]{1,0:T(8,128)S(1)}, u32[]{:S(2)}, u32[]{:S(2)}) collective-permute-start(f32[128,1024]{1,0:T(8,128)S(1)} %copy-done.61), channel_id=1, source_target_pairs={{0,4},{1,5},{2,6},{3,7},{4,0},{5,1},{6,2},{7,3},{8,12},{9,13},{10,... | collective-permute-start | bytes 1572872 | tf_op jit(solution)/shard_map/grad_conv_4/ppermute | solution.py:513
  203.2 27.7 %collective-permute-start.20 = (f32[128,1024]{1,0:T(8,128)S(1)}, f32[128,1024]{1,0:T(8,128)S(1)}, u32[]{:S(2)}, u32[]{:S(2)}) collective-permute-start(f32[128,1024]{1,0:T(8,128)S(1)} %copy-done.60), channel_id=1, source_target_pairs={{0,1},{1,0},{2,3},{3,2},{4,5},{5,4},{6,7},{7,6},{8,9},{9,8},{10,11... | collective-permute-start | bytes 1572872 | tf_op jit(solution)/shard_map/grad_conv_1/ppermute | solution.py:513
  203.7 61.7 %collective-permute-start.10 = (f32[128,1024]{1,0:T(8,128)S(1)}, f32[128,1024]{1,0:T(8,128)S(1)}, u32[]{:S(2)}, u32[]{:S(2)}) collective-permute-start(f32[128,1024]{1,0:T(8,128)S(1)} %get-tuple-element.80), channel_id=1, source_target_pairs={{0,6},{1,7},{2,4},{3,5},{4,2},{5,3},{6,0},{7,1},{8,14},{9,15},{10,... | collective-permute-start | bytes 1572872 | tf_op jit(solution)/shard_map/conv_6/ppermute | solution.py:513
  205.6 59.8 %collective-permute-start.8 = (f32[128,1024]{1,0:T(8,128)S(1)}, f32[128,1024]{1,0:T(8,128)S(1)}, u32[]{:S(2)}, u32[]{:S(2)}) collective-permute-start(f32[128,1024]{1,0:T(8,128)S(1)} %get-tuple-element.77), channel_id=1, source_target_pairs={{0,7},{1,6},{2,5},{3,4},{4,3},{5,2},{6,1},{7,0},{8,15},{9,14},{10,... | collective-permute-start | bytes 1572872 | tf_op jit(solution)/shard_map/conv_7/ppermute | solution.py:513
  266.2 33.6 %collective-permute-start.16 = (f32[128,1024]{1,0:T(8,128)}, f32[128,1024]{1,0:T(8,128)S(1)}, u32[]{:S(2)}, u32[]{:S(2)}) collective-permute-start(f32[128,1024]{1,0:T(8,128)} %get-tuple-element.88), channel_id=1, source_target_pairs={{0,5},{1,4},{2,7},{3,6},{4,1},{5,0},{6,3},{7,2},{8,13},{9,12},{10,... | collective-permute-start | bytes 1572872 | tf_op jit(solution)/shard_map/conv_5/ppermute | solution.py:513
  266.3 37.0 %collective-permute-start.19 = (f32[128,1024]{1,0:T(8,128)}, f32[128,1024]{1,0:T(8,128)S(1)}, u32[]{:S(2)}, u32[]{:S(2)}) collective-permute-start(f32[128,1024]{1,0:T(8,128)} %get-tuple-element.94), channel_id=1, source_target_pairs={{0,4},{1,5},{2,6},{3,7},{4,0},{5,1},{6,2},{7,3},{8,12},{9,13},{10,... | collective-permute-start | bytes 1572872 | tf_op jit(solution)/shard_map/conv_4/ppermute | solution.py:513
  269.5 46.8 %collective-permute-start.18 = (f32[128,1024]{1,0:T(8,128)}, f32[128,1024]{1,0:T(8,128)}, u32[]{:S(2)}, u32[]{:S(2)}) collective-permute-start(f32[128,1024]{1,0:T(8,128)} %get-tuple-element.92), channel_id=1, source_target_pairs={{0,1},{1,0},{2,3},{3,2},{4,5},{5,4},{6,7},{7,6},{8,9},{9,8},{10,11... | collective-permute-start | bytes 1572872 | tf_op jit(solution)/shard_map/conv_1/ppermute | solution.py:513
  269.5 59.4 %collective-permute-start.17 = (f32[128,1024]{1,0:T(8,128)}, f32[128,1024]{1,0:T(8,128)}, u32[]{:S(2)}, u32[]{:S(2)}) collective-permute-start(f32[128,1024]{1,0:T(8,128)} %get-tuple-element.90), channel_id=1, source_target_pairs={{0,3},{1,2},{2,1},{3,0},{4,7},{5,6},{6,5},{7,4},{8,11},{9,10},{10,... | collective-permute-start | bytes 1572872 | tf_op jit(solution)/shard_map/conv_3/ppermute | solution.py:513
  269.5 70.5 %collective-permute-start.12 = (f32[128,1024]{1,0:T(8,128)}, f32[128,1024]{1,0:T(8,128)}, u32[]{:S(2)}, u32[]{:S(2)}) collective-permute-start(f32[128,1024]{1,0:T(8,128)} %get-tuple-element.83), channel_id=1, source_target_pairs={{0,2},{1,3},{2,0},{3,1},{4,6},{5,7},{6,4},{7,5},{8,10},{9,11},{10,... | collective-permute-start | bytes 1572872 | tf_op jit(solution)/shard_map/conv_2/ppermute | solution.py:513
  300.7 41.4 %collective-permute-start.21 = (f32[128,1024]{1,0:T(8,128)}, f32[128,1024]{1,0:T(8,128)S(1)}, u32[]{:S(2)}, u32[]{:S(2)}) collective-permute-start(f32[128,1024]{1,0:T(8,128)} %get-tuple-element.99), channel_id=1, source_target_pairs={{0,6},{1,7},{2,4},{3,5},{4,2},{5,3},{6,0},{7,1},{8,14},{9,15},{10,... | collective-permute-start | bytes 1572872 | tf_op jit(solution)/shard_map/grad_gated_6/ppermute | solution.py:513
  304.1 39.7 %collective-permute-start.23 = (f32[128,1024]{1,0:T(8,128)}, f32[128,1024]{1,0:T(8,128)S(1)}, u32[]{:S(2)}, u32[]{:S(2)}) collective-permute-start(f32[128,1024]{1,0:T(8,128)} %get-tuple-element.104), channel_id=1, source_target_pairs={{0,7},{1,6},{2,5},{3,4},{4,3},{5,2},{6,1},{7,0},{8,15},{9,14},{10,... | collective-permute-start | bytes 1572872 | tf_op jit(solution)/shard_map/grad_gated_7/ppermute | solution.py:513
  316.3 28.4 %collective-permute-start.28 = (f32[32,1024]{1,0:T(8,128)S(1)}, f32[32,1024]{1,0:T(8,128)S(1)}, u32[]{:S(2)}, u32[]{:S(2)}) collective-permute-start(f32[32,1024]{1,0:T(8,128)S(1)} %get-tuple-element.135), channel_id=1, source_target_pairs={{0,2},{2,0},{4,6},{6,4},{1,3},{3,1},{5,7},{7,5},{8,10},{10,8},{12,... | collective-permute-start | bytes 393224 | tf_op jit(solution)/shard_map/rows_sum/ppermute | solution.py:513
  340.0 51.0 %collective-permute-start.24 = (f32[128,1024]{1,0:T(8,128)}, f32[128,1024]{1,0:T(8,128)S(1)}, u32[]{:S(2)}, u32[]{:S(2)}) collective-permute-start(f32[128,1024]{1,0:T(8,128)} %copy-done.58), channel_id=1, source_target_pairs={{0,5},{1,4},{2,7},{3,6},{4,1},{5,0},{6,3},{7,2},{8,13},{9,12},{10,... | collective-permute-start | bytes 1572872 | tf_op jit(solution)/shard_map/grad_gated_5/ppermute | solution.py:513
  340.0 27.1 %collective-permute-start.30 = (f32[32,1024]{1,0:T(8,128)S(1)}, f32[32,1024]{1,0:T(8,128)S(1)}, u32[]{:S(2)}, u32[]{:S(2)}) collective-permute-start(f32[32,1024]{1,0:T(8,128)S(1)} %get-tuple-element.136), channel_id=1, source_target_pairs={{0,6},{2,4},{4,2},{6,0},{1,7},{3,5},{5,3},{7,1},{8,14},{10,12},{12... | collective-permute-start | bytes 393224 | tf_op jit(solution)/shard_map/rows_sum/ppermute | solution.py:513
  342.8 38.7 %collective-permute-start.29 = (f32[32,1024]{1,0:T(8,128)S(1)}, f32[32,1024]{1,0:T(8,128)S(1)}, u32[]{:S(2)}, u32[]{:S(2)}) collective-permute-start(f32[32,1024]{1,0:T(8,128)S(1)} %get-tuple-element.137), channel_id=1, source_target_pairs={{0,4},{2,6},{4,0},{6,2},{1,5},{3,7},{5,1},{7,3},{8,12},{10,14},{12... | collective-permute-start | bytes 393224 | tf_op jit(solution)/shard_map/rows_sum/ppermute | solution.py:513
  344.6 47.2 %collective-permute-start.26 = (f32[128,1024]{1,0:T(8,128)}, f32[128,1024]{1,0:T(8,128)S(1)}, u32[]{:S(2)}, u32[]{:S(2)}) collective-permute-start(f32[128,1024]{1,0:T(8,128)} %copy-done.57), channel_id=1, source_target_pairs={{0,1},{1,0},{2,3},{3,2},{4,5},{5,4},{6,7},{7,6},{8,9},{9,8},{10,11... | collective-permute-start | bytes 1572872 | tf_op jit(solution)/shard_map/grad_gated_1/ppermute | solution.py:513
  344.7 48.0 %collective-permute-start.27 = (f32[128,1024]{1,0:T(8,128)}, f32[128,1024]{1,0:T(8,128)S(1)}, u32[]{:S(2)}, u32[]{:S(2)}) collective-permute-start(f32[128,1024]{1,0:T(8,128)} %copy-done.56), channel_id=1, source_target_pairs={{0,3},{1,2},{2,1},{3,0},{4,7},{5,6},{6,5},{7,4},{8,11},{9,10},{10,... | collective-permute-start | bytes 1572872 | tf_op jit(solution)/shard_map/grad_gated_3/ppermute | solution.py:513
  367.1 37.0 %collective-permute-start.25 = (f32[128,1024]{1,0:T(8,128)}, f32[128,1024]{1,0:T(8,128)}, u32[]{:S(2)}, u32[]{:S(2)}) collective-permute-start(f32[128,1024]{1,0:T(8,128)} %copy-done.55), channel_id=1, source_target_pairs={{0,4},{1,5},{2,6},{3,7},{4,0},{5,1},{6,2},{7,3},{8,12},{9,13},{10,... | collective-permute-start | bytes 1572872 | tf_op jit(solution)/shard_map/grad_gated_4/ppermute | solution.py:513
  381.5 34.1 %collective-permute-start.22 = (f32[128,1024]{1,0:T(8,128)}, f32[128,1024]{1,0:T(8,128)}, u32[]{:S(2)}, u32[]{:S(2)}) collective-permute-start(f32[128,1024]{1,0:T(8,128)} %copy-done.54), channel_id=1, source_target_pairs={{0,2},{1,3},{2,0},{3,1},{4,6},{5,7},{6,4},{7,5},{8,10},{9,11},{10,... | collective-permute-start | bytes 1572872 | tf_op jit(solution)/shard_map/grad_gated_2/ppermute | solution.py:513
  (68 other events, 863.9 us)
Sparse Core Ops, SparseCore 0:
  116.4 36.1 all-gather.2
  266.4 48.7 reduce-scatter.1

commit v7 on v6

--- a/solution.py
+++ b/solution.py
@@ -596,7 +596,7 @@
     for i in range(2, len(far)):
         order = order + near[i - 2 : i - 1] + far[i : i + 1]
     order = order[:-1] + near[len(far) - 2 :] + order[-1:]
-    last_order = far + near
+    last_order = far[:-1] + near + far[-1:]
     by_block = functools.partial(block_views, plan, owners)
     by_tile = functools.partial(tile_views, plan, (parts, rows, cols))
 
@@ -654,13 +654,15 @@
     tile_shape = (parts * cols, rows, height, side)
     cot, term = term_of(plan, me, spec, grad_conv, by_block, tile_shape, by_tile)
     back_out = grad_of(plan, me, filt, cot, owners, by_block)
-    grad_gated = exchange(back_out, "grad_gated", last_order, 3, 2)
-
     term = after([conv[step] for step in far[:2]], term)
     term = lax.psum_scatter(term, ("dp", "col"), scatter_dimension=0, tiled=False)
     with jax.named_scope("rows_sum"):
         arrived = [pairwise(term[i], "row", i) for i in range(1, rows)]
     total = sum(arrived, term[0]) * (1.0 / side)
+    back_out = list(back_out)
+    for step in far[3:] + near:
+        back_out[step] = after(total, back_out[step])
+    grad_gated = exchange(back_out, "grad_gated", last_order, 3, 1)
     every = [0] + order
     (grad_outer,) = gated_by(me, every, [conv[step] for step in every], [grad_out[0]])
     total = after(grad_outer, total)
@@ -675,7 +677,7 @@
         bit *= 2
     grad_filter = pieces.reshape(block, side)
 
-    every = [0] + far + near[::-1]
+    every = [0] + near + far
     gates = [signal[0], inner_gate[0]]
     early, late = every[:-1], every[-1:]
     done = gated_by(me, early, [grad_gated[step] for step in early], gates)

time: 431 us -> 417 us (0.968)
  starting transfers between devices: 94.3 us -> 67.4 us
  waiting for transfers between devices: 161 us -> 181 us
  local copies, waits for them, and re-layouts: 51.2 us -> 41.9 us
    ppermute x34, starting transfers between devices: 94.2 us -> 67.4 us  [pairwise(): lax.ppermute(block, axis, [(i, i ^ step) for i in range(lax.axis_size(axi...]
    ppermute x34, waiting for transfers between devices: 121 us -> 135 us  [pairwise(): lax.ppermute(block, axis, [(i, i ^ step) for i in range(lax.axis_size(axi...]
    unnamed x128 -> x104, local copies, waits for them, and re-layouts: 50 us -> 38 us
    reduce_scatter x1, waiting for transfers between devices: 9.98 us -> 16.5 us  [channel_shards(): lax.psum_scatter(term, ('dp', 'col'), scatter_dimension=0, tiled=False)]
  transfers between devices with their start and end apart: 36 -> 36, of which waited for: 10 -> 11; matrix products, arithmetic and copies ran while one was open for 3% -> 4% of each run, Pallas kernels for 22% -> 22%
where the time goes in v7:
time: 417 us; the launch traced here: 414 us
  waiting for transfers between devices  181 us (43%)
  Pallas kernels  93.4 us (22%)
  starting transfers between devices  67.4 us (16%)
  local copies, waits for them, and re-layouts  41.9 us (10%)
  other arithmetic  15.3 us (4%)
  between operations  14.6 us (4%)
    ppermute x34, waiting for transfers between devices, pairwise(): lax.ppermute(block, axis, [(i, i ^ step) for i in range(lax.axis_size(axi...  135 us
    pallas_call x4, Pallas kernels, call_kernel(): pl.pallas_call(kernel, out_shape=out_shape, in_specs=in_specs, out_specs=...  84 us
    ppermute x34, starting transfers between devices, pairwise(): lax.ppermute(block, axis, [(i, i ^ step) for i in range(lax.axis_size(axi...  67.4 us
    unnamed x104, local copies, waits for them, and re-layouts  38 us
    all_gather x1, waiting for transfers between devices, channel_shards(): over_all = [lax.all_gather(over_row, ('dp', 'col'))]  29.7 us
    reduce_scatter x1, waiting for transfers between devices, channel_shards(): lax.psum_scatter(term, ('dp', 'col'), scatter_dimension=0, tiled=False)  16.5 us
    pallas_call x3, Pallas kernels, gated_by(): pl.pallas_call(functools.partial(gate_kernel, steps, len(gates)), grid_sp...  9.47 us
  transfers between devices with their start and end apart: 36, of which 11 were waited for; matrix products, arithmetic and copies ran while one was open for 4% of the time, Pallas kernels for 22%

profile of v7, /device:TPU:7, one launch (start us, length us, event | category | flops | bytes accessed | tf_op | source)
XLA Modules:
  0.0 414.0 jit_solution(7379503732261901024)
XLA Ops:
  8.3 3.9 collective-permute-start.3
  13.2 3.8 multiply_bitcast_fusion.8
  17.3 3.8 collective-permute-start.5
  22.0 2.9 collective-permute-done.3.refs_7_
  24.9 25.6 %collective-permute-start.4 = (f32[160,1024]{1,0:T(8,128)S(1)}, f32[160,1024]{1,0:T(8,128)S(1)}, u32[]{:S(2)}, u32[]{:S(2)}) collective-permute-start(f32[160,1024]{1,0:T(8,128)S(1)} %get-tuple-element.68), channel_id=1, source_target_pairs={{0,4},{1,5},{2,6},{3,7},{4,0},{5,1},{6,2},{7,3},{8,12},{9,13},{10,... | collective-permute-start | bytes 1966088 | tf_op jit(solution)/shard_map/gated_4/ppermute | solution.py:513
  50.5 2.2 multiply_bitcast_fusion
  55.2 58.5 %collective-permute-done.4.refs_4_ = f32[160,1024]{1,0:T(8,128)S(1)} collective-permute-done((f32[160,1024]{1,0:T(8,128)S(1)}, f32[160,1024]{1,0:T(8,128)S(1)}, u32[]{:S(2)}, u32[]{:S(2)}) %collective-permute-start.4) | collective-permute-done | bytes 655392 | tf_op jit(solution)/shard_map/gated_4/ppermute | solution.py:513
  116.3 2.7 collective-permute-start.7
  120.0 2.7 collective-permute-start.14
  122.8 29.7 %all-gather.3.cloned.1.call-done = f32[32,32,1024]{2,1,0:T(8,128)} async-done(((f32[4,32,1024]{2,1,0:T(8,128)}), f32[32,32,1024]{2,1,0:T(8,128)}) %all-gather.3.cloned.1.call-update) | async-done | bytes 4194320 | tf_op jit(solution)/shard_map/all_gather | solution.py:645
  152.5 2.2 copy-done
  160.4 15.0 %filter_spectrum.1.filt = f32[2,528,1024]{2,1,0:T(8,128)S(1)} custom-call(s32[1]{0:T(128)} %bitcast.me, f32[8,4,32,1024]{3,2,1,0:T(8,128)S(1)} %bitcast.87, bf16[2,544,512]{2,1,0:T(8,128)(2,1)S(1)} %copy-done.10, bf16[2,512,512]{2,1,0:T(8,128)(2,1)S(1)} %copy-done.13, f32[2,528,1024]{2,1,0:T(8,128)S(1)} %copy-done, bf16[2,4,512,512]{3,2,1,0:T(8,128)(2,1)S(1)} %copy-done.2), custom_call_target="tpu_custom_call" | custom-call | flops 1048576 | bytes 1048576 | tf_op jit(solution)/shard_map/filter_spectrum/pallas_call | solution.py:417
  177.8 24.3 %conv_of.1 = (f32[2,528,1024]{2,1,0:T(8,128)S(1)}, f32[128,1024]{1,0:T(8,128)S(1)}, f32[128,1024]{1,0:T(8,128)}, f32[128,1024]{1,0:T(8,128)}, f32[128,1024]{1,0:...) custom-call(s32[1]{0:T(128)} %bitcast.me, ...), custom_call_target="tpu_custom_call" | custom-call | flops 1048576 | bytes 1048576 | tf_op jit(solution)/shard_map/conv_of/pallas_call | solution.py:417
  207.1 23.8 %collective-permute-done.11.refs_4_ = f32[128,1024]{1,0:T(8,128)S(1)} collective-permute-done((f32[128,1024]{1,0:T(8,128)S(1)}, f32[128,1024]{1,0:T(8,128)S(1)}, u32[]{:S(2)}, u32[]{:S(2)}) %collective-permute-start.11) | collective-permute-done | bytes 524320 | tf_op jit(solution)/shard_map/grad_conv_4/ppermute | solution.py:513
  230.9 30.4 %term_of.1 = (f32[2,528,1024]{2,1,0:T(8,128)S(1)}, f32[8,4,32,1024]{3,2,1,0:T(8,128)S(1)}) custom-call(s32[1]{0:T(128)} %bitcast.me, f32[2,528,1024]{2,1,0:T(8,128)S(1)} %get-tuple-element.99.gated, f32[128,1024]{1,0:T(8,128)S(1)} %copy-done.20, f32[128,1024]{1,0:T(8,128)S(1)} %collective-permute-done.20.refs_1_, ...), custom_call_target="tpu_custom_call" | custom-call | flops 1048576 | bytes 1048576 | tf_op jit(solution)/shard_map/term_of/pallas_call | solution.py:417
  269.0 2.5 collective-permute-start.16
  273.4 2.7 copy-done.1
  276.1 2.6 copy-done.4
  278.7 2.4 copy-done.6
  283.4 14.3 %grad_of.1 = (f32[128,1024]{1,0:T(8,128)S(1)}, f32[128,1024]{1,0:T(8,128)}, f32[128,1024]{1,0:T(8,128)}, f32[128,1024]{1,0:T(8,128)}, f32[128,1024]{1,0:T(8,128)...) custom-call(s32[1]{0:T(128)} %bitcast.me, f32[2,528,1024]{2,1,0:T(8,128)S(1)} %copy-done.6, ...), custom_call_target="tpu_custom_call" | custom-call | flops 1048576 | bytes 1048576 | tf_op jit(solution)/shard_map/grad_of/pallas_call | solution.py:417
  299.5 16.5 %reduce-scatter.2.cloned.1.call-done = f32[1,4,32,1024]{3,2,1,0:T(8,128)} async-done(((f32[8,4,32,1024]{3,2,1,0:T(8,128)}), f32[1,4,32,1024]{3,2,1,0:T(8,128)}) %reduce-scatter.2.cloned.1.call-update) | async-done | bytes 524304 | tf_op jit(solution)/shard_map/reduce_scatter | solution.py:658
  320.5 10.2 %collective-permute-done.12.refs_3_ = f32[128,1024]{1,0:T(8,128)} collective-permute-done((f32[128,1024]{1,0:T(8,128)}, f32[128,1024]{1,0:T(8,128)}, u32[]{:S(2)}, u32[]{:S(2)}) %collective-permute-start.12) | collective-permute-done | bytes 524320 | tf_op jit(solution)/shard_map/conv_2/ppermute | solution.py:513
  336.5 3.6 gate_out.3
  340.1 8.6 %collective-permute-done.23 = f32[32,1024]{1,0:T(8,128)S(1)} collective-permute-done((f32[32,1024]{1,0:T(8,128)S(1)}, f32[32,1024]{1,0:T(8,128)S(1)}, u32[]{:S(2)}, u32[]{:S(2)}) %collective-permute-start.23) | collective-permute-done | bytes 131104 | tf_op jit(solution)/shard_map/rows_sum/ppermute | solution.py:513
  349.8 2.6 collective-permute-start.31
  352.3 2.5 collective-permute-start.29
  355.3 2.7 collective-permute-start.26
  358.0 3.4 collective-permute-start.27
  362.3 23.0 %collective-permute-done.30.refs_6_ = f32[128,1024]{1,0:T(8,128)S(1)} collective-permute-done((f32[128,1024]{1,0:T(8,128)}, f32[128,1024]{1,0:T(8,128)S(1)}, u32[]{:S(2)}, u32[]{:S(2)}) %collective-permute-start.30) | collective-permute-done | bytes 524320 | tf_op jit(solution)/shard_map/grad_gated_5/ppermute | solution.py:513
  390.0 2.4 fusion
  392.4 6.2 %collective-permute-done.27.refs_2_ = f32[128,1024]{1,0:T(8,128)} collective-permute-done((f32[128,1024]{1,0:T(8,128)}, f32[128,1024]{1,0:T(8,128)}, u32[]{:S(2)}, u32[]{:S(2)}) %collective-permute-start.27) | collective-permute-done | bytes 524320 | tf_op jit(solution)/shard_map/grad_gated_3/ppermute | solution.py:513
  399.7 4.0 gate_out.4
  (171 shorter events, 57.9 us)
Async XLA Ops:
  7.2 145.4 %all-gather.3.cloned.1.call-start = ((), (), s32[]{:S(2)}) async-start(), calls=%async_computation.2 | async-start | bytes 4718592 | tf_op jit(solution)/shard_map/all_gather | solution.py:645
  8.3 16.5 %collective-permute-start.3 = (f32[128,1024]{1,0:T(8,128)S(1)}, f32[128,1024]{1,0:T(8,128)S(1)}, u32[]{:S(2)}, u32[]{:S(2)}) collective-permute-start(f32[128,1024]{1,0:T(8,128)S(1)} %multiply_bitcast_fusion.15), channel_id=1, source_target_pairs={{0,7},{1,6},{2,5},{3,4},{4,3},{5,2},{6,1},{7,0},{8,15},{9,14},{10,... | collective-permute-start | bytes 1572872 | tf_op jit(solution)/shard_map/gated_7/ppermute | solution.py:513
  17.2 35.6 %collective-permute-start.6 = (f32[160,1024]{1,0:T(8,128)S(1)}, f32[160,1024]{1,0:T(8,128)S(1)}, u32[]{:S(2)}, u32[]{:S(2)}) collective-permute-start(f32[160,1024]{1,0:T(8,128)S(1)} %get-tuple-element.146), channel_id=1, source_target_pairs={{0,6},{1,7},{2,4},{3,5},{4,2},{5,3},{6,0},{7,1},{8,14},{9,15},{10,... | collective-permute-start | bytes 1966088 | tf_op jit(solution)/shard_map/gated_6/ppermute | solution.py:513
  17.2 37.1 %collective-permute-start.1 = (f32[160,1024]{1,0:T(8,128)S(1)}, f32[160,1024]{1,0:T(8,128)S(1)}, u32[]{:S(2)}, u32[]{:S(2)}) collective-permute-start(f32[160,1024]{1,0:T(8,128)S(1)} %get-tuple-element.148), channel_id=1, source_target_pairs={{0,2},{1,3},{2,0},{3,1},{4,6},{5,7},{6,4},{7,5},{8,10},{9,11},{10,... | collective-permute-start | bytes 1966088 | tf_op jit(solution)/shard_map/gated_2/ppermute | solution.py:513
  17.3 98.0 %collective-permute-start.5 = (f32[128,1024]{1,0:T(8,128)}, f32[128,1024]{1,0:T(8,128)S(1)}, u32[]{:S(2)}, u32[]{:S(2)}) collective-permute-start(f32[128,1024]{1,0:T(8,128)} %get-tuple-element.137), channel_id=1, source_target_pairs={{0,5},{1,4},{2,7},{3,6},{4,1},{5,0},{6,3},{7,2},{8,13},{9,12},{10,... | collective-permute-start | bytes 1572872 | tf_op jit(solution)/shard_map/gated_5/ppermute | solution.py:513
  21.1 94.3 %collective-permute-start.2 = (f32[128,1024]{1,0:T(8,128)}, f32[128,1024]{1,0:T(8,128)}, u32[]{:S(2)}, u32[]{:S(2)}) collective-permute-start(f32[128,1024]{1,0:T(8,128)} %get-tuple-element.139), channel_id=1, source_target_pairs={{0,3},{1,2},{2,1},{3,0},{4,7},{5,6},{6,5},{7,4},{8,11},{9,10},{10,... | collective-permute-start | bytes 1572872 | tf_op jit(solution)/shard_map/gated_3/ppermute | solution.py:513
  24.9 88.8 %collective-permute-start.4 = (f32[160,1024]{1,0:T(8,128)S(1)}, f32[160,1024]{1,0:T(8,128)S(1)}, u32[]{:S(2)}, u32[]{:S(2)}) collective-permute-start(f32[160,1024]{1,0:T(8,128)S(1)} %get-tuple-element.68), channel_id=1, source_target_pairs={{0,4},{1,5},{2,6},{3,7},{4,0},{5,1},{6,2},{7,3},{8,12},{9,13},{10,... | collective-permute-start | bytes 1966088 | tf_op jit(solution)/shard_map/gated_4/ppermute | solution.py:513
  52.7 62.6 %collective-permute-start = (f32[128,1024]{1,0:T(8,128)}, f32[128,1024]{1,0:T(8,128)S(1)}, u32[]{:S(2)}, u32[]{:S(2)}) collective-permute-start(f32[128,1024]{1,0:T(8,128)} %get-tuple-element.141), channel_id=1, source_target_pairs={{0,1},{1,0},{2,3},{3,2},{4,5},{5,4},{6,7},{7,6},{8,9},{9,8},{10,11... | collective-permute-start | bytes 1572872 | tf_op jit(solution)/shard_map/gated_1/ppermute | solution.py:513
  116.2 199.7 %reduce-scatter.2.cloned.1.call-start = ((), (), s32[]{:S(2)}) async-start(), calls=%async_computation.1 | async-start | bytes 4718592 | tf_op jit(solution)/shard_map/reduce_scatter | solution.py:658
  116.3 59.2 %collective-permute-start.7 = (f32[128,1024]{1,0:T(8,128)}, f32[128,1024]{1,0:T(8,128)}, u32[]{:S(2)}, u32[]{:S(2)}) collective-permute-start(f32[128,1024]{1,0:T(8,128)} %get-tuple-element.70), channel_id=1, source_target_pairs={{0,7},{1,6},{2,5},{3,4},{4,3},{5,2},{6,1},{7,0},{8,15},{9,14},{10,... | collective-permute-start | bytes 1572872 | tf_op jit(solution)/shard_map/grad_conv_7/ppermute | solution.py:513
  119.0 84.0 %collective-permute-start.9 = (f32[128,1024]{1,0:T(8,128)}, f32[128,1024]{1,0:T(8,128)}, u32[]{:S(2)}, u32[]{:S(2)}) collective-permute-start(f32[128,1024]{1,0:T(8,128)} %get-tuple-element.82), channel_id=1, source_target_pairs={{0,6},{1,7},{2,4},{3,5},{4,2},{5,3},{6,0},{7,1},{8,14},{9,15},{10,... | collective-permute-start | bytes 1572872 | tf_op jit(solution)/shard_map/grad_conv_6/ppermute | solution.py:513
  120.0 83.5 %collective-permute-start.13 = (f32[128,1024]{1,0:T(8,128)}, f32[128,1024]{1,0:T(8,128)}, u32[]{:S(2)}, u32[]{:S(2)}) collective-permute-start(f32[128,1024]{1,0:T(8,128)} %get-tuple-element.88), channel_id=1, source_target_pairs={{0,5},{1,4},{2,7},{3,6},{4,1},{5,0},{6,3},{7,2},{8,13},{9,12},{10,... | collective-permute-start | bytes 1572872 | tf_op jit(solution)/shard_map/grad_conv_5/ppermute | solution.py:513
  120.0 85.4 %collective-permute-start.14 = (f32[128,1024]{1,0:T(8,128)}, f32[128,1024]{1,0:T(8,128)}, u32[]{:S(2)}, u32[]{:S(2)}) collective-permute-start(f32[128,1024]{1,0:T(8,128)} %get-tuple-element.89), channel_id=1, source_target_pairs={{0,2},{1,3},{2,0},{3,1},{4,6},{5,7},{6,4},{7,5},{8,10},{9,11},{10,... | collective-permute-start | bytes 1572872 | tf_op jit(solution)/shard_map/grad_conv_2/ppermute | solution.py:513
  122.8 84.3 %collective-permute-start.15 = (f32[128,1024]{1,0:T(8,128)}, f32[128,1024]{1,0:T(8,128)}, u32[]{:S(2)}, u32[]{:S(2)}) collective-permute-start(f32[128,1024]{1,0:T(8,128)} %get-tuple-element.90), channel_id=1, source_target_pairs={{0,3},{1,2},{2,1},{3,0},{4,7},{5,6},{6,5},{7,4},{8,11},{9,10},{10,... | collective-permute-start | bytes 1572872 | tf_op jit(solution)/shard_map/grad_conv_3/ppermute | solution.py:513
  175.5 55.4 %collective-permute-start.11 = (f32[128,1024]{1,0:T(8,128)S(1)}, f32[128,1024]{1,0:T(8,128)S(1)}, u32[]{:S(2)}, u32[]{:S(2)}) collective-permute-start(f32[128,1024]{1,0:T(8,128)S(1)} %copy-done.49), channel_id=1, source_target_pairs={{0,4},{1,5},{2,6},{3,7},{4,0},{5,1},{6,2},{7,3},{8,12},{9,13},{10,... | collective-permute-start | bytes 1572872 | tf_op jit(solution)/shard_map/grad_conv_4/ppermute | solution.py:513
  202.9 27.9 %collective-permute-start.20 = (f32[128,1024]{1,0:T(8,128)S(1)}, f32[128,1024]{1,0:T(8,128)S(1)}, u32[]{:S(2)}, u32[]{:S(2)}) collective-permute-start(f32[128,1024]{1,0:T(8,128)S(1)} %copy-done.48), channel_id=1, source_target_pairs={{0,1},{1,0},{2,3},{3,2},{4,5},{5,4},{6,7},{7,6},{8,9},{9,8},{10,11... | collective-permute-start | bytes 1572872 | tf_op jit(solution)/shard_map/grad_conv_1/ppermute | solution.py:513
  203.5 61.9 %collective-permute-start.10 = (f32[128,1024]{1,0:T(8,128)S(1)}, f32[128,1024]{1,0:T(8,128)S(1)}, u32[]{:S(2)}, u32[]{:S(2)}) collective-permute-start(f32[128,1024]{1,0:T(8,128)S(1)} %get-tuple-element.84), channel_id=1, source_target_pairs={{0,6},{1,7},{2,4},{3,5},{4,2},{5,3},{6,0},{7,1},{8,14},{9,15},{10,... | collective-permute-start | bytes 1572872 | tf_op jit(solution)/shard_map/conv_6/ppermute | solution.py:513
  205.4 60.8 %collective-permute-start.8 = (f32[128,1024]{1,0:T(8,128)S(1)}, f32[128,1024]{1,0:T(8,128)S(1)}, u32[]{:S(2)}, u32[]{:S(2)}) collective-permute-start(f32[128,1024]{1,0:T(8,128)S(1)} %get-tuple-element.81), channel_id=1, source_target_pairs={{0,7},{1,6},{2,5},{3,4},{4,3},{5,2},{6,1},{7,0},{8,15},{9,14},{10,... | collective-permute-start | bytes 1572872 | tf_op jit(solution)/shard_map/conv_7/ppermute | solution.py:513
  268.1 30.4 %collective-permute-start.19 = (f32[128,1024]{1,0:T(8,128)S(1)}, f32[128,1024]{1,0:T(8,128)S(1)}, u32[]{:S(2)}, u32[]{:S(2)}) collective-permute-start(f32[128,1024]{1,0:T(8,128)S(1)} %copy-done.45), channel_id=1, source_target_pairs={{0,4},{1,5},{2,6},{3,7},{4,0},{5,1},{6,2},{7,3},{8,12},{9,13},{10,... | collective-permute-start | bytes 1572872 | tf_op jit(solution)/shard_map/conv_4/ppermute | solution.py:513
  268.1 49.0 %collective-permute-start.18 = (f32[128,1024]{1,0:T(8,128)}, f32[128,1024]{1,0:T(8,128)}, u32[]{:S(2)}, u32[]{:S(2)}) collective-permute-start(f32[128,1024]{1,0:T(8,128)} %get-tuple-element.96), channel_id=1, source_target_pairs={{0,1},{1,0},{2,3},{3,2},{4,5},{5,4},{6,7},{7,6},{8,9},{9,8},{10,11... | collective-permute-start | bytes 1572872 | tf_op jit(solution)/shard_map/conv_1/ppermute | solution.py:513
  269.0 49.3 %collective-permute-start.17 = (f32[128,1024]{1,0:T(8,128)}, f32[128,1024]{1,0:T(8,128)}, u32[]{:S(2)}, u32[]{:S(2)}) collective-permute-start(f32[128,1024]{1,0:T(8,128)} %get-tuple-element.94), channel_id=1, source_target_pairs={{0,3},{1,2},{2,1},{3,0},{4,7},{5,6},{6,5},{7,4},{8,11},{9,10},{10,... | collective-permute-start | bytes 1572872 | tf_op jit(solution)/shard_map/conv_3/ppermute | solution.py:513
  269.0 51.4 %collective-permute-start.16 = (f32[128,1024]{1,0:T(8,128)}, f32[128,1024]{1,0:T(8,128)}, u32[]{:S(2)}, u32[]{:S(2)}) collective-permute-start(f32[128,1024]{1,0:T(8,128)} %get-tuple-element.92), channel_id=1, source_target_pairs={{0,5},{1,4},{2,7},{3,6},{4,1},{5,0},{6,3},{7,2},{8,13},{9,12},{10,... | collective-permute-start | bytes 1572872 | tf_op jit(solution)/shard_map/conv_5/ppermute | solution.py:513
  271.5 59.2 %collective-permute-start.12 = (f32[128,1024]{1,0:T(8,128)}, f32[128,1024]{1,0:T(8,128)}, u32[]{:S(2)}, u32[]{:S(2)}) collective-permute-start(f32[128,1024]{1,0:T(8,128)} %get-tuple-element.87), channel_id=1, source_target_pairs={{0,2},{1,3},{2,0},{3,1},{4,6},{5,7},{6,4},{7,5},{8,10},{9,11},{10,... | collective-permute-start | bytes 1572872 | tf_op jit(solution)/shard_map/conv_2/ppermute | solution.py:513
  299.3 53.1 %collective-permute-start.21 = (f32[128,1024]{1,0:T(8,128)}, f32[128,1024]{1,0:T(8,128)S(1)}, u32[]{:S(2)}, u32[]{:S(2)}) collective-permute-start(f32[128,1024]{1,0:T(8,128)} %get-tuple-element.103), channel_id=1, source_target_pairs={{0,7},{1,6},{2,5},{3,4},{4,3},{5,2},{6,1},{7,0},{8,15},{9,14},{10,... | collective-permute-start | bytes 1572872 | tf_op jit(solution)/shard_map/grad_gated_7/ppermute | solution.py:513
  317.0 23.0 %collective-permute-start.22 = (f32[32,1024]{1,0:T(8,128)S(1)}, f32[32,1024]{1,0:T(8,128)S(1)}, u32[]{:S(2)}, u32[]{:S(2)}) collective-permute-start(f32[32,1024]{1,0:T(8,128)S(1)} %get-tuple-element.143), channel_id=1, source_target_pairs={{0,2},{2,0},{4,6},{6,4},{1,3},{3,1},{5,7},{7,5},{8,10},{10,8},{12,... | collective-permute-start | bytes 393224 | tf_op jit(solution)/shard_map/rows_sum/ppermute | solution.py:513
  318.3 21.8 %collective-permute-start.24 = (f32[32,1024]{1,0:T(8,128)S(1)}, f32[32,1024]{1,0:T(8,128)S(1)}, u32[]{:S(2)}, u32[]{:S(2)}) collective-permute-start(f32[32,1024]{1,0:T(8,128)S(1)} %get-tuple-element.144), channel_id=1, source_target_pairs={{0,6},{2,4},{4,2},{6,0},{1,7},{3,5},{5,3},{7,1},{8,14},{10,12},{12... | collective-permute-start | bytes 393224 | tf_op jit(solution)/shard_map/rows_sum/ppermute | solution.py:513
  320.4 28.2 %collective-permute-start.23 = (f32[32,1024]{1,0:T(8,128)S(1)}, f32[32,1024]{1,0:T(8,128)S(1)}, u32[]{:S(2)}, u32[]{:S(2)}) collective-permute-start(f32[32,1024]{1,0:T(8,128)S(1)} %get-tuple-element.145), channel_id=1, source_target_pairs={{0,4},{2,6},{4,0},{6,2},{1,5},{3,7},{5,1},{7,3},{8,12},{10,14},{12... | collective-permute-start | bytes 393224 | tf_op jit(solution)/shard_map/rows_sum/ppermute | solution.py:513
  330.7 54.6 %collective-permute-start.30 = (f32[128,1024]{1,0:T(8,128)}, f32[128,1024]{1,0:T(8,128)S(1)}, u32[]{:S(2)}, u32[]{:S(2)}) collective-permute-start(f32[128,1024]{1,0:T(8,128)} %copy-done.43), channel_id=1, source_target_pairs={{0,5},{1,4},{2,7},{3,6},{4,1},{5,0},{6,3},{7,2},{8,13},{9,12},{10,... | collective-permute-start | bytes 1572872 | tf_op jit(solution)/shard_map/grad_gated_5/ppermute | solution.py:513
  352.3 40.1 %collective-permute-start.29 = (f32[128,1024]{1,0:T(8,128)}, f32[128,1024]{1,0:T(8,128)}, u32[]{:S(2)}, u32[]{:S(2)}) collective-permute-start(f32[128,1024]{1,0:T(8,128)} %get-tuple-element.120), channel_id=1, source_target_pairs={{0,6},{1,7},{2,4},{3,5},{4,2},{5,3},{6,0},{7,1},{8,14},{9,15},{10,... | collective-permute-start | bytes 1572872 | tf_op jit(solution)/shard_map/grad_gated_6/ppermute | solution.py:513
  354.9 50.4 %collective-permute-start.25 = (f32[128,1024]{1,0:T(8,128)}, f32[128,1024]{1,0:T(8,128)}, u32[]{:S(2)}, u32[]{:S(2)}) collective-permute-start(f32[128,1024]{1,0:T(8,128)} %get-tuple-element.108), channel_id=1, source_target_pairs={{0,4},{1,5},{2,6},{3,7},{4,0},{5,1},{6,2},{7,3},{8,12},{9,13},{10,... | collective-permute-start | bytes 1572872 | tf_op jit(solution)/shard_map/grad_gated_4/ppermute | solution.py:513
  355.3 37.2 %collective-permute-start.26 = (f32[128,1024]{1,0:T(8,128)}, f32[128,1024]{1,0:T(8,128)}, u32[]{:S(2)}, u32[]{:S(2)}) collective-permute-start(f32[128,1024]{1,0:T(8,128)} %get-tuple-element.112), channel_id=1, source_target_pairs={{0,2},{1,3},{2,0},{3,1},{4,6},{5,7},{6,4},{7,5},{8,10},{9,11},{10,... | collective-permute-start | bytes 1572872 | tf_op jit(solution)/shard_map/grad_gated_2/ppermute | solution.py:513
  358.0 40.7 %collective-permute-start.27 = (f32[128,1024]{1,0:T(8,128)}, f32[128,1024]{1,0:T(8,128)}, u32[]{:S(2)}, u32[]{:S(2)}) collective-permute-start(f32[128,1024]{1,0:T(8,128)} %get-tuple-element.115), channel_id=1, source_target_pairs={{0,3},{1,2},{2,1},{3,0},{4,7},{5,6},{6,5},{7,4},{8,11},{9,10},{10,... | collective-permute-start | bytes 1572872 | tf_op jit(solution)/shard_map/grad_gated_3/ppermute | solution.py:513
  (56 other events, 775.4 us)
Sparse Core Ops, SparseCore 0:
  116.4 36.1 all-gather.2
  267.2 48.7 reduce-scatter.1
